TPU v7x, 32 devices: a whole 2x2x4 slice. The times are simulated.
32 devices in a mesh: groups: 2 (over y), shard: 2 (over x), expert: 4 (over z), section: 2 (over core).
Axes of the slice: x: 2, y: 2, z: 4, core: 2. Of those that a mesh axis runs over, the one named last changes fastest.
Arguments:
- tokens: bfloat16 [2, 512, 6144], P(None, ('groups', 'shard', 'expert')), parts along dimension 1, may hold values from -6 to 6
- norm_gain: float32 [2, 6144], P('section'), may hold values from 0.5 to 2
- route_ids: int32 [2, 2, 512, 2], P('section', None, ('groups', 'shard', 'expert')), parts along dimension 2, may hold values from 0 to 3, all different within a row; in each aligned block of 32 rows (0 to 31, 32 to 63, ..., all dimensions but the last counted through in order) at most 18 rows name the same one
- route_weights: float32 [2, 2, 512, 2], P('section', None, ('groups', 'shard', 'expert')), parts along dimension 2, may hold values from 0.25 to 1
- gate_blocks: bfloat16 [2, 4, 64, 1, 128, 128], P('section', 'expert', 'shard'), may hold values from -0.5 to 0.5
- up_blocks: bfloat16 [2, 4, 64, 1, 128, 128], P('section', 'expert', 'shard'), may hold values from -0.5 to 0.5
- down_blocks: bfloat16 [2, 4, 64, 1, 128, 128], P('section', 'expert', 'shard'), may hold values from -0.4375 to 0.4375
- gate_rows: int32 [2, 4, 64, 1], P('section', 'expert', 'shard'), may hold values from 0 to 47
- down_cols: int32 [2, 4, 64, 1], P('section', 'expert', 'shard'), may hold values from 0 to 47
Outputs:
- hidden_states: bfloat16 [2, 2, 512, 6144], P('section', None, ('groups', 'shard', 'expert')), parts along dimension 2
There are 2 independent parts, one for each index of `groups`. A program takes and returns all parts, laid end to end along the dimension named above; an argument that names none is the same for every part. Nothing has to cross between parts.
Inputs may be any that keep to these rules, and one draw needn't show every extreme that they name: `route_ids`: the 2 experts of a token differ; among the 32 tokens of one device, one micro-batch and one layer, no expert is named by more than 18 tokens, a bound that some block reaches of them.
All inputs are finite; a program needn't handle non-finite values.
Results may differ from a plain program's by a relative error of at most 0.0064.
Values may be sent and summed in bfloat16 or wider, within the bound.
No kernel may reach another device: no remote copies, remote signals or barrier semaphores. Data moves between devices by JAX's collectives and lax.ppermute only.
A program may use at most 64 MiB of HBM per device.

v0:
```python
import jax
import jax.numpy as jnp
from jax import lax
from jax.sharding import PartitionSpec as P

TOP = 2


def passed_along(shard, axis, by):
    length = lax.axis_size(axis)
    pairs = [(i, i + by) for i in range(length) if 0 <= i + by < length]
    return lax.ppermute(shard, axis, pairs)


def normalize(values, gain_row):
    wide = values.astype(jnp.float32)
    scale = lax.rsqrt(jnp.mean(wide * wide, axis=-1, keepdims=True) + 1e-05)
    return (wide * scale * gain_row).astype(jnp.bfloat16)


def hidden_part(inputs, gate_w, up_w, down_w, row_index, col_index):
    row_total = inputs.shape[0]
    block_size = gate_w.shape[-1]
    block_rows = inputs.shape[1] // block_size
    blocks = inputs.reshape(row_total, block_rows, block_size)
    picked = jnp.take(blocks, row_index.reshape(-1), axis=1)
    picked = picked.reshape(row_total, row_index.shape[0], row_index.shape[1], block_size)
    gate = jnp.einsum("rckd,ckdf->rcf", picked, gate_w, preferred_element_type=jnp.float32)
    up_val = jnp.einsum("rckd,ckdf->rcf", picked, up_w, preferred_element_type=jnp.float32)
    hidden = (jax.nn.silu(gate) * up_val).astype(jnp.bfloat16)
    columns = jnp.arange(block_rows, dtype=jnp.int32)
    part_out = jnp.einsum("rcf,cfo->rco", hidden, down_w[:, 0], preferred_element_type=jnp.float32)
    destinations = (col_index[:, 0][:, None] == columns[None, :]).astype(jnp.float32)
    result = jnp.einsum("rco,cj->rjo", part_out, destinations, precision=lax.Precision.HIGHEST)
    return result


def body(
    tokens,
    norm_gain,
    route_ids,
    route_weights,
    gate_blocks,
    up_blocks,
    down_blocks,
    gate_rows,
    down_cols,
):
    experts_here = gate_blocks.shape[1]
    group_count = lax.axis_size("expert")
    expert_total = group_count * experts_here
    micro_count, row_count, model_width = tokens.shape
    capacity = min(row_count, max(row_count * 9 // 16, row_count * TOP // expert_total + 2))
    section_index = lax.axis_index("section")
    gain_row = norm_gain[0]
    local_blocks = (gate_blocks[0], up_blocks[0], down_blocks[0], gate_rows[0], down_cols[0])
    gathered = (
        lax.all_gather(local_blocks[0], "shard", axis=1, tiled=True),
        lax.all_gather(local_blocks[1], "shard", axis=1, tiled=True),
        lax.all_gather(local_blocks[2], "shard", axis=1, tiled=True),
        lax.all_gather(local_blocks[3], "shard", axis=1, tiled=True),
        lax.all_gather(local_blocks[4], "shard", axis=1, tiled=True),
    )
    handed = jnp.zeros((row_count, model_width), jnp.bfloat16)
    produced = []
    for tick in range(micro_count + 1):
        own_input = tokens[min(tick, micro_count - 1)]
        current = jnp.where(section_index == 0, own_input, handed)
        micro_index = jnp.clip(tick - section_index, 0, micro_count - 1)
        chosen_ids = lax.dynamic_index_in_dim(route_ids[0], micro_index, 0, keepdims=False)
        chosen_weights = lax.dynamic_index_in_dim(route_weights[0], micro_index, 0, keepdims=False)
        normed = normalize(current, gain_row)
        flat_ids = chosen_ids.reshape(-1)
        slot_count = flat_ids.shape[0]
        onehot = (flat_ids[:, None] == jnp.arange(expert_total, dtype=jnp.int32)[None, :]).astype(
            jnp.int32
        )
        before = jnp.cumsum(onehot, axis=0) - onehot
        target = flat_ids * capacity + jnp.sum(before * onehot, axis=1)
        matches = target[None, :] == jnp.arange(expert_total * capacity, dtype=jnp.int32)[:, None]
        filled = jnp.any(matches, axis=1)
        source = (
            jnp.sum(jnp.where(matches, jnp.arange(slot_count, dtype=jnp.int32)[None, :], 0), axis=1)
            // TOP
        )
        outgoing = jnp.where(filled[:, None], normed[source], jnp.zeros((), jnp.bfloat16))
        outgoing = outgoing.reshape(group_count, experts_here, capacity, model_width)
        arrived = lax.all_to_all(outgoing, "expert", split_axis=0, concat_axis=0, tiled=True)
        row_total = arrived.shape[0] * arrived.shape[2]
        inputs = arrived[:, 0].reshape(row_total, model_width)
        totals = hidden_part(
            inputs, gathered[0][0], gathered[1][0], gathered[2][0], gathered[3][0], gathered[4][0]
        )
        outputs = [
            totals.reshape(arrived.shape[0], arrived.shape[2], model_width).astype(jnp.bfloat16)
        ]
        returned = lax.all_to_all(
            jnp.stack(outputs, 1), "expert", split_axis=0, concat_axis=0, tiled=True
        )
        picked = returned.reshape(expert_total * capacity, model_width)[target].reshape(
            row_count, TOP, model_width
        )
        mixed_rows = current.astype(jnp.float32) + jnp.sum(
            chosen_weights[:, :, None] * picked.astype(jnp.float32), axis=1
        )
        result = mixed_rows.astype(jnp.bfloat16)
        produced.append(result)
        if tick < micro_count:
            handed = passed_along(result, "section", 1)
    finished = [
        jnp.where(section_index == 0, produced[index], produced[index + 1])
        for index in range(micro_count)
    ]
    return jnp.stack(finished, 0)[None]


def solution(mesh):
    in_specs = (
        P(None, ("groups", "shard", "expert"), None),
        P("section", None),
        P("section", None, ("groups", "shard", "expert"), None),
        P("section", None, ("groups", "shard", "expert"), None),
        P("section", "expert", "shard", None, None, None),
        P("section", "expert", "shard", None, None, None),
        P("section", "expert", "shard", None, None, None),
        P("section", "expert", "shard", None),
        P("section", "expert", "shard", None),
    )
    out_specs = P("section", None, ("groups", "shard", "expert"), None)
    return jax.shard_map(body, mesh=mesh, in_specs=in_specs, out_specs=out_specs, check_vma=False)
```

profile of v0, /device:TPU:9, one launch (start us, length us, event | category | flops | bytes accessed | tf_op | source)
XLA Modules:
  0.0 358.5 jit_solution(11724038737582841724)
XLA Ops:
  13.2 4.9 %all-to-all-start = ((bf16[4,1,18,6144]{3,2,1,0:T(8,128)(2,1)}), bf16[4,1,18,6144]{3,2,1,0:T(8,128)(2,1)S(1)}, u32[]{:S(2)}, u32[]{:S(2)}) async-start(bf16[4,1,18,6144]{3,2,1,0:T(8,128)(2,1)} %select_bitcast_fusion.2), calls=%async_computation | async-start | bytes 2359296 | tf_op jit(solution)/shard_map/all_to_all | solution.py:88
  19.5 3.6 all-reduce.2
  23.1 19.7 %all-to-all-done = bf16[4,1,18,6144]{3,2,1,0:T(8,128)(2,1)S(1)} async-done(((bf16[4,1,18,6144]{3,2,1,0:T(8,128)(2,1)}), bf16[4,1,18,6144]{3,2,1,0:T(8,128)(2,1)S(1)}, u32[]{:S(2)}, u32[]{:S(2)}) %all-to-all-start) | async-done | bytes 884768 | tf_op jit(solution)/shard_map/all_to_all | solution.py:88
  44.3 3.8 %fusion.28 = f32[64,72,128]{2,1,0:T(8,128)} fusion(bf16[1,1,64,1,128,128]{5,4,3,1,0,2:T(8,128)(2,1)} %all-gather.11.cloned.1.call-done, bf16[64,72,128]{2,1,0:T(8,128)(2,1)S(1)} %gather_fusion.6, pred[64]{0:T(512)(128)(4,1)S(1)} %compare_and_fusion), kind=kOutput, calls=%fused_computation.46 | convolution fusion | flops 151584768 | bytes 5636160 | tf_op jit(solution)/shard_map/rckd,ckdf->rcf/dot_general | solution.py:29
  48.1 29.9 %all-gather.13.cloned.1.call-done = bf16[1,1,64,1,128,128]{5,4,3,1,0,2:T(8,128)(2,1)} async-done(((bf16[1,1,32,1,128,128]{5,4,3,1,0,2:T(8,128)(2,1)}), bf16[1,1,64,1,128,128]{5,4,3,1,0,2:T(8,128)(2,1)}) %all-gather.13.cloned.1.call-update) | async-done | bytes 2097168 | tf_op jit(solution)/shard_map/all_gather | solution.py:60
  78.0 34.7 %all-gather.9.cloned.1.call-done = bf16[1,1,64,1,128,128]{5,4,3,1,0,2:T(8,128)(2,1)} async-done(((bf16[1,1,32,1,128,128]{5,4,3,1,0,2:T(8,128)(2,1)}), bf16[1,1,64,1,128,128]{5,4,3,1,0,2:T(8,128)(2,1)}) %all-gather.9.cloned.1.call-update) | async-done | bytes 2097168 | tf_op jit(solution)/shard_map/all_gather | solution.py:58
  112.7 5.8 %fusion.36 = f32[72,64,128]{2,0,1:T(8,128)} fusion(bf16[1,1,64,1,128,128]{5,4,3,1,0,2:T(8,128)(2,1)} %all-gather.13.cloned.1.call-done, f32[64,72,128]{2,1,0:T(8,128)} %fusion.28, bf16[1,1,64,1,128,128]{5,4,3,1,0,2:T(8,128)(2,1)} %all-gather.9.cloned.1.call-done, bf16[64,72,128]{2,1,0:T(8,128)(2,1)S(1)} %gather_fusion.6, pred[64]{0:T(512)(128)(4,1)S(1)} %compare_and_fusion), kind=kOutput, calls=%fused_computation.54 | convolution fusion | flops 306118656 | bytes 10092608 | tf_op jit(solution)/shard_map/rcf,cfo->rco/dot_general | solution.py:32
  118.5 3.1 fusion.72
  123.1 4.6 %all-to-all-start.1 = ((bf16[4,1,18,6144]{3,2,1,0:T(8,128)(2,1)}), bf16[4,1,18,6144]{3,2,1,0:T(8,128)(2,1)S(1)}, u32[]{:S(2)}, u32[]{:S(2)}) async-start(bf16[4,1,18,6144]{3,2,1,0:T(8,128)(2,1)} %bitcast.22), calls=%async_computation.1 | async-start | bytes 2359296 | tf_op jit(solution)/shard_map/all_to_all | solution.py:97
  130.0 22.3 %all-to-all-done.1 = bf16[4,1,18,6144]{3,2,1,0:T(8,128)(2,1)S(1)} async-done(((bf16[4,1,18,6144]{3,2,1,0:T(8,128)(2,1)}), bf16[4,1,18,6144]{3,2,1,0:T(8,128)(2,1)S(1)}, u32[]{:S(2)}, u32[]{:S(2)}) %all-to-all-start.1) | async-done | bytes 884768 | tf_op jit(solution)/shard_map/all_to_all | solution.py:97
  154.7 2.1 multiply_reduce_fusion.2
  158.3 2.9 collective-permute-done
  164.1 31.9 %all_to_all.30 = bf16[4,1,18,6144]{3,2,1,0:T(8,128)(2,1)S(1)} all-to-all(bf16[4,1,18,6144]{3,2,1,0:T(8,128)(2,1)S(1)} %select_bitcast_fusion.1), channel_id=1, replica_groups=mesh['groups'=2,'shard'=2,'expert'=4,'section'=2] {'expert'}, dimensions={0} | all-to-all | bytes 1769472 | tf_op jit(solution)/shard_map/all_to_all | solution.py:88
  199.0 1.9 gather_fusion.7
  200.8 3.6 %fusion.26 = f32[64,72,128]{2,1,0:T(8,128)} fusion(bf16[1,1,64,1,128,128]{5,4,3,1,0,2:T(8,128)(2,1)S(1)} %copy-done, bf16[64,72,128]{2,1,0:T(8,128)(2,1)} %gather_fusion.7, pred[64]{0:T(512)(128)(4,1)S(1)} %copy-done.18), kind=kOutput, calls=%fused_computation.44 | convolution fusion | flops 151584768 | bytes 5636160 | tf_op jit(solution)/shard_map/rckd,ckdf->rcf/dot_general | solution.py:29
  204.5 5.8 %fusion.39 = f32[72,64,128]{2,0,1:T(8,128)} fusion(bf16[1,1,64,1,128,128]{5,4,3,1,0,2:T(8,128)(2,1)} %all-gather.13.cloned.1.call-done, f32[64,72,128]{2,1,0:T(8,128)} %fusion.26, bf16[1,1,64,1,128,128]{5,4,3,1,0,2:T(8,128)(2,1)} %all-gather.9.cloned.1.call-done, bf16[64,72,128]{2,1,0:T(8,128)(2,1)S(1)} %copy-done.4, pred[64]{0:T(512)(128)(4,1)S(1)} %copy-done.18), kind=kOutput, calls=%fused_computation.55 | convolution fusion | flops 306118656 | bytes 10092608 | tf_op jit(solution)/shard_map/rcf,cfo->rco/dot_general | solution.py:32
  210.3 3.1 fusion.69
  214.9 6.2 %all-to-all-start.3 = ((bf16[4,1,18,6144]{3,2,1,0:T(8,128)(2,1)}), bf16[4,1,18,6144]{3,2,1,0:T(8,128)(2,1)}, u32[]{:S(2)}, u32[]{:S(2)}) async-start(bf16[4,1,18,6144]{3,2,1,0:T(8,128)(2,1)} %bitcast.35), calls=%async_computation.3 | async-start | bytes 2359296 | tf_op jit(solution)/shard_map/all_to_all | solution.py:97
  222.3 23.4 %all-to-all-done.3 = bf16[4,1,18,6144]{3,2,1,0:T(8,128)(2,1)} async-done(((bf16[4,1,18,6144]{3,2,1,0:T(8,128)(2,1)}), bf16[4,1,18,6144]{3,2,1,0:T(8,128)(2,1)}, u32[]{:S(2)}, u32[]{:S(2)}) %all-to-all-start.3) | async-done | bytes 884768 | tf_op jit(solution)/shard_map/all_to_all | solution.py:97
  247.2 1.9 gather_fusion.3
  249.1 3.0 reshape.505
  252.1 3.6 multiply_reduce_fusion.1
  258.0 3.1 collective-permute-done.1
  262.3 2.0 gather_fusion.4
  265.9 32.0 %all_to_all.31 = bf16[4,1,18,6144]{3,2,1,0:T(8,128)(2,1)S(1)} all-to-all(bf16[4,1,18,6144]{3,2,1,0:T(8,128)(2,1)S(1)} %select_bitcast_fusion), channel_id=1, replica_groups=mesh['groups'=2,'shard'=2,'expert'=4,'section'=2] {'expert'}, dimensions={0} | all-to-all | bytes 1769472 | tf_op jit(solution)/shard_map/all_to_all | solution.py:88
  300.7 1.9 gather_fusion.8
  302.6 3.6 %fusion.24 = f32[64,72,128]{2,1,0:T(8,128)} fusion(bf16[1,1,64,1,128,128]{5,4,3,1,0,2:T(8,128)(2,1)S(1)} %copy-done, bf16[64,72,128]{2,1,0:T(8,128)(2,1)} %gather_fusion.8, pred[64]{0:T(512)(128)(4,1)S(1)} %copy-done.18), kind=kOutput, calls=%fused_computation.42 | convolution fusion | flops 151584768 | bytes 5636160 | tf_op jit(solution)/shard_map/rckd,ckdf->rcf/dot_general | solution.py:29
  306.2 5.8 %fusion.42 = f32[72,64,128]{2,0,1:T(8,128)} fusion(bf16[1,1,64,1,128,128]{5,4,3,1,0,2:T(8,128)(2,1)} %all-gather.13.cloned.1.call-done, f32[64,72,128]{2,1,0:T(8,128)} %fusion.24, bf16[1,1,64,1,128,128]{5,4,3,1,0,2:T(8,128)(2,1)} %all-gather.9.cloned.1.call-done, bf16[64,72,128]{2,1,0:T(8,128)(2,1)S(1)} %copy-done.3, pred[64]{0:T(512)(128)(4,1)S(1)} %copy-done.18), kind=kOutput, calls=%fused_computation.56 | convolution fusion | flops 306118656 | bytes 10092608 | tf_op jit(solution)/shard_map/rcf,cfo->rco/dot_general | solution.py:32
  312.1 3.1 fusion.66
  316.7 5.4 %all-to-all-start.5 = ((bf16[4,1,18,6144]{3,2,1,0:T(8,128)(2,1)}), bf16[4,1,18,6144]{3,2,1,0:T(8,128)(2,1)S(1)}, u32[]{:S(2)}, u32[]{:S(2)}) async-start(bf16[4,1,18,6144]{3,2,1,0:T(8,128)(2,1)} %bitcast.48), calls=%async_computation.5 | async-start | bytes 2359296 | tf_op jit(solution)/shard_map/all_to_all | solution.py:97
  322.4 24.1 %all-to-all-done.5 = bf16[4,1,18,6144]{3,2,1,0:T(8,128)(2,1)S(1)} async-done(((bf16[4,1,18,6144]{3,2,1,0:T(8,128)(2,1)}), bf16[4,1,18,6144]{3,2,1,0:T(8,128)(2,1)S(1)}, u32[]{:S(2)}, u32[]{:S(2)}) %all-to-all-start.5) | async-done | bytes 884768 | tf_op jit(solution)/shard_map/all_to_all | solution.py:97
  348.8 2.1 multiply_reduce_fusion
  (177 shorter events, 39.3 us)
Async XLA Ops:
  6.5 3.6 %copy-start.1 = (bf16[2,32,6144]{2,1,0:T(8,128)(2,1)S(1)}, bf16[2,32,6144]{2,1,0:T(8,128)(2,1)}, u32[]{:S(2)}) copy-start(bf16[2,32,6144]{2,1,0:T(8,128)(2,1)} %param.11) | copy-start | bytes 2359300
  6.5 37.8 %all-gather.11.cloned.1.call-start = ((), (), s32[]{:S(2)}) async-start(), calls=%async_computation.7 | async-start | bytes 3145728 | tf_op jit(solution)/shard_map/all_gather | solution.py:59
  6.5 3.9 %copy-start.14 = (f32[1,6144]{1,0:T(1,128)S(1)}, f32[1,6144]{1,0:T(1,128)}, u32[]{:S(2)}) copy-start(f32[1,6144]{1,0:T(1,128)} %param.12) | copy-start | bytes 73732
  7.3 70.7 %all-gather.13.cloned.1.call-start = ((), (), s32[]{:S(2)}) async-start(), calls=%async_computation.8 | async-start | bytes 3145728 | tf_op jit(solution)/shard_map/all_gather | solution.py:60
  8.0 104.7 %all-gather.9.cloned.1.call-start = ((), (), s32[]{:S(2)}) async-start(), calls=%async_computation.6 | async-start | bytes 3145728 | tf_op jit(solution)/shard_map/all_gather | solution.py:58
  13.2 4.9 %copy-start.33 = (u32[32]{0:T(128)S(1)}, u32[32]{0:T(128)}, u32[]{:S(2)}) copy-start(u32[32]{0:T(128)} %constant.115) | copy-start | bytes 388
  13.2 6.1 %copy-start.31 = (s32[1,1,32,1]{2,3,1,0:T(1,128)S(1)}, s32[1,1,32,1]{2,3,1,0:T(1,128)}, u32[]{:S(2)}) copy-start(s32[1,1,32,1]{2,3,1,0:T(1,128)} %param.18) | copy-start | bytes 388
  13.2 6.2 %copy-start.32 = (s32[1,1,32,1]{2,3,1,0:T(1,128)S(1)}, s32[1,1,32,1]{2,3,1,0:T(1,128)}, u32[]{:S(2)}) copy-start(s32[1,1,32,1]{2,3,1,0:T(1,128)} %param.19) | copy-start | bytes 388
  13.2 29.5 %all-to-all-start = ((bf16[4,1,18,6144]{3,2,1,0:T(8,128)(2,1)}), bf16[4,1,18,6144]{3,2,1,0:T(8,128)(2,1)S(1)}, u32[]{:S(2)}, u32[]{:S(2)}) async-start(bf16[4,1,18,6144]{3,2,1,0:T(8,128)(2,1)} %select_bitcast_fusion.2), calls=%async_computation | async-start | bytes 2359296 | tf_op jit(solution)/shard_map/all_to_all | solution.py:88
  23.0 95.5 %copy-start.21 = (s32[64]{0:T(128)}, s32[64]{0:T(128)S(1)}, u32[]{:S(2)}) copy-start(s32[64]{0:T(128)S(1)} %get-tuple-element.7) | copy-start | bytes 772
  23.0 20.4 %copy-start.16 = (s32[1024]{0:T(1024)}, s32[1024]{0:T(1024)S(1)}, u32[]{:S(2)}) copy-start(s32[1024]{0:T(1024)S(1)} %pad_clamp_fusion.5) | copy-start | bytes 12292
  23.1 89.6 %copy-start.17 = (pred[64]{0:T(512)(128)(4,1)}, pred[64]{0:T(512)(128)(4,1)S(1)}, u32[]{:S(2)}) copy-start(pred[64]{0:T(512)(128)(4,1)S(1)} %compare_and_fusion) | copy-start | bytes 196
  121.7 6.2 %copy-start.20 = (f32[1,2,32,2]{2,3,1,0:T(2,128)S(1)}, f32[1,2,32,2]{2,3,1,0:T(2,128)}, u32[]{:S(2)}) copy-start(f32[1,2,32,2]{2,3,1,0:T(2,128)} %param.14) | copy-start | bytes 1540
  123.1 29.2 %all-to-all-start.1 = ((bf16[4,1,18,6144]{3,2,1,0:T(8,128)(2,1)}), bf16[4,1,18,6144]{3,2,1,0:T(8,128)(2,1)S(1)}, u32[]{:S(2)}, u32[]{:S(2)}) async-start(bf16[4,1,18,6144]{3,2,1,0:T(8,128)(2,1)} %bitcast.22), calls=%async_computation.1 | async-start | bytes 2359296 | tf_op jit(solution)/shard_map/all_to_all | solution.py:97
  156.7 4.8 %copy-start.15 = (f32[1,6144]{1,0:T(1,128)S(1)}, f32[1,6144]{1,0:T(1,128)}, u32[]{:S(2)}) copy-start(f32[1,6144]{1,0:T(1,128)} %param.12) | copy-start | bytes 73732
  156.8 4.6 %copy-start.9 = (bf16[32,6144]{1,0:T(8,128)(2,1)}, bf16[32,6144]{1,0:T(8,128)(2,1)S(1)}, u32[]{:S(2)}) copy-start(bf16[32,6144]{1,0:T(8,128)(2,1)S(1)} %fusion.98) | copy-start | bytes 1179652
  156.8 4.4 %collective-permute-start = (bf16[32,6144]{1,0:T(8,128)(2,1)S(1)}, bf16[32,6144]{1,0:T(8,128)(2,1)S(1)}, u32[]{:S(2)}, u32[]{:S(2)}) collective-permute-start(bf16[32,6144]{1,0:T(8,128)(2,1)S(1)} %fusion.98), channel_id=1, source_target_pairs={{0,1},{2,3},{4,5},{6,7},{8,9},{10,11},{12,13},{14,15},{16,17},{18,... | collective-permute-start | bytes 1179656 | tf_op jit(solution)/shard_map/ppermute | solution.py:12
  200.8 3.6 %copy-start.4 = (bf16[64,72,128]{2,1,0:T(8,128)(2,1)S(1)}, bf16[64,72,128]{2,1,0:T(8,128)(2,1)}, u32[]{:S(2)}) copy-start(bf16[64,72,128]{2,1,0:T(8,128)(2,1)} %gather_fusion.7) | copy-start | bytes 3538948
  204.5 5.8 %copy-start.22 = (s32[64]{0:T(128)S(1)}, s32[64]{0:T(128)}, u32[]{:S(2)}) copy-start(s32[64]{0:T(128)} %copy-done.21) | copy-start | bytes 772
  213.4 7.8 %copy-start.27 = (s32[1,1,32,2]{2,3,1,0:T(2,128)S(1)}, s32[1,1,32,2]{2,3,1,0:T(2,128)}, u32[]{:S(2)}) copy-start(s32[1,1,32,2]{2,3,1,0:T(2,128)} %get-tuple-element.25) | copy-start | bytes 772
  213.4 7.9 %copy-start.24 = (f32[32,2]{0,1:T(2,128)S(1)}, f32[32,2]{0,1:T(2,128)}, u32[]{:S(2)}) copy-start(f32[32,2]{0,1:T(2,128)} %get-tuple-element.22) | copy-start | bytes 772
  213.4 8.0 %copy-start.26 = (s32[1,1,32,2]{2,3,1,0:T(2,128)S(1)}, s32[1,1,32,2]{2,3,1,0:T(2,128)}, u32[]{:S(2)}) copy-start(s32[1,1,32,2]{2,3,1,0:T(2,128)} %get-tuple-element.11) | copy-start | bytes 772
  214.9 7.3 %copy-start.29 = (s32[64]{0:T(128)S(1)}, s32[64]{0:T(128)}, u32[]{:S(2)}) copy-start(s32[64]{0:T(128)} %copy-done.28) | copy-start | bytes 772
  214.9 30.7 %all-to-all-start.3 = ((bf16[4,1,18,6144]{3,2,1,0:T(8,128)(2,1)}), bf16[4,1,18,6144]{3,2,1,0:T(8,128)(2,1)}, u32[]{:S(2)}, u32[]{:S(2)}) async-start(bf16[4,1,18,6144]{3,2,1,0:T(8,128)(2,1)} %bitcast.35), calls=%async_computation.3 | async-start | bytes 2359296 | tf_op jit(solution)/shard_map/all_to_all | solution.py:97
  252.1 3.6 %copy-start.10 = (bf16[32,6144]{1,0:T(8,128)(2,1)S(1)}, bf16[32,6144]{1,0:T(8,128)(2,1)}, u32[]{:S(2)}) copy-start(bf16[32,6144]{1,0:T(8,128)(2,1)} %copy-done.9) | copy-start | bytes 1179652
  255.7 5.4 %copy-start.2 = (bf16[2,32,6144]{2,1,0:T(8,128)(2,1)S(1)}, bf16[2,32,6144]{2,1,0:T(8,128)(2,1)}, u32[]{:S(2)}) copy-start(bf16[2,32,6144]{2,1,0:T(8,128)(2,1)} %param.11) | copy-start | bytes 2359300
  256.6 4.8 %copy-start.12 = (bf16[32,6144]{1,0:T(8,128)(2,1)}, bf16[32,6144]{1,0:T(8,128)(2,1)S(1)}, u32[]{:S(2)}) copy-start(bf16[32,6144]{1,0:T(8,128)(2,1)S(1)} %get-tuple-element.9) | copy-start | bytes 1179652
  256.6 4.5 %collective-permute-start.1 = (bf16[32,6144]{1,0:T(8,128)(2,1)S(1)}, bf16[32,6144]{1,0:T(8,128)(2,1)S(1)}, u32[]{:S(2)}, u32[]{:S(2)}) collective-permute-start(bf16[32,6144]{1,0:T(8,128)(2,1)S(1)} %get-tuple-element.9), channel_id=1, source_target_pairs={{0,1},{2,3},{4,5},{6,7},{8,9},{10,11},{12,13},{14,15},{16,17},{18,... | collective-permute-start | bytes 1179656 | tf_op jit(solution)/shard_map/ppermute | solution.py:12
  302.6 3.6 %copy-start.3 = (bf16[64,72,128]{2,1,0:T(8,128)(2,1)S(1)}, bf16[64,72,128]{2,1,0:T(8,128)(2,1)}, u32[]{:S(2)}) copy-start(bf16[64,72,128]{2,1,0:T(8,128)(2,1)} %gather_fusion.8) | copy-start | bytes 3538948
  315.2 6.9 %copy-start.25 = (s32[1,1,32,2]{2,3,1,0:T(2,128)S(1)}, s32[1,1,32,2]{2,3,1,0:T(2,128)}, u32[]{:S(2)}) copy-start(s32[1,1,32,2]{2,3,1,0:T(2,128)} %get-tuple-element.10) | copy-start | bytes 772
  315.2 7.1 %copy-start.23 = (f32[32,2]{0,1:T(2,128)S(1)}, f32[32,2]{0,1:T(2,128)}, u32[]{:S(2)}) copy-start(f32[32,2]{0,1:T(2,128)} %get-tuple-element.20) | copy-start | bytes 772
  316.7 29.8 %all-to-all-start.5 = ((bf16[4,1,18,6144]{3,2,1,0:T(8,128)(2,1)}), bf16[4,1,18,6144]{3,2,1,0:T(8,128)(2,1)S(1)}, u32[]{:S(2)}, u32[]{:S(2)}) async-start(bf16[4,1,18,6144]{3,2,1,0:T(8,128)(2,1)} %bitcast.48), calls=%async_computation.5 | async-start | bytes 2359296 | tf_op jit(solution)/shard_map/all_to_all | solution.py:97
  (13 other events, 26.4 us)
Sparse Core Ops, SparseCore 0:
  8.9 34.3 all-gather.10
  44.8 33.1 all-gather.12
  79.5 33.1 all-gather.8
where the time goes:
time: 365 us; the launch traced here: 359 us
  waiting for transfers between devices  162 us (44%)
  blocking collectives  67.5 us (18%)
  local copies, waits for them, and re-layouts  38.1 us (10%)
  matrix products  37.9 us (10%)
  starting transfers between devices  23.7 us (6%)
  other arithmetic  14.8 us (4%)
  between operations  14.4 us (4%)
    all_to_all x3, waiting for transfers between devices, body(): lax.all_to_all(jnp.stack(outputs, 1), 'expert', split_axis=0, concat_axis...  69.8 us
    all_to_all x2, blocking collectives, body(): lax.all_to_all(outgoing, 'expert', split_axis=0, concat_axis=0, tiled=True)  63.9 us
    all_gather x1, waiting for transfers between devices, body(): lax.all_gather(local_blocks[0], 'shard', axis=1, tiled=True)  34.7 us
    all_gather x1, waiting for transfers between devices, body(): lax.all_gather(local_blocks[2], 'shard', axis=1, tiled=True)  29.9 us
    all_to_all x1, waiting for transfers between devices, body(): lax.all_to_all(outgoing, 'expert', split_axis=0, concat_axis=0, tiled=True)  19.7 us
    dot_general x3, matrix products, hidden_part(): jnp.einsum('rcf,cfo->rco', hidden, down_w[:, 0], preferred_element_type=j...  17.5 us
    all_to_all x3, starting transfers between devices, body(): lax.all_to_all(jnp.stack(outputs, 1), 'expert', split_axis=0, concat_axis...  16.2 us
    dot_general x3, matrix products, hidden_part(): jnp.einsum('rckd,ckdf->rcf', picked, up_w, preferred_element_type=jnp.flo...  11.1 us
  transfers between devices with their start and end apart: 9, of which 8 were waited for; matrix products, arithmetic and copies ran while one was open for 4% of the time, Pallas kernels for 0%

commit v1 on v0

v1 whole, which is shorter than its diff:
```python
import functools
import math

import jax
import jax.numpy as jnp
from jax import lax
from jax.experimental import pallas as pl
from jax.experimental.pallas import tpu as pltpu
from jax.sharding import PartitionSpec as P

TOP = 2
LANES = 128
EPS = 1e-05
MIB = 1 << 20


def up_to(value, unit):
    return -(-value // unit) * unit


def group_of(capacity):
    return 16 // math.gcd(capacity, 16)


def iota(shape, axis):
    return lax.broadcasted_iota(jnp.int32, shape, axis)


def split_by(values, unit):
    quotient = jnp.floor((values.astype(jnp.float32) + 0.5) * (1.0 / unit)).astype(jnp.int32)
    return quotient, values - quotient * unit


def dot(left, right, contract=((1,), (0,))):
    return lax.dot_general(left, right, (contract, ((), ())), preferred_element_type=jnp.float32)


def spread_columns(values, rows):
    tokens = values.shape[1]
    token = split_by(iota((rows, tokens), 0), tokens)[1]
    same = iota((rows, tokens), 1) == token
    return [
        jnp.sum(jnp.where(same, values[choice : choice + 1, :], 0.0), axis=1, keepdims=True) for choice in range(TOP)
    ]


def picks_to_send(ids, experts, capacity, group):
    tokens = ids.shape[1]
    expert = iota((up_to(experts, 16), tokens), 0)
    hit = (ids[0:1, :] == expert) | (ids[1:2, :] == expert)
    hit = jnp.where(hit, 1.0, 0.0).astype(jnp.bfloat16)
    shape = (tokens, group * tokens)
    block, token = split_by(iota(shape, 1), tokens)
    earlier = jnp.where(iota(shape, 0) < token, 1.0, 0.0).astype(jnp.bfloat16)
    same = jnp.where(iota(shape, 0) == token, 1.0, 0.0).astype(jnp.bfloat16)
    slot = dot(hit, earlier)
    here = dot(hit, same)
    first = (block[0:1, :] * capacity).astype(jnp.float32)
    key = jnp.where(here > 0.5, slot + first, -1.0)
    row = iota((group * capacity, group * tokens), 0).astype(jnp.float32)
    return jnp.concatenate(
        [jnp.where(row == key[k : k + 1, :], 1.0, 0.0) for k in range(experts)], axis=0
    ).astype(jnp.bfloat16)


def picks_to_mix(ids, experts, capacity, group):
    tokens = ids.shape[1]
    rows = group * tokens
    token = split_by(iota((rows, tokens), 0), tokens)[1]
    first = (split_by(iota((rows, 1), 0), tokens)[0] * capacity).astype(jnp.float32)
    columns = iota((rows, experts * group * capacity), 1).astype(jnp.float32)
    earlier = iota((rows, tokens), 1) < token
    chosen = spread_columns(ids.astype(jnp.float32), rows)
    parts = []
    for choice in range(TOP):
        expert = chosen[choice]
        named = (ids[0:1, :].astype(jnp.float32) == expert) | (ids[1:2, :].astype(jnp.float32) == expert)
        slot = jnp.sum(jnp.where(named & earlier, 1.0, 0.0), axis=1, keepdims=True)
        key = expert * (group * capacity) + first + slot
        parts.append(jnp.where(columns == key, 1.0, 0.0))
    return jnp.concatenate(parts, axis=0).astype(jnp.bfloat16)


class Layer:
    def __init__(self, info, layer, own, other):
        self.held = info[0] == layer
        self.section, self.own, self.other = info[0], own, other

    def rows(self, at):
        return jnp.where(self.held, self.own[at][0, self.section], self.other[at][0, self.section])

    def gain(self, at, block):
        lanes = slice(block * LANES, (block + 1) * LANES)
        return jnp.where(self.held, self.own[at][0:1, lanes], self.other[at][0:1, lanes])


def send_rows(ids, state, scale, gain_of, out, experts, group, capacity, tokens):
    count = group * capacity
    blocks = state.shape[0] // tokens
    picks = picks_to_send(ids, experts, capacity, group)
    scale = jnp.concatenate([scale] * group, axis=0)
    for number in range(blocks // group):
        rows = state[number * group * tokens : (number + 1) * group * tokens, :]
        gain = jnp.concatenate(
            [jnp.broadcast_to(gain_of(number * group + j), (tokens, LANES)) for j in range(group)], axis=0
        )
        normed = (rows.astype(jnp.float32) * scale * gain).astype(jnp.bfloat16)
        picked = dot(picks, normed).astype(jnp.bfloat16)
        for e in range(experts):
            start = e * blocks * capacity + number * count
            out[start : start + count, :] = picked[e * count : (e + 1) * count, :]


def first_send_kernel(experts, capacity, group, info, tokens_ref, ids, gain, other_ids, other_gain, *rest):
    out, given, state, arrived = rest[-4:]
    section = info[0]
    copy = pltpu.make_async_copy(tokens_ref.at[section], given, arrived.at[0])
    copy.start()
    copy.wait()
    layer = Layer(info, 0, (ids, gain), (other_ids, other_gain))
    tokens, width = given.shape
    blocks = width // LANES
    total = jnp.zeros((tokens, 1), jnp.float32)
    for b in range(blocks):
        part = given[:, b * LANES : (b + 1) * LANES]
        state[b * tokens : (b + 1) * tokens, :] = part
        wide = part.astype(jnp.float32)
        total += jnp.sum(wide * wide, axis=1, keepdims=True)
    scale = lax.rsqrt(total * (1.0 / width) + EPS)
    send_rows(layer.rows(0), state, scale, lambda b: layer.gain(1, b), out, experts, group, capacity, tokens)


def mix_rows(picks, base, weights, returned, number, experts, blocks, group, capacity, tokens):
    count = group * capacity
    starts = [e * blocks * capacity + number * count for e in range(experts)]
    given = jnp.concatenate([returned[start : start + count, :] for start in starts], axis=0)
    picked = dot(picks, given)
    rows = group * tokens
    total = base.astype(jnp.float32)
    for choice in range(TOP):
        total += weights[choice] * picked[choice * rows : (choice + 1) * rows, :]
    return total.astype(jnp.bfloat16)


def relay_kernel(experts, capacity, group, info, tokens_ref, returned, ids, weights, gain, other_ids, other_weights, other_gain, *rest):
    state_out, state, out, given, arrived = rest
    section = info[0]
    copy = pltpu.make_async_copy(tokens_ref.at[section], given, arrived.at[0])
    copy.start()
    first = Layer(info, 0, (ids, weights), (other_ids, other_weights))
    second = Layer(info, 1, (ids, gain), (other_ids, other_gain))
    tokens, width = given.shape
    blocks = width // LANES
    picks = picks_to_mix(first.rows(0), experts, capacity, group)
    shares = spread_columns(first.rows(1), group * tokens)
    total = jnp.zeros((tokens, 1), jnp.float32)
    copy.wait()
    for number in range(blocks // group):
        base = jnp.concatenate(
            [given[:, b * LANES : (b + 1) * LANES] for b in range(number * group, (number + 1) * group)], axis=0
        )
        mixed = mix_rows(picks, base, shares, returned, number, experts, blocks, group, capacity, tokens)
        state[number * group * tokens : (number + 1) * group * tokens, :] = mixed
        wide = mixed.astype(jnp.float32)
        square = jnp.sum(wide * wide, axis=1, keepdims=True)
        for j in range(group):
            b = number * group + j
            state_out[:, b * LANES : (b + 1) * LANES] = mixed[j * tokens : (j + 1) * tokens, :]
            total += square[j * tokens : (j + 1) * tokens, :]
    scale = lax.rsqrt(total * (1.0 / width) + EPS)
    send_rows(second.rows(0), state, scale, lambda b: second.gain(1, b), out, experts, group, capacity, tokens)


def last_kernel(experts, capacity, group, info, first, state, returned, ids, weights, other_ids, other_weights, out, leaving):
    layer = Layer(info, 1, (ids, weights), (other_ids, other_weights))
    tokens, width = out.shape
    blocks = width // LANES
    picks = picks_to_mix(layer.rows(0), experts, capacity, group)
    shares = spread_columns(layer.rows(1), group * tokens)
    for number in range(blocks // group):
        base = state[number * group * tokens : (number + 1) * group * tokens, :]
        mixed = mix_rows(picks, base, shares, returned, number, experts, blocks, group, capacity, tokens)
        for j in range(group):
            b = number * group + j
            out[:, b * LANES : (b + 1) * LANES] = mixed[j * tokens : (j + 1) * tokens, :]

    @pl.when(info[0] == 0)
    def _():
        leaving[...] = out[...]

    @pl.when(info[0] != 0)
    def _():
        leaving[...] = first[...]


def join_kernel(info, first, second, came, out):
    @pl.when(info[0] == 0)
    def _():
        out[0, 0] = first[...]
        out[0, 1] = came[...]

    @pl.when(info[0] != 0)
    def _():
        out[0, 0] = came[...]
        out[0, 1] = second[...]


def expert_kernel(section, experts, capacity, group, split, unroll, info, *refs):
    @pl.when(info[0] == section)
    def _():
        expert_rows(experts, capacity, group, split, unroll, *refs)


def expert_rows(experts, capacity, group, split, unroll, *refs):
    halves, first = [], 0
    for pieces in split:
        halves.append(refs[first : first + pieces])
        first += pieces
    given, out = refs[first], refs[-11]
    numbers, places, placed, weights, arrived, state, hidden, total, made, left = refs[-10:]
    blocks = state.shape[0]
    padded = state.shape[1] // experts
    columns = (weights.shape[1] - 1) // 3
    count = group * capacity
    sizes = [columns] * 3 + [1]

    def load(half, which):
        source, start = halves[half][0], which * columns
        if len(halves[half]) > 1:
            source, start = halves[half][min(which, 2)], columns if which == 3 else 0
        return pltpu.make_async_copy(
            source.at[pl.ds(start, sizes[which])],
            weights.at[half, pl.ds(which * columns, sizes[which])],
            arrived.at[half, which],
        )

    for which in (3, 0, 1, 2):
        for half in range(len(halves)):
            load(half, which).start()

    shape = (group * padded, count)
    block, slot = split_by(iota((group * padded, 1), 0), padded)
    key = jnp.where(slot < capacity, block * capacity + slot, -1)
    spread = jnp.where(iota(shape, 1) == key, 1.0, 0.0).astype(jnp.bfloat16)
    for number in range(blocks // group):
        starts = [e * blocks * capacity + number * count for e in range(experts)]
        spaced = [dot(spread, given[start : start + count, :]) for start in starts]
        for j in range(group):
            rows = jnp.concatenate([s[j * padded : (j + 1) * padded, :] for s in spaced], axis=0)
            state[number * group + j] = rows.astype(jnp.bfloat16)
            total[number * group + j] = jnp.zeros(rows.shape, jnp.float32)

    for half in range(len(halves)):
        load(half, 3).wait()
        numbers[half] = weights[half, 3 * columns, :16, :].astype(jnp.float32)[:8, :].astype(jnp.int32)
    moves = [pltpu.make_async_copy(numbers.at[half], places.at[half], placed.at[half]) for half in range(len(halves))]
    for move in moves:
        move.start()
    for move in moves:
        move.wait()

    for half in range(len(halves)):
        load(half, 0).wait()
        load(half, 1).wait()

        def up_step(at, carry, half=half):
            for i in range(unroll):
                c = at * unroll + i
                rows = state[places[half, 0, c]]
                both = dot(rows, jnp.concatenate([weights[half, c], weights[half, columns + c]], axis=1))
                gate, up = both[:, :LANES], both[:, LANES:]
                hidden[half * columns + c] = (gate / (1.0 + jnp.exp(-gate)) * up).astype(jnp.bfloat16)
            return carry

        lax.fori_loop(0, columns // unroll, up_step, 0)

    for half in range(len(halves)):
        load(half, 2).wait()

        def down_step(at, carry, half=half):
            produced = []
            for i in range(unroll):
                c = at * unroll + i
                produced.append(dot(hidden[half * columns + c], weights[half, 2 * columns + c]))
            for i in range(unroll):
                to = places[half, 1, at * unroll + i]
                total[to] = total[to] + produced[i]
            return carry

        lax.fori_loop(0, columns // unroll, down_step, 0)

    block, slot = split_by(iota((count, 1), 0), capacity)
    packing = jnp.where(iota((count, group * padded), 1) == block * padded + slot, 1.0, 0.0).astype(jnp.bfloat16)
    size = blocks * capacity
    copies = [
        pltpu.make_async_copy(made.at[pl.ds(e * size, size)], out.at[pl.ds(e * size, size)], left.at[e])
        for e in range(experts)
    ]
    for e in range(experts):
        for number in range(blocks // group):
            spaced = jnp.concatenate(
                [total[number * group + j, e * padded : (e + 1) * padded, :] for j in range(group)], axis=0
            ).astype(jnp.bfloat16)
            start = e * size + number * count
            made[start : start + count, :] = dot(packing, spaced).astype(jnp.bfloat16)
        copies[e].start()
    for copy in copies:
        copy.wait()


def pack_kernel(info, in_rows, out_cols, *refs):
    stored, (out, kept, arrived, left) = refs[:3], refs[-4:]
    columns = (kept.shape[0] - 1) // 3

    def take(which):
        return pltpu.make_async_copy(stored[which], kept.at[pl.ds(which * columns, columns)], arrived.at[which])

    def give(which):
        span = pl.ds(which * columns, columns + which // 2)
        return pltpu.make_async_copy(kept.at[span], out.at[span], left.at[which])

    for which in range(3):
        take(which).start()
    spread = jnp.where(iota((columns, LANES), 0) == iota((columns, LANES), 1), 1.0, 0.0).astype(jnp.bfloat16)
    row = iota((LANES, LANES), 0)
    rows, cols = (
        dot(jnp.broadcast_to(p[...].astype(jnp.float32), (LANES, columns)).astype(jnp.bfloat16), spread)
        for p in (in_rows, out_cols)
    )
    kept[3 * columns] = jnp.where(row == 0, rows, jnp.where(row == 1, cols, 0.0)).astype(jnp.bfloat16)
    for which in range(3):
        take(which).wait()
        give(which).start()
    for which in range(3):
        give(which).wait()


def tie_kernel(*refs):
    pass


SMEM = pl.BlockSpec(memory_space=pltpu.SMEM)
VMEM = pl.BlockSpec(memory_space=pltpu.VMEM)
ANY = pl.BlockSpec(memory_space=pl.ANY)


def cost(microseconds):
    return pl.CostEstimate(flops=0, bytes_accessed=int(microseconds * 3.69e6), transcendentals=0)


def held(*arrays):
    return [pltpu.with_memory_space_constraint(a, pltpu.HBM) for a in arrays]


def pack(info, places, weights, after):
    columns, *block = weights[0].shape
    shape = (3 * columns + 1, *block)
    return pl.pallas_call(
        pack_kernel,
        out_shape=pltpu.HBM(shape, jnp.bfloat16),
        in_specs=[SMEM, VMEM, VMEM] + [ANY] * (3 + len(after)),
        out_specs=ANY,
        scratch_shapes=[
            pltpu.VMEM(shape, jnp.bfloat16),
            pltpu.SemaphoreType.DMA((3,)),
            pltpu.SemaphoreType.DMA((3,)),
        ],
        compiler_params=pltpu.CompilerParams(vmem_limit_bytes=8 * MIB),
        cost_estimate=cost(4),
        name="pack",
    )(info, *places, *held(*weights), *after)


def tie(array, *others):
    return pl.pallas_call(
        tie_kernel,
        out_shape=pltpu.HBM(array.shape, array.dtype),
        in_specs=[ANY] * (1 + len(others)),
        out_specs=ANY,
        input_output_aliases={0: 0},
        cost_estimate=cost(0),
        name="tie",
    )(*held(array), *others)


def body(tokens, norm_gain, route_ids, route_weights, gate_blocks, up_blocks, down_blocks, gate_rows, down_cols):
    experts = lax.axis_size("expert")
    sections = lax.axis_size("section")
    shards = lax.axis_size("shard")
    micro_count, row_count, width = tokens.shape
    assert sections == micro_count == TOP and gate_blocks.shape[1] == 1
    blocks = width // LANES
    capacity = min(row_count, max(row_count * 9 // 16, row_count * TOP // experts + 2))
    group = group_of(capacity)
    packed_rows = experts * blocks * capacity
    padded = up_to(capacity, 8)
    bf16, f32 = jnp.bfloat16, jnp.float32
    info = lax.axis_index("section").astype(jnp.int32).reshape(1)
    weights = [a.reshape(a.shape[2:3] + a.shape[4:]) for a in (gate_blocks, up_blocks, down_blocks)]
    places = [a.reshape(1, -1) for a in (gate_rows, down_cols)]
    ids, shares = jnp.swapaxes(route_ids, 2, 3), jnp.swapaxes(route_weights, 2, 3)
    swap = [(0, 1), (1, 0)]

    def across(array, section):
        pairs = [(a * sections + section, b * sections + section) for a, b in swap]
        return lax.ppermute(array, ("shard", "section"), pairs)

    def other(array, pairs=swap):
        return lax.ppermute(array, "section", pairs)

    paired = shards == 2
    if not paired:
        weights = [lax.all_gather(a, "shard", axis=0, tiled=True) for a in weights]
        places = [lax.all_gather(a, "shard", axis=1, tiled=True) for a in places]
    columns = weights[0].shape[0]
    assert columns <= LANES

    other_ids, other_shares, other_gain = other(ids), other(shares), other(norm_gain)
    rows_shape = jax.ShapeDtypeStruct((packed_rows, LANES), bf16)
    state_shape = jax.ShapeDtypeStruct((row_count, width), bf16)
    blocks_shape = jax.ShapeDtypeStruct((blocks * row_count, LANES), bf16)
    tokens_scratch = [pltpu.VMEM((row_count, width), bf16)]

    def call(kernel, name, microseconds, out_shape, args, specs, scratch, limit):
        return pl.pallas_call(
            kernel,
            out_shape=out_shape,
            in_specs=specs,
            out_specs=jax.tree.map(lambda _: VMEM, out_shape),
            scratch_shapes=scratch,
            compiler_params=pltpu.CompilerParams(vmem_limit_bytes=limit * MIB),
            cost_estimate=cost(microseconds),
            name=name,
        )(*args)

    def exchange(rows):
        rows = rows.reshape(experts, packed_rows // experts, LANES)
        return lax.all_to_all(rows, "expert", split_axis=0, concat_axis=0, tiled=True).reshape(packed_rows, LANES)

    def expert_on(section, sources, rows, earlier):
        return pl.pallas_call(
            functools.partial(
                expert_kernel, section, experts, capacity, group, [len(s) for s in sources], math.gcd(columns, 16)
            ),
            out_shape=rows_shape,
            in_specs=[SMEM] + [ANY] * sum(len(s) for s in sources) + [VMEM] + [ANY] * len(earlier),
            out_specs=ANY,
            scratch_shapes=[
                pltpu.VMEM((len(sources), 8, LANES), jnp.int32),
                pltpu.SMEM((len(sources), 8, LANES), jnp.int32),
                pltpu.SemaphoreType.DMA((len(sources),)),
                pltpu.VMEM((len(sources), 3 * columns + 1) + weights[0].shape[1:], bf16),
                pltpu.SemaphoreType.DMA((len(sources), 4)),
                pltpu.VMEM((blocks, experts * padded, LANES), bf16),
                pltpu.VMEM((len(sources) * columns, experts * padded, LANES), bf16),
                pltpu.VMEM((blocks, experts * padded, LANES), f32),
                pltpu.VMEM((packed_rows, LANES), bf16),
                pltpu.SemaphoreType.DMA((experts,)),
            ],
            input_output_aliases={2 + sum(len(s) for s in sources): 0} if earlier else {},
            compiler_params=pltpu.CompilerParams(vmem_limit_bytes=20 * MIB),
            cost_estimate=cost(7),
            name="expert",
        )(info, *held(*(a for s in sources for a in s)), rows, *earlier)

    packed = pack(info, places, weights, [])
    swapped = other(packed)
    sent = call(
        functools.partial(first_send_kernel, experts, capacity, group),
        "first_send",
        3,
        rows_shape,
        (info, *held(tokens), ids, norm_gain, other_ids, other_gain, packed, other_shares),
        [SMEM, ANY, VMEM, VMEM, VMEM, VMEM, ANY, ANY],
        tokens_scratch + [pltpu.VMEM((blocks * row_count, LANES), bf16), pltpu.SemaphoreType.DMA((1,))],
        12,
    )
    given_rows = exchange(sent)
    if paired:
        moved = tie(across(packed, 0), given_rows)
        passed = other(moved, [(0, 1)])
        sources = [[[packed], [moved]], [[swapped], [passed]]]
    else:
        sources = [[[packed]], [[swapped]]]
    done = expert_on(0, sources[0], given_rows, [])
    if paired:
        swapped = tie(swapped, done)
        whole = across(swapped, 0)
    returned = exchange(expert_on(1, sources[1], given_rows, [done]))
    first, state, sent = call(
        functools.partial(relay_kernel, experts, capacity, group),
        "relay",
        3,
        [state_shape, blocks_shape, rows_shape],
        (info, *held(tokens), returned, ids, shares, norm_gain, other_ids, other_shares, other_gain),
        [SMEM, ANY] + [VMEM] * 7,
        tokens_scratch + [pltpu.SemaphoreType.DMA((1,))],
        12,
    )
    given_rows = exchange(sent)
    if paired:
        whole = tie(whole, first)
        passed = other(whole, [(0, 1)])
        sources = [[[swapped], [whole]], [[packed], [passed]]]
    else:
        sources = [[[swapped]], [[packed]]]
    done = expert_on(0, sources[0], given_rows, [])
    returned = exchange(expert_on(1, sources[1], given_rows, [done]))
    second, leaving = call(
        functools.partial(last_kernel, experts, capacity, group),
        "last",
        3,
        [state_shape] * 2,
        (info, first, state, returned, ids, shares, other_ids, other_shares),
        [SMEM] + [VMEM] * 7,
        [],
        12,
    )
    return call(
        join_kernel,
        "join",
        1,
        jax.ShapeDtypeStruct((1, micro_count, row_count, width), bf16),
        (info, first, second, other(leaving)),
        [SMEM] + [VMEM] * 3,
        [],
        12,
    )


def solution(mesh):
    in_specs = (
        P(None, ("groups", "shard", "expert"), None),
        P("section", None),
        P("section", None, ("groups", "shard", "expert"), None),
        P("section", None, ("groups", "shard", "expert"), None),
        P("section", "expert", "shard", None, None, None),
        P("section", "expert", "shard", None, None, None),
        P("section", "expert", "shard", None, None, None),
        P("section", "expert", "shard", None),
        P("section", "expert", "shard", None),
    )
    out_specs = P("section", None, ("groups", "shard", "expert"), None)
    return jax.shard_map(body, mesh=mesh, in_specs=in_specs, out_specs=out_specs, check_vma=False)
```

time: 365 us -> 157 us (0.43); the launches traced: 359 us -> 154 us
  waiting for transfers between devices: 162 us -> 29.6 us
  matrix products: 37.9 us -> 0 us
  local copies, waits for them, and re-layouts: 38.1 us -> 10.1 us
  Pallas kernels: 0 us -> 27.1 us
  other arithmetic: 14.8 us -> 0 us
  between operations: 14.4 us -> 0.19 us
  starting transfers between devices: 23.7 us -> 18 us
    all_to_all x4 -> x1, waiting for transfers between devices: 89.5 us -> 17.8 us  [exchange(): lax.all_to_all(rows, 'expert', split_axis=0, concat_axis=0, tiled=True)]
    all_gather x3 -> x0, waiting for transfers between devices: 64.6 us -> none  [the longest x1 34.7 us: body(): lax.all_gather(local_blocks[0], 'shard', axis=1, tiled=True)]
    dot_general x9 -> x0, matrix products: 37.9 us -> none  [the longest x3 17.5 us: hidden_part(): jnp.einsum('rcf,cfo->rco', hidden, down_w[:, 0], preferred_element_type=j...]
    pallas_call x0 -> x12, Pallas kernels: none -> 27.1 us  [the longest x4 16.6 us: expert_on(): pl.pallas_call(functools.partial(expert_kernel, section, experts, capacit...]
    all_to_all x4 -> x1, starting transfers between devices: 21.1 us -> 4.75 us  [exchange(): lax.all_to_all(rows, 'expert', split_axis=0, concat_axis=0, tiled=True)]
    gather x12 -> x0, local copies, waits for them, and re-layouts: 14.6 us -> none  [the longest x6 6.19 us: body(): normed[source]]
    ppermute x2 -> x9, starting transfers between devices: 2.57 us -> 13.3 us  [the longest x7 8.51 us: other(): return lax.ppermute(array, 'section', pairs)]
    convert_element_type x6 -> x0, local copies, waits for them, and re-layouts: 9.36 us -> none  [the longest x3 4.96 us: body(): picked.astype(jnp.float32)]
  transfers between devices with their start and end apart: 9 -> 10, of which waited for: 8 -> 5; matrix products, arithmetic and copies ran while one was open for 4% -> 0% of each run, Pallas kernels for 0% -> 4%
where the time goes in v1:
time: 157 us; the launch traced here: 154 us
  blocking collectives  69.2 us (44%)
  waiting for transfers between devices  29.6 us (19%)
  Pallas kernels  27.1 us (17%)
  starting transfers between devices  18 us (11%)
  local copies, waits for them, and re-layouts  10.1 us (6%)
    all_to_all x3, blocking collectives, exchange(): lax.all_to_all(rows, 'expert', split_axis=0, concat_axis=0, tiled=True)  69.2 us
    all_to_all x1, waiting for transfers between devices, exchange(): lax.all_to_all(rows, 'expert', split_axis=0, concat_axis=0, tiled=True)  17.8 us
    pallas_call x4, Pallas kernels, expert_on(): pl.pallas_call(functools.partial(expert_kernel, section, experts, capacit...  16.6 us
    ppermute x7, waiting for transfers between devices, other(): return lax.ppermute(array, 'section', pairs)  11.8 us
    unnamed x29, local copies, waits for them, and re-layouts  10.1 us
    ppermute x7, starting transfers between devices, other(): return lax.ppermute(array, 'section', pairs)  8.51 us
    pallas_call x4, Pallas kernels, call(): pl.pallas_call(kernel, out_shape=out_shape, in_specs=specs, out_specs=jax...  7.57 us
    all_to_all x1, starting transfers between devices, exchange(): lax.all_to_all(rows, 'expert', split_axis=0, concat_axis=0, tiled=True)  4.75 us
  transfers between devices with their start and end apart: 10, of which 5 were waited for; matrix products, arithmetic and copies ran while one was open for 0% of the time, Pallas kernels for 4%

profile of v1, /device:TPU:9, one launch (start us, length us, event | category | flops | bytes accessed | tf_op | source)
XLA Modules:
  0.0 154.3 jit_solution(17018205677431881759)
XLA Ops:
  0.0 0.7 copy-done.10
  0.7 0.7 copy-done.11
  1.4 2.9 %pack.1.rest_0_.refs_0_ = bf16[97,128,128]{2,1,0:T(8,128)(2,1)} custom-call(s32[1]{0:T(128)} %bitcast.info, s32[1,32]{1,0:T(1,128)S(1)} %bitcast.31, s32[1,32]{1,0:T(1,128)S(1)} %bitcast.32, bf16[32,128,128]{2,1,0:T(8,128)(2,1)} %bitcast.33, bf16[32,128,128]{2,1,0:T(8,128)(2,1)} %bitcast.34, bf16[32,128,128]{2,1,0:T(8,128)(2,1)} %bitcast.35), custom_call_target="tpu_custom_call" | custom-call | bytes 14760000 | tf_op jit(solution)/shard_map/pack/pallas_call | solution.py:358
  4.3 2.4 %collective-permute-start.1 = (bf16[97,128,128]{2,1,0:T(8,128)(2,1)}, bf16[97,128,128]{2,1,0:T(8,128)(2,1)}, u32[]{:S(2)}, u32[]{:S(2)}) collective-permute-start(bf16[97,128,128]{2,1,0:T(8,128)(2,1)} %pack.1.rest_0_.refs_0_), channel_id=1, source_target_pairs={{0,8},{8,0},{2,10},{10,2},{4,12},{12,4},{6,14},{14,6},{16,24},{24,... | collective-permute-start | bytes 9535496 | tf_op jit(solution)/shard_map/ppermute | solution.py:406
  6.7 1.8 %collective-permute-start.3 = (f32[1,6144]{1,0:T(1,128)S(1)}, f32[1,6144]{1,0:T(1,128)S(1)}, u32[]{:S(2)}, u32[]{:S(2)}) collective-permute-start(f32[1,6144]{1,0:T(1,128)S(1)} %copy-done.7), channel_id=1, source_target_pairs={{0,1},{1,0},{2,3},{3,2},{4,5},{5,4},{6,7},{7,6},{8,9},{9,8},{10,11... | collective-permute-start | bytes 73736 | tf_op jit(solution)/shard_map/ppermute | solution.py:409
  9.0 0.6 collective-permute-done.2.other_ids
  9.8 1.9 %copy-done = bf16[97,128,128]{2,1,0:T(8,128)(2,1)S(1)} copy-done((bf16[97,128,128]{2,1,0:T(8,128)(2,1)S(1)}, bf16[97,128,128]{2,1,0:T(8,128)(2,1)}, u32[]{:S(2)}) %copy-start) | copy-done | bytes 3178520
  11.7 2.2 %first_send.1 = bf16[3456,128]{1,0:T(8,128)(2,1)S(1)} custom-call(s32[1]{0:T(128)} %bitcast.info, bf16[2,32,6144]{2,1,0:T(8,128)(2,1)} %tokens_ref.3, s32[1,2,2,32]{3,2,1,0:T(2,128)S(1)} %bitcast.25, f32[1,6144]{1,0:T(1,128)S(1)} %copy-done.7, s32[1,2,2,32]{3,2,1,0:T(2,128)S(1)} %collective-permute-done.2.other_ids, ...), custom_call_target="tpu_custom_call" | custom-call | bytes 11070000 | tf_op jit(solution)/shard_map/first_send/pallas_call | solution.py:425
  13.9 0.9 copy-done.6
  14.8 4.8 %all-to-all-start = ((bf16[4,864,128]{2,1,0:T(8,128)(2,1)}), bf16[4,864,128]{2,1,0:T(8,128)(2,1)}, u32[]{:S(2)}, u32[]{:S(2)}) async-start(bf16[4,864,128]{2,1,0:T(8,128)(2,1)} %bitcast.22), calls=%async_computation | async-start | bytes 1769472 | tf_op jit(solution)/shard_map/all_to_all | solution.py:438
  19.6 0.9 collective-permute-start
  20.5 17.8 %all-to-all-done = bf16[4,864,128]{2,1,0:T(8,128)(2,1)} async-done(((bf16[4,864,128]{2,1,0:T(8,128)(2,1)}), bf16[4,864,128]{2,1,0:T(8,128)(2,1)}, u32[]{:S(2)}, u32[]{:S(2)}) %all-to-all-start) | async-done | bytes 884768 | tf_op jit(solution)/shard_map/all_to_all | solution.py:438
  38.3 1.3 collective-permute-start.5
  39.6 1.3 expert.4.refs_1_
  41.0 0.8 copy-done.3
  41.8 9.7 %collective-permute-done.5.refs_1_ = bf16[97,128,128]{2,1,0:T(8,128)(2,1)S(1)} collective-permute-done((bf16[97,128,128]{2,1,0:T(8,128)(2,1)}, bf16[97,128,128]{2,1,0:T(8,128)(2,1)S(1)}, u32[]{:S(2)}, u32[]{:S(2)}) %collective-permute-start.5) | collective-permute-done | bytes 3178528 | tf_op jit(solution)/shard_map/ppermute | solution.py:409
  51.5 1.7 %copy-done.12 = bf16[97,128,128]{2,1,0:T(8,128)(2,1)} copy-done((bf16[97,128,128]{2,1,0:T(8,128)(2,1)}, bf16[97,128,128]{2,1,0:T(8,128)(2,1)S(1)}, u32[]{:S(2)}) %copy-start.12) | copy-done | bytes 3178520
  53.2 8.2 %expert.5 = bf16[3456,128]{1,0:T(8,128)(2,1)S(1)} custom-call(s32[1]{0:T(128)} %bitcast.info, bf16[97,128,128]{2,1,0:T(8,128)(2,1)} %collective-permute-done.refs_0_, bf16[97,128,128]{2,1,0:T(8,128)(2,1)} %copy-done.12, bf16[3456,128]{1,0:T(8,128)(2,1)} %bitcast.9.refs_1_.refs_2_, bf16[3456,128]{1,0:T(8,128)(2,1)S(1)} %copy.16.refs_3_), custom_call_target="tpu_custom_call", output_to_operand_aliasing={{}: (4, {})} | custom-call | bytes 25830000 | tf_op jit(solution)/shard_map/expert/pallas_call | solution.py:441
  61.4 0.9 copy-done.2
  62.3 2.4 %collective-permute-start.6 = (bf16[97,128,128]{2,1,0:T(8,128)(2,1)}, bf16[97,128,128]{2,1,0:T(8,128)(2,1)}, u32[]{:S(2)}, u32[]{:S(2)}) collective-permute-start(bf16[97,128,128]{2,1,0:T(8,128)(2,1)} %tie.4.refs_0_), channel_id=1, source_target_pairs={{0,8},{8,0},{2,10},{10,2},{4,12},{12,4},{6,14},{14,6},{16,24},{24,... | collective-permute-start | bytes 9535496 | tf_op jit(solution)/shard_map/ppermute | solution.py:406
  64.7 25.0 %all_to_all.20 = bf16[4,864,128]{2,1,0:T(8,128)(2,1)S(1)} all-to-all(bf16[4,864,128]{2,1,0:T(8,128)(2,1)} %bitcast.16), channel_id=1, replica_groups=mesh['groups'=2,'shard'=2,'expert'=4,'section'=2] {'expert'}, dimensions={0} | all-to-all | bytes 1769472 | tf_op jit(solution)/shard_map/all_to_all | solution.py:438
  89.7 3.0 %relay.1 = (bf16[32,6144]{1,0:T(8,128)(2,1)S(1)}, bf16[1536,128]{1,0:T(8,128)(2,1)S(1)}, bf16[3456,128]{1,0:T(8,128)(2,1)S(1)}) custom-call(s32[1]{0:T(128)} %bitcast.info, bf16[2,32,6144]{2,1,0:T(8,128)(2,1)} %tokens_ref.3, bf16[3456,128]{1,0:T(8,128)(2,1)S(1)} %bitcast.21, s32[1,2,2,32]{3,2,1,0:T(2,128)S(1)} %bitcast.26, f32[1,2,2,32]{3,2,1,0:T(2,128)S(1)} %bitcast.29, ...), custom_call_target="tpu_custom_call" | custom-call | bytes 11070000 | tf_op jit(solution)/shard_map/relay/pallas_call | solution.py:425
  92.7 0.7 copy-done.4
  93.4 1.3 collective-permute-start.7
  94.7 20.1 %all_to_all.21 = bf16[4,864,128]{2,1,0:T(8,128)(2,1)S(1)} all-to-all(bf16[4,864,128]{2,1,0:T(8,128)(2,1)S(1)} %bitcast.23), channel_id=1, replica_groups=mesh['groups'=2,'shard'=2,'expert'=4,'section'=2] {'expert'}, dimensions={0} | all-to-all | bytes 1769472 | tf_op jit(solution)/shard_map/all_to_all | solution.py:438
  115.0 1.7 %copy-done.13 = bf16[97,128,128]{2,1,0:T(8,128)(2,1)} copy-done((bf16[97,128,128]{2,1,0:T(8,128)(2,1)}, bf16[97,128,128]{2,1,0:T(8,128)(2,1)S(1)}, u32[]{:S(2)}) %copy-start.13) | copy-done | bytes 3178520
  116.7 7.0 %expert.7 = bf16[3456,128]{1,0:T(8,128)(2,1)S(1)} custom-call(s32[1]{0:T(128)} %bitcast.info, bf16[97,128,128]{2,1,0:T(8,128)(2,1)} %pack.1.rest_0_.refs_0_, bf16[97,128,128]{2,1,0:T(8,128)(2,1)} %copy-done.13, bf16[3456,128]{1,0:T(8,128)(2,1)S(1)} %bitcast.18, bf16[3456,128]{1,0:T(8,128)(2,1)S(1)} %expert.6.refs_3_), custom_call_target="tpu_custom_call", output_to_operand_aliasing={{}: (4, {})} | custom-call | bytes 25830000 | tf_op jit(solution)/shard_map/expert/pallas_call | solution.py:441
  123.7 24.1 %all_to_all.22 = bf16[4,864,128]{2,1,0:T(8,128)(2,1)S(1)} all-to-all(bf16[4,864,128]{2,1,0:T(8,128)(2,1)S(1)} %bitcast.19), channel_id=1, replica_groups=mesh['groups'=2,'shard'=2,'expert'=4,'section'=2] {'expert'}, dimensions={0} | all-to-all | bytes 1769472 | tf_op jit(solution)/shard_map/all_to_all | solution.py:438
  147.8 1.4 last.1
  149.2 2.8 %collective-permute-start.8 = (bf16[32,6144]{1,0:T(8,128)(2,1)S(1)}, bf16[32,6144]{1,0:T(8,128)(2,1)S(1)}, u32[]{:S(2)}, u32[]{:S(2)}) collective-permute-start(bf16[32,6144]{1,0:T(8,128)(2,1)S(1)} %get-tuple-element.14), channel_id=1, source_target_pairs={{0,1},{1,0},{2,3},{3,2},{4,5},{5,4},{6,7},{7,6},{8,9},{9,8},{10,11... | collective-permute-start | bytes 1179656 | tf_op jit(solution)/shard_map/ppermute | solution.py:409
  152.0 1.3 collective-permute-done.8.came
  153.3 0.9 join.1
  (32 shorter events, 0.9 us)
Async XLA Ops:
  0.0 6.7 %copy-start.7 = (f32[1,6144]{1,0:T(1,128)S(1)}, f32[1,6144]{1,0:T(1,128)}, u32[]{:S(2)}) copy-start(f32[1,6144]{1,0:T(1,128)} %gain.3) | copy-start | bytes 73732
  0.0 8.4 %copy-start.8 = (s32[1,2,32,2]{2,3,1,0:T(2,128)S(1)}, s32[1,2,32,2]{2,3,1,0:T(2,128)}, u32[]{:S(2)}) copy-start(s32[1,2,32,2]{2,3,1,0:T(2,128)} %param.11) | copy-start | bytes 1540
  0.0 8.5 %copy-start.9 = (f32[1,2,32,2]{2,3,1,0:T(2,128)S(1)}, f32[1,2,32,2]{2,3,1,0:T(2,128)}, u32[]{:S(2)}) copy-start(f32[1,2,32,2]{2,3,1,0:T(2,128)} %param.12) | copy-start | bytes 1540
  0.0 0.7 copy-start.10
  0.7 0.7 copy-start.11
  4.3 34.0 %collective-permute-start.1 = (bf16[97,128,128]{2,1,0:T(8,128)(2,1)}, bf16[97,128,128]{2,1,0:T(8,128)(2,1)}, u32[]{:S(2)}, u32[]{:S(2)}) collective-permute-start(bf16[97,128,128]{2,1,0:T(8,128)(2,1)} %pack.1.rest_0_.refs_0_), channel_id=1, source_target_pairs={{0,8},{8,0},{2,10},{10,2},{4,12},{12,4},{6,14},{14,6},{16,24},{24,... | collective-permute-start | bytes 9535496 | tf_op jit(solution)/shard_map/ppermute | solution.py:406
  6.7 3.1 %collective-permute-start.3 = (f32[1,6144]{1,0:T(1,128)S(1)}, f32[1,6144]{1,0:T(1,128)S(1)}, u32[]{:S(2)}, u32[]{:S(2)}) collective-permute-start(f32[1,6144]{1,0:T(1,128)S(1)} %copy-done.7), channel_id=1, source_target_pairs={{0,1},{1,0},{2,3},{3,2},{4,5},{5,4},{6,7},{7,6},{8,9},{9,8},{10,11... | collective-permute-start | bytes 73736 | tf_op jit(solution)/shard_map/ppermute | solution.py:409
  8.5 1.2 collective-permute-start.2
  8.5 1.2 collective-permute-start.4
  9.8 1.9 %copy-start = (bf16[97,128,128]{2,1,0:T(8,128)(2,1)S(1)}, bf16[97,128,128]{2,1,0:T(8,128)(2,1)}, u32[]{:S(2)}) copy-start(bf16[97,128,128]{2,1,0:T(8,128)(2,1)} %pack.1.rest_0_.refs_0_) | copy-start | bytes 9535492
  11.7 7.9 %copy-start.1 = (bf16[97,128,128]{2,1,0:T(8,128)(2,1)S(1)}, bf16[97,128,128]{2,1,0:T(8,128)(2,1)}, u32[]{:S(2)}) copy-start(bf16[97,128,128]{2,1,0:T(8,128)(2,1)} %pack.1.rest_0_.refs_0_) | copy-start | bytes 9535492
  13.9 0.9 copy-start.6
  14.8 23.4 %all-to-all-start = ((bf16[4,864,128]{2,1,0:T(8,128)(2,1)}), bf16[4,864,128]{2,1,0:T(8,128)(2,1)}, u32[]{:S(2)}, u32[]{:S(2)}) async-start(bf16[4,864,128]{2,1,0:T(8,128)(2,1)} %bitcast.22), calls=%async_computation | async-start | bytes 1769472 | tf_op jit(solution)/shard_map/all_to_all | solution.py:438
  19.6 21.4 %collective-permute-start = (bf16[97,128,128]{2,1,0:T(8,128)(2,1)S(1)}, bf16[97,128,128]{2,1,0:T(8,128)(2,1)}, u32[]{:S(2)}, u32[]{:S(2)}) collective-permute-start(bf16[97,128,128]{2,1,0:T(8,128)(2,1)S(1)} %copy-done.1), channel_id=1, source_target_pairs={{0,1},{1,0},{2,3},{3,2},{4,5},{5,4},{6,7},{7,6},{8,9},{9,8},{10,11... | collective-permute-start | bytes 9535496 | tf_op jit(solution)/shard_map/ppermute | solution.py:409
  38.3 13.2 %collective-permute-start.5 = (bf16[97,128,128]{2,1,0:T(8,128)(2,1)}, bf16[97,128,128]{2,1,0:T(8,128)(2,1)S(1)}, u32[]{:S(2)}, u32[]{:S(2)}) collective-permute-start(bf16[97,128,128]{2,1,0:T(8,128)(2,1)} %tie.3.refs_1_), channel_id=1, source_target_pairs={{0,1},{2,3},{4,5},{6,7},{8,9},{10,11},{12,13},{14,15},{16,17},{18,... | collective-permute-start | bytes 9535496 | tf_op jit(solution)/shard_map/ppermute | solution.py:409
  40.9 0.9 copy-start.3
  51.5 1.7 %copy-start.12 = (bf16[97,128,128]{2,1,0:T(8,128)(2,1)}, bf16[97,128,128]{2,1,0:T(8,128)(2,1)S(1)}, u32[]{:S(2)}) copy-start(bf16[97,128,128]{2,1,0:T(8,128)(2,1)S(1)} %collective-permute-done.5.refs_1_) | copy-start | bytes 9535492
  61.3 0.9 copy-start.2
  62.3 31.1 %collective-permute-start.6 = (bf16[97,128,128]{2,1,0:T(8,128)(2,1)}, bf16[97,128,128]{2,1,0:T(8,128)(2,1)}, u32[]{:S(2)}, u32[]{:S(2)}) collective-permute-start(bf16[97,128,128]{2,1,0:T(8,128)(2,1)} %tie.4.refs_0_), channel_id=1, source_target_pairs={{0,8},{8,0},{2,10},{10,2},{4,12},{12,4},{6,14},{14,6},{16,24},{24,... | collective-permute-start | bytes 9535496 | tf_op jit(solution)/shard_map/ppermute | solution.py:406
  92.7 0.7 copy-start.4
  93.4 21.6 %collective-permute-start.7 = (bf16[97,128,128]{2,1,0:T(8,128)(2,1)}, bf16[97,128,128]{2,1,0:T(8,128)(2,1)S(1)}, u32[]{:S(2)}, u32[]{:S(2)}) collective-permute-start(bf16[97,128,128]{2,1,0:T(8,128)(2,1)} %tie.5.refs_1_), channel_id=1, source_target_pairs={{0,1},{2,3},{4,5},{6,7},{8,9},{10,11},{12,13},{14,15},{16,17},{18,... | collective-permute-start | bytes 9535496 | tf_op jit(solution)/shard_map/ppermute | solution.py:409
  115.0 32.8 %copy-start.5 = (bf16[32,6144]{1,0:T(8,128)(2,1)S(1)}, bf16[32,6144]{1,0:T(8,128)(2,1)}, u32[]{:S(2)}) copy-start(bf16[32,6144]{1,0:T(8,128)(2,1)} %copy-done.4) | copy-start | bytes 1179652
  115.0 1.7 %copy-start.13 = (bf16[97,128,128]{2,1,0:T(8,128)(2,1)}, bf16[97,128,128]{2,1,0:T(8,128)(2,1)S(1)}, u32[]{:S(2)}) copy-start(bf16[97,128,128]{2,1,0:T(8,128)(2,1)S(1)} %collective-permute-done.7.refs_1_) | copy-start | bytes 9535492
  149.2 4.1 %collective-permute-start.8 = (bf16[32,6144]{1,0:T(8,128)(2,1)S(1)}, bf16[32,6144]{1,0:T(8,128)(2,1)S(1)}, u32[]{:S(2)}, u32[]{:S(2)}) collective-permute-start(bf16[32,6144]{1,0:T(8,128)(2,1)S(1)} %get-tuple-element.14), channel_id=1, source_target_pairs={{0,1},{1,0},{2,3},{3,2},{4,5},{5,4},{6,7},{7,6},{8,9},{9,8},{10,11... | collective-permute-start | bytes 1179656 | tf_op jit(solution)/shard_map/ppermute | solution.py:409

commit v2 on v1

v2 whole, which is shorter than its diff:
```python
import functools
import itertools
import math

import jax
import jax.numpy as jnp
from jax import lax
from jax.experimental import pallas as pl
from jax.experimental.pallas import tpu as pltpu
from jax.sharding import PartitionSpec as P

TOP = 2
LANES = 128
EPS = 1e-05
MIB = 1 << 20


def up_to(value, unit):
    return -(-value // unit) * unit


def group_of(capacity):
    return 16 // math.gcd(capacity, 16)


def iota(shape, axis):
    return lax.broadcasted_iota(jnp.int32, shape, axis)


def split_by(values, unit):
    quotient = jnp.floor((values.astype(jnp.float32) + 0.5) * (1.0 / unit)).astype(jnp.int32)
    return quotient, values - quotient * unit


def dot(left, right, contract=((1,), (0,))):
    return lax.dot_general(left, right, (contract, ((), ())), preferred_element_type=jnp.float32)


def spread_columns(values, rows):
    tokens = values.shape[1]
    token = split_by(iota((rows, tokens), 0), tokens)[1]
    same = iota((rows, tokens), 1) == token
    return [
        jnp.sum(jnp.where(same, values[choice : choice + 1, :], 0.0), axis=1, keepdims=True) for choice in range(TOP)
    ]


def picks_to_send(ids, experts, capacity, group):
    tokens = ids.shape[1]
    expert = iota((up_to(experts, 16), tokens), 0)
    hit = (ids[0:1, :] == expert) | (ids[1:2, :] == expert)
    hit = jnp.where(hit, 1.0, 0.0).astype(jnp.bfloat16)
    shape = (tokens, group * tokens)
    block, token = split_by(iota(shape, 1), tokens)
    earlier = jnp.where(iota(shape, 0) < token, 1.0, 0.0).astype(jnp.bfloat16)
    same = jnp.where(iota(shape, 0) == token, 1.0, 0.0).astype(jnp.bfloat16)
    slot = dot(hit, earlier)
    here = dot(hit, same)
    first = (block[0:1, :] * capacity).astype(jnp.float32)
    key = jnp.where(here > 0.5, slot + first, -1.0)
    row = iota((group * capacity, group * tokens), 0).astype(jnp.float32)
    return jnp.concatenate(
        [jnp.where(row == key[k : k + 1, :], 1.0, 0.0) for k in range(experts)], axis=0
    ).astype(jnp.bfloat16)


def picks_to_mix(ids, experts, capacity, group):
    tokens = ids.shape[1]
    rows = group * tokens
    token = split_by(iota((rows, tokens), 0), tokens)[1]
    first = (split_by(iota((rows, 1), 0), tokens)[0] * capacity).astype(jnp.float32)
    columns = iota((rows, experts * group * capacity), 1).astype(jnp.float32)
    earlier = iota((rows, tokens), 1) < token
    chosen = spread_columns(ids.astype(jnp.float32), rows)
    parts = []
    for choice in range(TOP):
        expert = chosen[choice]
        named = (ids[0:1, :].astype(jnp.float32) == expert) | (ids[1:2, :].astype(jnp.float32) == expert)
        slot = jnp.sum(jnp.where(named & earlier, 1.0, 0.0), axis=1, keepdims=True)
        key = expert * (group * capacity) + first + slot
        parts.append(jnp.where(columns == key, 1.0, 0.0))
    return jnp.concatenate(parts, axis=0).astype(jnp.bfloat16)


class Layer:
    def __init__(self, info, layer, own, other):
        self.held = info[0] == layer
        self.section, self.me, self.own, self.other = info[0], info[1], own, other

    def rows(self, at):
        return jnp.where(self.held, self.own[at][0, self.section], self.other[at][0, self.section])

    def partners(self, at):
        return self.rows(at) ^ self.me

    def gain(self, at, block):
        lanes = slice(block * LANES, (block + 1) * LANES)
        return jnp.where(self.held, self.own[at][0:1, lanes], self.other[at][0:1, lanes])


def send_rows(partners, state, scale, gain_of, outs, group, capacity, tokens):
    count = group * capacity
    blocks = state.shape[0] // tokens
    picks = picks_to_send(partners, len(outs), capacity, group)
    scale = jnp.concatenate([scale] * group, axis=0)
    for number in range(blocks // group):
        rows = state[number * group * tokens : (number + 1) * group * tokens, :]
        gain = jnp.concatenate(
            [jnp.broadcast_to(gain_of(number * group + j), (tokens, LANES)) for j in range(group)], axis=0
        )
        normed = (rows.astype(jnp.float32) * scale * gain).astype(jnp.bfloat16)
        picked = dot(picks, normed).astype(jnp.bfloat16)
        for k, out in enumerate(outs):
            out[number * count : (number + 1) * count, :] = picked[k * count : (k + 1) * count, :]


def first_send_kernel(partners, capacity, group, info, tokens_ref, ids, gain, other_ids, other_gain, *rest):
    outs, (given, state, arrived) = rest[-partners - 3 : -3], rest[-3:]
    section = info[0]
    copy = pltpu.make_async_copy(tokens_ref.at[section], given, arrived.at[0])
    copy.start()
    copy.wait()
    layer = Layer(info, 0, (ids, gain), (other_ids, other_gain))
    tokens, width = given.shape
    blocks = width // LANES
    total = jnp.zeros((tokens, 1), jnp.float32)
    for b in range(blocks):
        part = given[:, b * LANES : (b + 1) * LANES]
        state[b * tokens : (b + 1) * tokens, :] = part
        wide = part.astype(jnp.float32)
        total += jnp.sum(wide * wide, axis=1, keepdims=True)
    scale = lax.rsqrt(total * (1.0 / width) + EPS)
    send_rows(layer.partners(0), state, scale, lambda b: layer.gain(1, b), outs, group, capacity, tokens)


def mix_rows(picks, base, weights, returned, number, group, capacity, tokens):
    count = group * capacity
    given = jnp.concatenate([part[number * count : (number + 1) * count, :] for part in returned], axis=0)
    picked = dot(picks, given)
    rows = group * tokens
    total = base.astype(jnp.float32)
    for choice in range(TOP):
        total += weights[choice] * picked[choice * rows : (choice + 1) * rows, :]
    return total.astype(jnp.bfloat16)


def relay_kernel(partners, capacity, group, info, tokens_ref, ids, weights, gain, other_ids, other_weights, other_gain, *rest):
    returned, (state_out, state), outs = rest[:partners], rest[-partners - 4 : -partners - 2], rest[-partners - 2 : -2]
    given, arrived = rest[-2:]
    section = info[0]
    copy = pltpu.make_async_copy(tokens_ref.at[section], given, arrived.at[0])
    copy.start()
    first = Layer(info, 0, (ids, weights), (other_ids, other_weights))
    second = Layer(info, 1, (ids, gain), (other_ids, other_gain))
    tokens, width = given.shape
    blocks = width // LANES
    picks = picks_to_mix(first.partners(0), partners, capacity, group)
    shares = spread_columns(first.rows(1), group * tokens)
    total = jnp.zeros((tokens, 1), jnp.float32)
    copy.wait()
    for number in range(blocks // group):
        base = jnp.concatenate(
            [given[:, b * LANES : (b + 1) * LANES] for b in range(number * group, (number + 1) * group)], axis=0
        )
        mixed = mix_rows(picks, base, shares, returned, number, group, capacity, tokens)
        state[number * group * tokens : (number + 1) * group * tokens, :] = mixed
        wide = mixed.astype(jnp.float32)
        square = jnp.sum(wide * wide, axis=1, keepdims=True)
        for j in range(group):
            b = number * group + j
            state_out[:, b * LANES : (b + 1) * LANES] = mixed[j * tokens : (j + 1) * tokens, :]
            total += square[j * tokens : (j + 1) * tokens, :]
    scale = lax.rsqrt(total * (1.0 / width) + EPS)
    send_rows(second.partners(0), state, scale, lambda b: second.gain(1, b), outs, group, capacity, tokens)


def last_kernel(partners, capacity, group, info, first, state, ids, weights, other_ids, other_weights, *rest):
    returned, (out, leaving) = rest[:partners], rest[partners:]
    layer = Layer(info, 1, (ids, weights), (other_ids, other_weights))
    tokens, width = out.shape
    blocks = width // LANES
    picks = picks_to_mix(layer.partners(0), partners, capacity, group)
    shares = spread_columns(layer.rows(1), group * tokens)
    for number in range(blocks // group):
        base = state[number * group * tokens : (number + 1) * group * tokens, :]
        mixed = mix_rows(picks, base, shares, returned, number, group, capacity, tokens)
        for j in range(group):
            b = number * group + j
            out[:, b * LANES : (b + 1) * LANES] = mixed[j * tokens : (j + 1) * tokens, :]

    @pl.when(info[0] == 0)
    def _():
        leaving[...] = out[...]

    @pl.when(info[0] != 0)
    def _():
        leaving[...] = first[...]


def join_kernel(info, first, second, came, out):
    @pl.when(info[0] == 0)
    def _():
        out[0, 0] = first[...]
        out[0, 1] = came[...]

    @pl.when(info[0] != 0)
    def _():
        out[0, 0] = came[...]
        out[0, 1] = second[...]


def expert_kernel(section, partners, capacity, group, split, unroll, info, *refs):
    @pl.when(info[0] == section)
    def _():
        expert_rows(partners, capacity, group, split, unroll, *refs)


def expert_rows(partners, capacity, group, split, unroll, *refs):
    halves, first = [], 0
    for pieces in split:
        halves.append(refs[first : first + pieces])
        first += pieces
    sent, outs = refs[first : -10 - partners][:partners], refs[-10 - partners : -10]
    numbers, places, placed, weights, arrived, state, hidden, total, made, left = refs[-10:]
    blocks = state.shape[0]
    padded = state.shape[1] // partners
    columns = (weights.shape[1] - 1) // 3
    count = group * capacity
    sizes = [columns] * 3 + [1]

    def part_of(k, number):
        return sent[k][number * count : (number + 1) * count, :]

    def load(half, which):
        source, start = halves[half][0], which * columns
        if len(halves[half]) > 1:
            source, start = halves[half][min(which, 2)], columns if which == 3 else 0
        return pltpu.make_async_copy(
            source.at[pl.ds(start, sizes[which])],
            weights.at[half, pl.ds(which * columns, sizes[which])],
            arrived.at[half, which],
        )

    for which in (3, 0, 1, 2):
        for half in range(len(halves)):
            load(half, which).start()

    shape = (group * padded, count)
    block, slot = split_by(iota((group * padded, 1), 0), padded)
    key = jnp.where(slot < capacity, block * capacity + slot, -1)
    spread = jnp.where(iota(shape, 1) == key, 1.0, 0.0).astype(jnp.bfloat16)
    for number in range(blocks // group):
        spaced = [dot(spread, part_of(k, number)) for k in range(partners)]
        for j in range(group):
            rows = jnp.concatenate([s[j * padded : (j + 1) * padded, :] for s in spaced], axis=0)
            state[number * group + j] = rows.astype(jnp.bfloat16)
            total[number * group + j] = jnp.zeros(rows.shape, jnp.float32)

    for half in range(len(halves)):
        load(half, 3).wait()
        numbers[half] = weights[half, 3 * columns, :16, :].astype(jnp.float32)[:8, :].astype(jnp.int32)
    moves = [pltpu.make_async_copy(numbers.at[half], places.at[half], placed.at[half]) for half in range(len(halves))]
    for move in moves:
        move.start()
    for move in moves:
        move.wait()

    for half in range(len(halves)):
        load(half, 0).wait()
        load(half, 1).wait()

        def up_step(at, carry, half=half):
            for i in range(unroll):
                c = at * unroll + i
                rows = state[places[half, 0, c]]
                both = dot(rows, jnp.concatenate([weights[half, c], weights[half, columns + c]], axis=1))
                gate, up = both[:, :LANES], both[:, LANES:]
                hidden[half * columns + c] = (gate / (1.0 + jnp.exp(-gate)) * up).astype(jnp.bfloat16)
            return carry

        lax.fori_loop(0, columns // unroll, up_step, 0)

    for half in range(len(halves)):
        load(half, 2).wait()

        def down_step(at, carry, half=half):
            produced = []
            for i in range(unroll):
                c = at * unroll + i
                produced.append(dot(hidden[half * columns + c], weights[half, 2 * columns + c]))
            for i in range(unroll):
                to = places[half, 1, at * unroll + i]
                total[to] = total[to] + produced[i]
            return carry

        lax.fori_loop(0, columns // unroll, down_step, 0)

    block, slot = split_by(iota((count, 1), 0), capacity)
    packing = jnp.where(iota((count, group * padded), 1) == block * padded + slot, 1.0, 0.0).astype(jnp.bfloat16)
    copies = [pltpu.make_async_copy(made.at[k], outs[k], left.at[k]) for k in range(partners)]
    for k in range(partners - 1, -1, -1):
        for number in range(blocks // group):
            spaced = jnp.concatenate(
                [total[number * group + j, k * padded : (k + 1) * padded, :] for j in range(group)], axis=0
            ).astype(jnp.bfloat16)
            made[k, number * count : (number + 1) * count, :] = dot(packing, spaced).astype(jnp.bfloat16)
        copies[k].start()
    for copy in copies:
        copy.wait()


def pack_kernel(info, in_rows, out_cols, *refs):
    stored, (out, kept, numbers, named, arrived, left) = refs[:3], refs[-6:]
    columns = stored[0].shape[0]
    names = [
        pltpu.make_async_copy(source, numbers.at[at], named.at[at]) for at, source in enumerate((in_rows, out_cols))
    ]

    def take(at):
        return pltpu.make_async_copy(stored[at], kept.at[pl.ds(at * columns, columns)], arrived.at[at])

    def give(at):
        span = pl.ds(at * columns, columns + at // 2)
        return pltpu.make_async_copy(kept.at[span], out.at[span], left.at[at])

    for name in names:
        name.start()
    for at in range(3):
        take(at).start()
    spread = jnp.where(iota((columns, LANES), 0) == iota((columns, LANES), 1), 1.0, 0.0).astype(jnp.bfloat16)
    row = iota((LANES, LANES), 0)
    for name in names:
        name.wait()
    rows, cols = (
        dot(jnp.broadcast_to(numbers[at].astype(jnp.float32), (LANES, columns)).astype(jnp.bfloat16), spread)
        for at in range(2)
    )
    kept[3 * columns] = jnp.where(row == 0, rows, jnp.where(row == 1, cols, 0.0)).astype(jnp.bfloat16)
    for at in range(3):
        take(at).wait()
        give(at).start()
    for at in range(3):
        give(at).wait()


def tie_kernel(*refs):
    pass


SMEM = pl.BlockSpec(memory_space=pltpu.SMEM)
VMEM = pl.BlockSpec(memory_space=pltpu.VMEM)
ANY = pl.BlockSpec(memory_space=pl.ANY)


def held(*arrays):
    return [pltpu.with_memory_space_constraint(a, pltpu.HBM) for a in arrays]


def pack(info, places, weights, after):
    columns, *block = weights[0].shape
    shape = (3 * columns + 1, *block)
    return pl.pallas_call(
        pack_kernel,
        out_shape=pltpu.HBM(shape, jnp.bfloat16),
        in_specs=[SMEM] + [ANY] * (5 + len(after)),
        out_specs=ANY,
        scratch_shapes=[
            pltpu.VMEM(shape, jnp.bfloat16),
            pltpu.VMEM((2, 1, columns), jnp.int32),
            pltpu.SemaphoreType.DMA((2,)),
            pltpu.SemaphoreType.DMA((3,)),
            pltpu.SemaphoreType.DMA((3,)),
        ],
        compiler_params=pltpu.CompilerParams(vmem_limit_bytes=8 * MIB),
        name="pack",
    )(info, *held(*places, *weights), *after)


def tie(array, *others):
    return pl.pallas_call(
        tie_kernel,
        out_shape=pltpu.HBM(array.shape, array.dtype),
        in_specs=[ANY] * (1 + len(others)),
        out_specs=ANY,
        input_output_aliases={0: 0},
        name="tie",
    )(*held(array), *others)


def body(tokens, norm_gain, route_ids, route_weights, gate_blocks, up_blocks, down_blocks, gate_rows, down_cols):
    partners = lax.axis_size("expert")
    sections = lax.axis_size("section")
    shards = lax.axis_size("shard")
    micro_count, row_count, width = tokens.shape
    assert sections == micro_count == 2 and gate_blocks.shape[1] == 1 and partners & (partners - 1) == 0
    blocks = width // LANES
    capacity = min(row_count, max(row_count * 9 // 16, row_count * TOP // partners + 2))
    group = group_of(capacity)
    rows_shape = jax.ShapeDtypeStruct((blocks * capacity, LANES), jnp.bfloat16)
    padded = up_to(capacity, 8)
    bf16, f32 = jnp.bfloat16, jnp.float32
    info = jnp.stack([lax.axis_index(a) for a in ("section", "expert", "groups")]).astype(jnp.int32)
    weights = [a.reshape(a.shape[2:3] + a.shape[4:]) for a in (gate_blocks, up_blocks, down_blocks)]
    places = [a.reshape(1, -1) for a in (gate_rows, down_cols)]
    ids, shares = jnp.swapaxes(route_ids, 2, 3), jnp.swapaxes(route_weights, 2, 3)
    swap = [(0, 1), (1, 0)]

    def across(array):
        axes = ("groups", "shard", "expert", "section")
        sizes = [lax.axis_size(a) for a in axes]
        pairs = []
        for place in itertools.product(*(range(n) for n in sizes)):
            target = list(place)
            turned = 0 if place[3] else 1
            target[turned] = 1 - place[turned]
            pairs.append(tuple(sum(p * math.prod(sizes[i + 1 :]) for i, p in enumerate(q)) for q in (place, target)))
        return lax.ppermute(array, axes, pairs)

    def other(array, pairs=swap):
        return lax.ppermute(array, "section", pairs)

    paired = shards == 2 and lax.axis_size("groups") == 2
    if not paired:
        weights = [lax.all_gather(a, "shard", axis=0, tiled=True) for a in weights]
        places = [lax.all_gather(a, "shard", axis=1, tiled=True) for a in places]
    columns = weights[0].shape[0]
    assert columns <= LANES

    other_ids, other_shares, other_gain = other(ids), other(shares), other(norm_gain)
    state_shape = jax.ShapeDtypeStruct((row_count, width), bf16)
    blocks_shape = jax.ShapeDtypeStruct((blocks * row_count, LANES), bf16)
    tokens_scratch = [pltpu.VMEM((row_count, width), bf16)]

    def call(kernel, name, out_shape, args, specs, scratch, limit):
        return pl.pallas_call(
            kernel,
            out_shape=out_shape,
            in_specs=specs,
            out_specs=jax.tree.map(lambda _: VMEM, out_shape),
            scratch_shapes=scratch,
            compiler_params=pltpu.CompilerParams(vmem_limit_bytes=limit * MIB),
            name=name,
        )(*args)

    def exchange(parts):
        moved = list(parts)
        for k in range(partners - 1, 0, -1):
            moved[k] = lax.ppermute(parts[k], "expert", [(i, i ^ k) for i in range(partners)])
        return moved

    def expert_on(section, sources, rows, earlier):
        inputs = sum(len(s) for s in sources)
        return pl.pallas_call(
            functools.partial(
                expert_kernel,
                section,
                partners,
                capacity,
                group,
                [len(s) for s in sources],
                math.gcd(columns, 16),
            ),
            out_shape=[pltpu.HBM(rows_shape.shape, bf16)] * partners,
            in_specs=[SMEM] + [ANY] * inputs + [VMEM] * len(rows) + [ANY] * len(earlier),
            out_specs=[ANY] * partners,
            scratch_shapes=[
                pltpu.VMEM((len(sources), 8, LANES), jnp.int32),
                pltpu.SMEM((len(sources), 8, LANES), jnp.int32),
                pltpu.SemaphoreType.DMA((len(sources),)),
                pltpu.VMEM((len(sources), 3 * columns + 1) + weights[0].shape[1:], bf16),
                pltpu.SemaphoreType.DMA((len(sources), 4)),
                pltpu.VMEM((blocks, partners * padded, LANES), bf16),
                pltpu.VMEM((len(sources) * columns, partners * padded, LANES), bf16),
                pltpu.VMEM((blocks, partners * padded, LANES), f32),
                pltpu.VMEM((partners,) + rows_shape.shape, bf16),
                pltpu.SemaphoreType.DMA((partners,)),
            ],
            input_output_aliases={1 + inputs + len(rows) + k: k for k in range(len(earlier))},
            compiler_params=pltpu.CompilerParams(vmem_limit_bytes=20 * MIB),
            name="expert",
        )(info, *(a for s in sources for a in s), *rows, *held(*earlier))

    packed = pack(info, places, weights, [])
    sent = call(
        functools.partial(first_send_kernel, partners, capacity, group),
        "first_send",
        [rows_shape] * partners,
        (info, *held(tokens), ids, norm_gain, other_ids, other_gain, other_shares),
        [SMEM, ANY, VMEM, VMEM, VMEM, VMEM, ANY],
        tokens_scratch + [pltpu.VMEM((blocks * row_count, LANES), bf16), pltpu.SemaphoreType.DMA((1,))],
        12,
    )
    rows = exchange(sent)
    swapped = other(pack(info, places, weights, rows[1:]))
    if paired:
        moved = tie(across(packed), *rows[1:])
        passed = other(moved, [(0, 1)])
        whole = across(swapped)
        sources = [[held(packed), held(moved)], [held(swapped), [passed]]]
    else:
        sources = [[held(packed)], [held(swapped)]]
    done = expert_on(0, sources[0], rows, [])
    returned = exchange(expert_on(1, sources[1], rows, done))
    first, state, *sent = call(
        functools.partial(relay_kernel, partners, capacity, group),
        "relay",
        [state_shape, blocks_shape] + [rows_shape] * partners,
        (info, *held(tokens), ids, shares, norm_gain, other_ids, other_shares, other_gain, *held(returned[0]), *returned[1:]),
        [SMEM, ANY] + [VMEM] * (6 + partners),
        tokens_scratch + [pltpu.SemaphoreType.DMA((1,))],
        12,
    )
    given_rows = exchange(sent)
    if paired:
        whole = tie(whole, first)
        passed = other(whole, [(0, 1)])
        sources = [[held(swapped), held(whole)], [held(packed), [passed]]]
    else:
        sources = [[held(swapped)], [held(packed)]]
    done = expert_on(0, sources[0], given_rows, [])
    returned = exchange(expert_on(1, sources[1], given_rows, done))
    second, leaving = call(
        functools.partial(last_kernel, partners, capacity, group),
        "last",
        [state_shape] * 2,
        (info, first, state, ids, shares, other_ids, other_shares, *held(returned[0]), *returned[1:]),
        [SMEM] + [VMEM] * (6 + partners),
        [],
        12,
    )
    return call(
        join_kernel,
        "join",
        jax.ShapeDtypeStruct((1, micro_count, row_count, width), bf16),
        (info, first, second, other(leaving)),
        [SMEM] + [VMEM] * 3,
        [],
        12,
    )


def solution(mesh):
    in_specs = (
        P(None, ("groups", "shard", "expert"), None),
        P("section", None),
        P("section", None, ("groups", "shard", "expert"), None),
        P("section", None, ("groups", "shard", "expert"), None),
        P("section", "expert", "shard", None, None, None),
        P("section", "expert", "shard", None, None, None),
        P("section", "expert", "shard", None, None, None),
        P("section", "expert", "shard", None),
        P("section", "expert", "shard", None),
    )
    out_specs = P("section", None, ("groups", "shard", "expert"), None)
    return jax.shard_map(body, mesh=mesh, in_specs=in_specs, out_specs=out_specs, check_vma=False)
```

time: 157 us -> 142 us (0.904)
  blocking collectives: 69.2 us -> 0 us
  waiting for transfers between devices: 29.6 us -> 84 us
  local copies, waits for them, and re-layouts: 10.1 us -> 0.78 us
  Pallas kernels: 27.1 us -> 32.5 us
  starting transfers between devices: 18 us -> 22.8 us
    ppermute x2 -> x14, waiting for transfers between devices: 0.01 us -> 78.1 us  [the longest x12 72.1 us: exchange(): lax.ppermute(parts[k], 'expert', [(i, i ^ k) for i in range(partners)])]
    all_to_all x3 -> x0, blocking collectives: 69.2 us -> none  [exchange(): lax.all_to_all(rows, 'expert', split_axis=0, concat_axis=0, tiled=True)]
    all_to_all x1 -> x0, waiting for transfers between devices: 17.8 us -> none  [exchange(): lax.all_to_all(rows, 'expert', split_axis=0, concat_axis=0, tiled=True)]
    ppermute x2 -> x14, starting transfers between devices: 4.75 us -> 15.8 us  [the longest x12 13.2 us: exchange(): lax.ppermute(parts[k], 'expert', [(i, i ^ k) for i in range(partners)])]
    unnamed x29 -> x22, local copies, waits for them, and re-layouts: 10.1 us -> 0.78 us
    ppermute x7, waiting for transfers between devices: 11.8 us -> 5.87 us  [other(): return lax.ppermute(array, 'section', pairs)]
    all_to_all x1 -> x0, starting transfers between devices: 4.75 us -> none  [exchange(): lax.all_to_all(rows, 'expert', split_axis=0, concat_axis=0, tiled=True)]
    pallas_call x1 -> x2, Pallas kernels: 2.92 us -> 7.42 us  [pack(): pl.pallas_call(pack_kernel, out_shape=pltpu.HBM(shape, jnp.bfloat16), in_...]
  transfers between devices with their start and end apart: 10 -> 21, of which waited for: 5 -> 14; matrix products, arithmetic and copies ran while one was open for 0% -> 0% of each run, Pallas kernels for 4% -> 16%
where the time goes in v2:
time: 142 us; the launch traced here: 140 us
  waiting for transfers between devices  84 us (59%)
  Pallas kernels  32.5 us (23%)
  starting transfers between devices  22.8 us (16%)
    ppermute x12, waiting for transfers between devices, exchange(): lax.ppermute(parts[k], 'expert', [(i, i ^ k) for i in range(partners)])  72.1 us
    pallas_call x4, Pallas kernels, expert_on(): pl.pallas_call(functools.partial(expert_kernel, section, partners, capaci...  14.7 us
    ppermute x12, starting transfers between devices, exchange(): lax.ppermute(parts[k], 'expert', [(i, i ^ k) for i in range(partners)])  13.2 us
    pallas_call x4, Pallas kernels, call(): pl.pallas_call(kernel, out_shape=out_shape, in_specs=specs, out_specs=jax...  10.4 us
    pallas_call x2, Pallas kernels, pack(): pl.pallas_call(pack_kernel, out_shape=pltpu.HBM(shape, jnp.bfloat16), in_...  7.42 us
    ppermute x7, starting transfers between devices, other(): return lax.ppermute(array, 'section', pairs)  6.94 us
    ppermute x2, waiting for transfers between devices, across(): return lax.ppermute(array, axes, pairs)  6 us
    ppermute x7, waiting for transfers between devices, other(): return lax.ppermute(array, 'section', pairs)  5.87 us
  transfers between devices with their start and end apart: 21, of which 14 were waited for; matrix products, arithmetic and copies ran while one was open for 0% of the time, Pallas kernels for 16%

profile of v2, /device:TPU:9, one launch (start us, length us, event | category | flops | bytes accessed | tf_op | source)
XLA Modules:
  0.0 140.4 jit_solution(17746760622273264193)
XLA Ops:
  1.3 3.7 %pack.3.refs_0_ = bf16[97,128,128]{2,1,0:T(8,128)(2,1)} custom-call(s32[3]{0:T(128)S(1)} %pad_add_fusion.info, s32[1,32]{1,0:T(1,128)} %bitcast.23, s32[1,32]{1,0:T(1,128)} %bitcast.25, bf16[32,128,128]{2,1,0:T(8,128)(2,1)} %bitcast.17, bf16[32,128,128]{2,1,0:T(8,128)(2,1)} %bitcast.19, bf16[32,128,128]{2,1,0:T(8,128)(2,1)} %bitcast.21), custom_call_target="tpu_custom_call" | custom-call | tf_op jit(solution)/shard_map/pack/pallas_call | solution.py:362
  5.0 1.3 collective-permute-start.7
  6.3 2.6 %first_send.1 = (bf16[864,128]{1,0:T(8,128)(2,1)S(1)}, bf16[864,128]{1,0:T(8,128)(2,1)S(1)}, bf16[864,128]{1,0:T(8,128)(2,1)S(1)}, bf16[864,128]{1,0:T(8,128)(2,1)S(1)}) custom-call(s32[3]{0:T(128)S(1)} %pad_add_fusion.info, bf16[2,32,6144]{2,1,0:T(8,128)(2,1)} %tokens_ref.3, s32[1,2,2,32]{3,2,1,0:T(2,128)S(1)} %bitcast.11, f32[1,6144]{1,0:T(1,128)S(1)} %copy-done.8, ...), custom_call_target="tpu_custom_call" | custom-call | tf_op jit(solution)/shard_map/first_send/pallas_call | solution.py:435
  9.1 2.3 %collective-permute-start.4 = (bf16[864,128]{1,0:T(8,128)(2,1)S(1)}, bf16[864,128]{1,0:T(8,128)(2,1)S(1)}, u32[]{:S(2)}, u32[]{:S(2)}) collective-permute-start(bf16[864,128]{1,0:T(8,128)(2,1)S(1)} %get-tuple-element.34), channel_id=1, source_target_pairs={{0,4},{2,6},{4,0},{6,2},{1,5},{3,7},{5,1},{7,3},{8,12},{10,14},{12... | collective-permute-start | bytes 663560 | tf_op jit(solution)/shard_map/ppermute | solution.py:448
  11.6 6.2 %collective-permute-done.3.refs_3_.refs_1_ = bf16[864,128]{1,0:T(8,128)(2,1)S(1)} collective-permute-done((bf16[864,128]{1,0:T(8,128)(2,1)S(1)}, bf16[864,128]{1,0:T(8,128)(2,1)S(1)}, u32[]{:S(2)}, u32[]{:S(2)}) %collective-permute-start.3) | collective-permute-done | bytes 221216 | tf_op jit(solution)/shard_map/ppermute | solution.py:448
  17.8 3.8 %collective-permute-done.4.refs_4_.refs_2_ = bf16[864,128]{1,0:T(8,128)(2,1)S(1)} collective-permute-done((bf16[864,128]{1,0:T(8,128)(2,1)S(1)}, bf16[864,128]{1,0:T(8,128)(2,1)S(1)}, u32[]{:S(2)}, u32[]{:S(2)}) %collective-permute-start.4) | collective-permute-done | bytes 221216 | tf_op jit(solution)/shard_map/ppermute | solution.py:448
  21.5 9.5 %collective-permute-done.5.refs_5_.refs_3_ = bf16[864,128]{1,0:T(8,128)(2,1)S(1)} collective-permute-done((bf16[864,128]{1,0:T(8,128)(2,1)S(1)}, bf16[864,128]{1,0:T(8,128)(2,1)S(1)}, u32[]{:S(2)}, u32[]{:S(2)}) %collective-permute-start.5) | collective-permute-done | bytes 221216 | tf_op jit(solution)/shard_map/ppermute | solution.py:448
  31.0 3.7 %pack.2 = bf16[97,128,128]{2,1,0:T(8,128)(2,1)} custom-call(s32[3]{0:T(128)S(1)} %pad_add_fusion.info, s32[1,32]{1,0:T(1,128)} %bitcast.24, s32[1,32]{1,0:T(1,128)} %bitcast.26, bf16[32,128,128]{2,1,0:T(8,128)(2,1)} %bitcast.18, bf16[32,128,128]{2,1,0:T(8,128)(2,1)} %bitcast.20, bf16[32,128,128]{2,1,0:T(8,128)(2,1)} %bitcast.22, ...), custom_call_target="tpu_custom_call" | custom-call | tf_op jit(solution)/shard_map/pack/pallas_call | solution.py:362
  34.8 1.3 collective-permute-start.6
  36.1 6.0 %collective-permute-done.7.refs_0_ = bf16[97,128,128]{2,1,0:T(8,128)(2,1)} collective-permute-done((bf16[97,128,128]{2,1,0:T(8,128)(2,1)}, bf16[97,128,128]{2,1,0:T(8,128)(2,1)}, u32[]{:S(2)}, u32[]{:S(2)}) %collective-permute-start.7) | collective-permute-done | bytes 3178528 | tf_op jit(solution)/shard_map/ppermute | solution.py:417
  42.1 1.3 collective-permute-start.8
  43.4 1.3 collective-permute-start.12
  45.4 4.5 %collective-permute-done.8.refs_1_ = bf16[97,128,128]{2,1,0:T(8,128)(2,1)S(1)} collective-permute-done((bf16[97,128,128]{2,1,0:T(8,128)(2,1)}, bf16[97,128,128]{2,1,0:T(8,128)(2,1)S(1)}, u32[]{:S(2)}, u32[]{:S(2)}) %collective-permute-start.8) | collective-permute-done | bytes 3178528 | tf_op jit(solution)/shard_map/ppermute | solution.py:420
  49.9 6.6 %expert.5 = (bf16[864,128]{1,0:T(8,128)(2,1)}, bf16[864,128]{1,0:T(8,128)(2,1)}, bf16[864,128]{1,0:T(8,128)(2,1)}, bf16[864,128]{1,0:T(8,128)(2,1)}) custom-call(s32[3]{0:T(128)S(1)} %pad_add_fusion.info, bf16[97,128,128]{2,1,0:T(8,128)(2,1)} %collective-permute-done.6.refs_0_, ...), custom_call_target="tpu_custom_call", output_to_operand_aliasing={{0}: (7, {}), {1}: (8, {}), {2}: (9, {}), {3}: (10, {})} | custom-call | tf_op jit(solution)/shard_map/expert/pallas_call | solution.py:453
  56.5 2.4 %collective-permute-start.10 = (bf16[864,128]{1,0:T(8,128)(2,1)}, bf16[864,128]{1,0:T(8,128)(2,1)S(1)}, u32[]{:S(2)}, u32[]{:S(2)}) collective-permute-start(bf16[864,128]{1,0:T(8,128)(2,1)} %get-tuple-element.43), channel_id=1, source_target_pairs={{0,4},{2,6},{4,0},{6,2},{1,5},{3,7},{5,1},{7,3},{8,12},{10,14},{12... | collective-permute-start | bytes 663560 | tf_op jit(solution)/shard_map/ppermute | solution.py:448
  60.1 11.4 %collective-permute-done.10.rest_2_ = bf16[864,128]{1,0:T(8,128)(2,1)S(1)} collective-permute-done((bf16[864,128]{1,0:T(8,128)(2,1)}, bf16[864,128]{1,0:T(8,128)(2,1)S(1)}, u32[]{:S(2)}, u32[]{:S(2)}) %collective-permute-start.10) | collective-permute-done | bytes 221216 | tf_op jit(solution)/shard_map/ppermute | solution.py:448
  71.5 4.7 %collective-permute-done.11.rest_3_ = bf16[864,128]{1,0:T(8,128)(2,1)S(1)} collective-permute-done((bf16[864,128]{1,0:T(8,128)(2,1)}, bf16[864,128]{1,0:T(8,128)(2,1)S(1)}, u32[]{:S(2)}, u32[]{:S(2)}) %collective-permute-start.11) | collective-permute-done | bytes 221216 | tf_op jit(solution)/shard_map/ppermute | solution.py:448
  76.2 4.0 %relay.1 = (bf16[32,6144]{1,0:T(8,128)(2,1)S(1)}, bf16[1536,128]{1,0:T(8,128)(2,1)S(1)}, bf16[864,128]{1,0:T(8,128)(2,1)S(1)}, bf16[864,128]{1,0:T(8,128)(2,1)S(...) custom-call(s32[3]{0:T(128)S(1)} %pad_add_fusion.info, bf16[2,32,6144]{2,1,0:T(8,128)(2,1)} %tokens_ref.3, ...), custom_call_target="tpu_custom_call" | custom-call | tf_op jit(solution)/shard_map/relay/pallas_call | solution.py:435
  80.9 1.3 collective-permute-start.13
  82.3 3.4 %collective-permute-start.15 = (bf16[864,128]{1,0:T(8,128)(2,1)S(1)}, bf16[864,128]{1,0:T(8,128)(2,1)S(1)}, u32[]{:S(2)}, u32[]{:S(2)}) collective-permute-start(bf16[864,128]{1,0:T(8,128)(2,1)S(1)} %get-tuple-element.49), channel_id=1, source_target_pairs={{0,4},{2,6},{4,0},{6,2},{1,5},{3,7},{5,1},{7,3},{8,12},{10,14},{12... | collective-permute-start | bytes 663560 | tf_op jit(solution)/shard_map/ppermute | solution.py:448
  85.6 1.4 %collective-permute-done.14.refs_3_ = bf16[864,128]{1,0:T(8,128)(2,1)S(1)} collective-permute-done((bf16[864,128]{1,0:T(8,128)(2,1)S(1)}, bf16[864,128]{1,0:T(8,128)(2,1)S(1)}, u32[]{:S(2)}, u32[]{:S(2)}) %collective-permute-start.14) | collective-permute-done | bytes 221216 | tf_op jit(solution)/shard_map/ppermute | solution.py:448
  87.0 12.2 %collective-permute-done.15.refs_4_ = bf16[864,128]{1,0:T(8,128)(2,1)S(1)} collective-permute-done((bf16[864,128]{1,0:T(8,128)(2,1)S(1)}, bf16[864,128]{1,0:T(8,128)(2,1)S(1)}, u32[]{:S(2)}, u32[]{:S(2)}) %collective-permute-start.15) | collective-permute-done | bytes 221216 | tf_op jit(solution)/shard_map/ppermute | solution.py:448
  99.2 4.7 %collective-permute-done.16.refs_5_ = bf16[864,128]{1,0:T(8,128)(2,1)S(1)} collective-permute-done((bf16[864,128]{1,0:T(8,128)(2,1)S(1)}, bf16[864,128]{1,0:T(8,128)(2,1)S(1)}, u32[]{:S(2)}, u32[]{:S(2)}) %collective-permute-start.16) | collective-permute-done | bytes 221216 | tf_op jit(solution)/shard_map/ppermute | solution.py:448
  104.9 6.6 %expert.7 = (bf16[864,128]{1,0:T(8,128)(2,1)}, bf16[864,128]{1,0:T(8,128)(2,1)}, bf16[864,128]{1,0:T(8,128)(2,1)}, bf16[864,128]{1,0:T(8,128)(2,1)}) custom-call(s32[3]{0:T(128)S(1)} %pad_add_fusion.info, bf16[97,128,128]{2,1,0:T(8,128)(2,1)} %pack.3.refs_0_, ...), custom_call_target="tpu_custom_call", output_to_operand_aliasing={{0}: (7, {}), {1}: (8, {}), {2}: (9, {}), {3}: (10, {})} | custom-call | tf_op jit(solution)/shard_map/expert/pallas_call | solution.py:453
  111.5 3.4 %collective-permute-start.18 = (bf16[864,128]{1,0:T(8,128)(2,1)}, bf16[864,128]{1,0:T(8,128)(2,1)S(1)}, u32[]{:S(2)}, u32[]{:S(2)}) collective-permute-start(bf16[864,128]{1,0:T(8,128)(2,1)} %get-tuple-element.57), channel_id=1, source_target_pairs={{0,4},{2,6},{4,0},{6,2},{1,5},{3,7},{5,1},{7,3},{8,12},{10,14},{12... | collective-permute-start | bytes 663560 | tf_op jit(solution)/shard_map/ppermute | solution.py:448
  114.9 2.7 %collective-permute-done.17.rest_1_ = bf16[864,128]{1,0:T(8,128)(2,1)S(1)} collective-permute-done((bf16[864,128]{1,0:T(8,128)(2,1)}, bf16[864,128]{1,0:T(8,128)(2,1)S(1)}, u32[]{:S(2)}, u32[]{:S(2)}) %collective-permute-start.17) | collective-permute-done | bytes 221216 | tf_op jit(solution)/shard_map/ppermute | solution.py:448
  117.6 10.8 %collective-permute-done.18.rest_2_ = bf16[864,128]{1,0:T(8,128)(2,1)S(1)} collective-permute-done((bf16[864,128]{1,0:T(8,128)(2,1)}, bf16[864,128]{1,0:T(8,128)(2,1)S(1)}, u32[]{:S(2)}, u32[]{:S(2)}) %collective-permute-start.18) | collective-permute-done | bytes 221216 | tf_op jit(solution)/shard_map/ppermute | solution.py:448
  128.4 4.9 %collective-permute-done.19.rest_3_ = bf16[864,128]{1,0:T(8,128)(2,1)S(1)} collective-permute-done((bf16[864,128]{1,0:T(8,128)(2,1)}, bf16[864,128]{1,0:T(8,128)(2,1)S(1)}, u32[]{:S(2)}, u32[]{:S(2)}) %collective-permute-start.19) | collective-permute-done | bytes 221216 | tf_op jit(solution)/shard_map/ppermute | solution.py:448
  133.3 2.4 %last.1 = (bf16[32,6144]{1,0:T(8,128)(2,1)S(1)}, bf16[32,6144]{1,0:T(8,128)(2,1)S(1)}) custom-call(s32[3]{0:T(128)S(1)} %pad_add_fusion.info, bf16[32,6144]{1,0:T(8,128)(2,1)S(1)} %copy-done.7, bf16[1536,128]{1,0:T(8,128)(2,1)S(1)} %get-tuple-element.46.state, s32[1,2,2,32]{3,2,1,0:T(2,128)S(1)} %bitcast.13, f32[1,2,2,32]{3,2,1,0:T(2,128)S(1)} %bitcast.16, ...), custom_call_target="tpu_custom_call" | custom-call | tf_op jit(solution)/shard_map/last/pallas_call | solution.py:435
  135.7 1.9 %collective-permute-start.20 = (bf16[32,6144]{1,0:T(8,128)(2,1)S(1)}, bf16[32,6144]{1,0:T(8,128)(2,1)S(1)}, u32[]{:S(2)}, u32[]{:S(2)}) collective-permute-start(bf16[32,6144]{1,0:T(8,128)(2,1)S(1)} %get-tuple-element.60), channel_id=1, source_target_pairs={{0,1},{1,0},{2,3},{3,2},{4,5},{5,4},{6,7},{7,6},{8,9},{9,8},{10,11... | collective-permute-start | bytes 1179656 | tf_op jit(solution)/shard_map/ppermute | solution.py:420
  137.6 1.3 collective-permute-done.20.came
  138.9 1.5 %join.1 = bf16[1,2,32,6144]{3,2,1,0:T(8,128)(2,1)} custom-call(s32[3]{0:T(128)S(1)} %pad_add_fusion.info, bf16[32,6144]{1,0:T(8,128)(2,1)S(1)} %copy-done.7, bf16[32,6144]{1,0:T(8,128)(2,1)S(1)} %get-tuple-element.59.second, bf16[32,6144]{1,0:T(8,128)(2,1)S(1)} %collective-permute-done.20.came), custom_call_target="tpu_custom_call" | custom-call | tf_op jit(solution)/shard_map/join/pallas_call | solution.py:435
  (45 shorter events, 5.4 us)
Async XLA Ops:
  0.0 6.3 %collective-permute-start = (s32[1,2,2,32]{3,2,1,0:T(2,128)}, s32[1,2,2,32]{3,2,1,0:T(2,128)S(1)}, u32[]{:S(2)}, u32[]{:S(2)}) collective-permute-start(s32[1,2,2,32]{3,2,1,0:T(2,128)} %bitcast.10), channel_id=1, source_target_pairs={{0,1},{1,0},{2,3},{3,2},{4,5},{5,4},{6,7},{7,6},{8,9},{9,8},{10,11... | collective-permute-start | bytes 1544 | tf_op jit(solution)/shard_map/ppermute | solution.py:420
  0.7 5.6 %collective-permute-start.1 = (f32[1,2,2,32]{3,2,1,0:T(2,128)}, f32[1,2,2,32]{3,2,1,0:T(2,128)S(1)}, u32[]{:S(2)}, u32[]{:S(2)}) collective-permute-start(f32[1,2,2,32]{3,2,1,0:T(2,128)} %bitcast.14), channel_id=1, source_target_pairs={{0,1},{1,0},{2,3},{3,2},{4,5},{5,4},{6,7},{7,6},{8,9},{9,8},{10,11... | collective-permute-start | bytes 1544 | tf_op jit(solution)/shard_map/ppermute | solution.py:420
  0.7 5.6 %collective-permute-start.2 = (f32[1,6144]{1,0:T(1,128)}, f32[1,6144]{1,0:T(1,128)S(1)}, u32[]{:S(2)}, u32[]{:S(2)}) collective-permute-start(f32[1,6144]{1,0:T(1,128)} %gain.3), channel_id=1, source_target_pairs={{0,1},{1,0},{2,3},{3,2},{4,5},{5,4},{6,7},{7,6},{8,9},{9,8},{10,11... | collective-permute-start | bytes 73736 | tf_op jit(solution)/shard_map/ppermute | solution.py:420
  1.2 5.1 %copy-start.8 = (f32[1,6144]{1,0:T(1,128)S(1)}, f32[1,6144]{1,0:T(1,128)}, u32[]{:S(2)}) copy-start(f32[1,6144]{1,0:T(1,128)} %gain.3) | copy-start | bytes 73732
  1.2 5.1 %copy-start.9 = (s32[1,2,32,2]{2,3,1,0:T(2,128)S(1)}, s32[1,2,32,2]{2,3,1,0:T(2,128)}, u32[]{:S(2)}) copy-start(s32[1,2,32,2]{2,3,1,0:T(2,128)} %param.11) | copy-start | bytes 1540
  5.0 37.1 %collective-permute-start.7 = (bf16[97,128,128]{2,1,0:T(8,128)(2,1)}, bf16[97,128,128]{2,1,0:T(8,128)(2,1)}, u32[]{:S(2)}, u32[]{:S(2)}) collective-permute-start(bf16[97,128,128]{2,1,0:T(8,128)(2,1)} %pack.3.refs_0_), channel_id=1, source_target_pairs={{0,8},{1,17},{2,10},{3,19},{4,12},{5,21},{6,14},{7,23},{8,0},{9,25... | collective-permute-start | bytes 9535496 | tf_op jit(solution)/shard_map/ppermute | solution.py:417
  8.9 8.9 %collective-permute-start.3 = (bf16[864,128]{1,0:T(8,128)(2,1)S(1)}, bf16[864,128]{1,0:T(8,128)(2,1)S(1)}, u32[]{:S(2)}, u32[]{:S(2)}) collective-permute-start(bf16[864,128]{1,0:T(8,128)(2,1)S(1)} %get-tuple-element.33), channel_id=1, source_target_pairs={{0,2},{2,0},{4,6},{6,4},{1,3},{3,1},{5,7},{7,5},{8,10},{10,8},{12,... | collective-permute-start | bytes 663560 | tf_op jit(solution)/shard_map/ppermute | solution.py:448
  9.1 12.4 %collective-permute-start.4 = (bf16[864,128]{1,0:T(8,128)(2,1)S(1)}, bf16[864,128]{1,0:T(8,128)(2,1)S(1)}, u32[]{:S(2)}, u32[]{:S(2)}) collective-permute-start(bf16[864,128]{1,0:T(8,128)(2,1)S(1)} %get-tuple-element.34), channel_id=1, source_target_pairs={{0,4},{2,6},{4,0},{6,2},{1,5},{3,7},{5,1},{7,3},{8,12},{10,14},{12... | collective-permute-start | bytes 663560 | tf_op jit(solution)/shard_map/ppermute | solution.py:448
  11.5 19.6 %collective-permute-start.5 = (bf16[864,128]{1,0:T(8,128)(2,1)S(1)}, bf16[864,128]{1,0:T(8,128)(2,1)S(1)}, u32[]{:S(2)}, u32[]{:S(2)}) collective-permute-start(bf16[864,128]{1,0:T(8,128)(2,1)S(1)} %get-tuple-element.35), channel_id=1, source_target_pairs={{0,6},{2,4},{4,2},{6,0},{1,7},{3,5},{5,3},{7,1},{8,14},{10,12},{12... | collective-permute-start | bytes 663560 | tf_op jit(solution)/shard_map/ppermute | solution.py:448
  17.8 17.0 %copy-start = (bf16[864,128]{1,0:T(8,128)(2,1)}, bf16[864,128]{1,0:T(8,128)(2,1)S(1)}, u32[]{:S(2)}) copy-start(bf16[864,128]{1,0:T(8,128)(2,1)S(1)} %collective-permute-done.3.refs_3_.refs_1_) | copy-start | bytes 663556
  21.5 13.2 %copy-start.2 = (bf16[864,128]{1,0:T(8,128)(2,1)}, bf16[864,128]{1,0:T(8,128)(2,1)S(1)}, u32[]{:S(2)}) copy-start(bf16[864,128]{1,0:T(8,128)(2,1)S(1)} %collective-permute-done.4.refs_4_.refs_2_) | copy-start | bytes 663556
  31.0 3.8 %copy-start.4 = (bf16[864,128]{1,0:T(8,128)(2,1)}, bf16[864,128]{1,0:T(8,128)(2,1)S(1)}, u32[]{:S(2)}) copy-start(bf16[864,128]{1,0:T(8,128)(2,1)S(1)} %collective-permute-done.5.refs_5_.refs_3_) | copy-start | bytes 663556
  34.8 8.6 %collective-permute-start.6 = (bf16[97,128,128]{2,1,0:T(8,128)(2,1)}, bf16[97,128,128]{2,1,0:T(8,128)(2,1)}, u32[]{:S(2)}, u32[]{:S(2)}) collective-permute-start(bf16[97,128,128]{2,1,0:T(8,128)(2,1)} %pack.2), channel_id=1, source_target_pairs={{0,1},{1,0},{2,3},{3,2},{4,5},{5,4},{6,7},{7,6},{8,9},{9,8},{10,11... | collective-permute-start | bytes 9535496 | tf_op jit(solution)/shard_map/ppermute | solution.py:420
  36.1 8.6 %copy-start.1 = (bf16[864,128]{1,0:T(8,128)(2,1)S(1)}, bf16[864,128]{1,0:T(8,128)(2,1)}, u32[]{:S(2)}) copy-start(bf16[864,128]{1,0:T(8,128)(2,1)} %copy-done) | copy-start | bytes 663556
  36.1 8.6 %copy-start.3 = (bf16[864,128]{1,0:T(8,128)(2,1)S(1)}, bf16[864,128]{1,0:T(8,128)(2,1)}, u32[]{:S(2)}) copy-start(bf16[864,128]{1,0:T(8,128)(2,1)} %copy-done.2) | copy-start | bytes 663556
  36.1 8.6 %copy-start.5 = (bf16[864,128]{1,0:T(8,128)(2,1)S(1)}, bf16[864,128]{1,0:T(8,128)(2,1)}, u32[]{:S(2)}) copy-start(bf16[864,128]{1,0:T(8,128)(2,1)} %copy-done.4) | copy-start | bytes 663556
  42.1 7.8 %collective-permute-start.8 = (bf16[97,128,128]{2,1,0:T(8,128)(2,1)}, bf16[97,128,128]{2,1,0:T(8,128)(2,1)S(1)}, u32[]{:S(2)}, u32[]{:S(2)}) collective-permute-start(bf16[97,128,128]{2,1,0:T(8,128)(2,1)} %tie.2.refs_1_), channel_id=1, source_target_pairs={{0,1},{2,3},{4,5},{6,7},{8,9},{10,11},{12,13},{14,15},{16,17},{18,... | collective-permute-start | bytes 9535496 | tf_op jit(solution)/shard_map/ppermute | solution.py:420
  43.4 37.5 %collective-permute-start.12 = (bf16[97,128,128]{2,1,0:T(8,128)(2,1)}, bf16[97,128,128]{2,1,0:T(8,128)(2,1)}, u32[]{:S(2)}, u32[]{:S(2)}) collective-permute-start(bf16[97,128,128]{2,1,0:T(8,128)(2,1)} %collective-permute-done.6.refs_0_), channel_id=1, source_target_pairs={{0,8},{1,17},{2,10},{3,19},{4,12},{5,21},{6,14},{7,23},{8,0},{9,25... | collective-permute-start | bytes 9535496 | tf_op jit(solution)/shard_map/ppermute | solution.py:417
  49.9 26.3 %copy-start.10 = (f32[1,2,32,2]{2,3,1,0:T(2,128)S(1)}, f32[1,2,32,2]{2,3,1,0:T(2,128)}, u32[]{:S(2)}) copy-start(f32[1,2,32,2]{2,3,1,0:T(2,128)} %param.12) | copy-start | bytes 1540
  56.5 15.0 %collective-permute-start.10 = (bf16[864,128]{1,0:T(8,128)(2,1)}, bf16[864,128]{1,0:T(8,128)(2,1)S(1)}, u32[]{:S(2)}, u32[]{:S(2)}) collective-permute-start(bf16[864,128]{1,0:T(8,128)(2,1)} %get-tuple-element.43), channel_id=1, source_target_pairs={{0,4},{2,6},{4,0},{6,2},{1,5},{3,7},{5,1},{7,3},{8,12},{10,14},{12... | collective-permute-start | bytes 663560 | tf_op jit(solution)/shard_map/ppermute | solution.py:448
  58.9 17.3 %collective-permute-start.11 = (bf16[864,128]{1,0:T(8,128)(2,1)}, bf16[864,128]{1,0:T(8,128)(2,1)S(1)}, u32[]{:S(2)}, u32[]{:S(2)}) collective-permute-start(bf16[864,128]{1,0:T(8,128)(2,1)} %get-tuple-element.44), channel_id=1, source_target_pairs={{0,6},{2,4},{4,2},{6,0},{1,7},{3,5},{5,3},{7,1},{8,14},{10,12},{12... | collective-permute-start | bytes 663560 | tf_op jit(solution)/shard_map/ppermute | solution.py:448
  58.9 17.3 %collective-permute-start.9 = (bf16[864,128]{1,0:T(8,128)(2,1)}, bf16[864,128]{1,0:T(8,128)(2,1)S(1)}, u32[]{:S(2)}, u32[]{:S(2)}) collective-permute-start(bf16[864,128]{1,0:T(8,128)(2,1)} %get-tuple-element.42), channel_id=1, source_target_pairs={{0,2},{2,0},{4,6},{6,4},{1,3},{3,1},{5,7},{7,5},{8,10},{10,8},{12,... | collective-permute-start | bytes 663560 | tf_op jit(solution)/shard_map/ppermute | solution.py:448
  80.1 0.7 copy-start.6
  80.9 24.0 %collective-permute-start.13 = (bf16[97,128,128]{2,1,0:T(8,128)(2,1)}, bf16[97,128,128]{2,1,0:T(8,128)(2,1)S(1)}, u32[]{:S(2)}, u32[]{:S(2)}) collective-permute-start(bf16[97,128,128]{2,1,0:T(8,128)(2,1)} %tie.3.refs_1_), channel_id=1, source_target_pairs={{0,1},{2,3},{4,5},{6,7},{8,9},{10,11},{12,13},{14,15},{16,17},{18,... | collective-permute-start | bytes 9535496 | tf_op jit(solution)/shard_map/ppermute | solution.py:420
  82.2 4.8 %collective-permute-start.14 = (bf16[864,128]{1,0:T(8,128)(2,1)S(1)}, bf16[864,128]{1,0:T(8,128)(2,1)S(1)}, u32[]{:S(2)}, u32[]{:S(2)}) collective-permute-start(bf16[864,128]{1,0:T(8,128)(2,1)S(1)} %get-tuple-element.48), channel_id=1, source_target_pairs={{0,2},{2,0},{4,6},{6,4},{1,3},{3,1},{5,7},{7,5},{8,10},{10,8},{12,... | collective-permute-start | bytes 663560 | tf_op jit(solution)/shard_map/ppermute | solution.py:448
  82.3 17.0 %collective-permute-start.15 = (bf16[864,128]{1,0:T(8,128)(2,1)S(1)}, bf16[864,128]{1,0:T(8,128)(2,1)S(1)}, u32[]{:S(2)}, u32[]{:S(2)}) collective-permute-start(bf16[864,128]{1,0:T(8,128)(2,1)S(1)} %get-tuple-element.49), channel_id=1, source_target_pairs={{0,4},{2,6},{4,0},{6,2},{1,5},{3,7},{5,1},{7,3},{8,12},{10,14},{12... | collective-permute-start | bytes 663560 | tf_op jit(solution)/shard_map/ppermute | solution.py:448
  85.6 18.4 %collective-permute-start.16 = (bf16[864,128]{1,0:T(8,128)(2,1)S(1)}, bf16[864,128]{1,0:T(8,128)(2,1)S(1)}, u32[]{:S(2)}, u32[]{:S(2)}) collective-permute-start(bf16[864,128]{1,0:T(8,128)(2,1)S(1)} %get-tuple-element.50), channel_id=1, source_target_pairs={{0,6},{2,4},{4,2},{6,0},{1,7},{3,5},{5,3},{7,1},{8,14},{10,12},{12... | collective-permute-start | bytes 663560 | tf_op jit(solution)/shard_map/ppermute | solution.py:448
  104.9 28.4 %copy-start.7 = (bf16[32,6144]{1,0:T(8,128)(2,1)S(1)}, bf16[32,6144]{1,0:T(8,128)(2,1)}, u32[]{:S(2)}) copy-start(bf16[32,6144]{1,0:T(8,128)(2,1)} %copy-done.6) | copy-start | bytes 1179652
  111.5 6.1 %collective-permute-start.17 = (bf16[864,128]{1,0:T(8,128)(2,1)}, bf16[864,128]{1,0:T(8,128)(2,1)S(1)}, u32[]{:S(2)}, u32[]{:S(2)}) collective-permute-start(bf16[864,128]{1,0:T(8,128)(2,1)} %get-tuple-element.56), channel_id=1, source_target_pairs={{0,2},{2,0},{4,6},{6,4},{1,3},{3,1},{5,7},{7,5},{8,10},{10,8},{12,... | collective-permute-start | bytes 663560 | tf_op jit(solution)/shard_map/ppermute | solution.py:448
  111.5 16.9 %collective-permute-start.18 = (bf16[864,128]{1,0:T(8,128)(2,1)}, bf16[864,128]{1,0:T(8,128)(2,1)S(1)}, u32[]{:S(2)}, u32[]{:S(2)}) collective-permute-start(bf16[864,128]{1,0:T(8,128)(2,1)} %get-tuple-element.57), channel_id=1, source_target_pairs={{0,4},{2,6},{4,0},{6,2},{1,5},{3,7},{5,1},{7,3},{8,12},{10,14},{12... | collective-permute-start | bytes 663560 | tf_op jit(solution)/shard_map/ppermute | solution.py:448
  114.9 18.4 %collective-permute-start.19 = (bf16[864,128]{1,0:T(8,128)(2,1)}, bf16[864,128]{1,0:T(8,128)(2,1)S(1)}, u32[]{:S(2)}, u32[]{:S(2)}) collective-permute-start(bf16[864,128]{1,0:T(8,128)(2,1)} %get-tuple-element.58), channel_id=1, source_target_pairs={{0,6},{2,4},{4,2},{6,0},{1,7},{3,5},{5,3},{7,1},{8,14},{10,12},{12... | collective-permute-start | bytes 663560 | tf_op jit(solution)/shard_map/ppermute | solution.py:448
  135.7 3.2 %collective-permute-start.20 = (bf16[32,6144]{1,0:T(8,128)(2,1)S(1)}, bf16[32,6144]{1,0:T(8,128)(2,1)S(1)}, u32[]{:S(2)}, u32[]{:S(2)}) collective-permute-start(bf16[32,6144]{1,0:T(8,128)(2,1)S(1)} %get-tuple-element.60), channel_id=1, source_target_pairs={{0,1},{1,0},{2,3},{3,2},{4,5},{5,4},{6,7},{7,6},{8,9},{9,8},{10,11... | collective-permute-start | bytes 1179656 | tf_op jit(solution)/shard_map/ppermute | solution.py:420

commit v3 on v2

v3 whole, which is shorter than its diff:
```python
import functools
import itertools
import math

import jax
import jax.numpy as jnp
from jax import lax
from jax.experimental import pallas as pl
from jax.experimental.pallas import tpu as pltpu
from jax.sharding import PartitionSpec as P

TOP = 2
LANES = 128
EPS = 1e-05
MIB = 1 << 20


def up_to(value, unit):
    return -(-value // unit) * unit


def group_of(capacity):
    return 16 // math.gcd(capacity, 16)


def iota(shape, axis):
    return lax.broadcasted_iota(jnp.int32, shape, axis)


def split_by(values, unit):
    quotient = jnp.floor((values.astype(jnp.float32) + 0.5) * (1.0 / unit)).astype(jnp.int32)
    return quotient, values - quotient * unit


def dot(left, right, contract=((1,), (0,))):
    return lax.dot_general(left, right, (contract, ((), ())), preferred_element_type=jnp.float32)


def side_by_side(left, rights):
    products = []
    for at in range(0, len(rights), 2):
        pair = rights[at : at + 2]
        product = dot(left, jnp.concatenate(pair, axis=1))
        products += [product[:, i * LANES : (i + 1) * LANES] for i in range(len(pair))]
    return products


def spread_columns(values, rows):
    tokens = values.shape[1]
    token = split_by(iota((rows, tokens), 0), tokens)[1]
    same = iota((rows, tokens), 1) == token
    return [
        jnp.sum(jnp.where(same, values[choice : choice + 1, :], 0.0), axis=1, keepdims=True) for choice in range(TOP)
    ]


def picks_to_send(ids, experts, capacity, group):
    tokens = ids.shape[1]
    expert = iota((up_to(experts, 16), tokens), 0)
    hit = (ids[0:1, :] == expert) | (ids[1:2, :] == expert)
    hit = jnp.where(hit, 1.0, 0.0).astype(jnp.bfloat16)
    shape = (tokens, group * tokens)
    block, token = split_by(iota(shape, 1), tokens)
    earlier = jnp.where(iota(shape, 0) < token, 1.0, 0.0).astype(jnp.bfloat16)
    same = jnp.where(iota(shape, 0) == token, 1.0, 0.0).astype(jnp.bfloat16)
    slot = dot(hit, earlier)
    here = dot(hit, same)
    first = (block[0:1, :] * capacity).astype(jnp.float32)
    key = jnp.where(here > 0.5, slot + first, -1.0)
    row = iota((group * capacity, group * tokens), 0).astype(jnp.float32)
    return jnp.concatenate(
        [jnp.where(row == key[k : k + 1, :], 1.0, 0.0) for k in range(experts)], axis=0
    ).astype(jnp.bfloat16)


def picks_to_mix(ids, experts, capacity, group):
    tokens = ids.shape[1]
    rows = group * tokens
    token = split_by(iota((rows, tokens), 0), tokens)[1]
    first = (split_by(iota((rows, 1), 0), tokens)[0] * capacity).astype(jnp.float32)
    columns = iota((rows, experts * group * capacity), 1).astype(jnp.float32)
    earlier = iota((rows, tokens), 1) < token
    chosen = spread_columns(ids.astype(jnp.float32), rows)
    parts = []
    for choice in range(TOP):
        expert = chosen[choice]
        named = (ids[0:1, :].astype(jnp.float32) == expert) | (ids[1:2, :].astype(jnp.float32) == expert)
        slot = jnp.sum(jnp.where(named & earlier, 1.0, 0.0), axis=1, keepdims=True)
        key = expert * (group * capacity) + first + slot
        parts.append(jnp.where(columns == key, 1.0, 0.0))
    return jnp.concatenate(parts, axis=0).astype(jnp.bfloat16)


def send_rows(partners, state, scale, gain_of, outs, group, capacity, tokens):
    count = group * capacity
    blocks = state.shape[0] // tokens
    picks = picks_to_send(partners, len(outs), capacity, group)
    scale = jnp.concatenate([scale] * group, axis=0)
    normed = []
    for number in range(blocks // group):
        rows = state[number * group * tokens : (number + 1) * group * tokens, :]
        gain = jnp.concatenate(
            [jnp.broadcast_to(gain_of(number * group + j), (tokens, LANES)) for j in range(group)], axis=0
        )
        normed.append((rows.astype(jnp.float32) * scale * gain).astype(jnp.bfloat16))
    for number, picked in enumerate(side_by_side(picks, normed)):
        for k, out in enumerate(outs):
            out[number * count : (number + 1) * count, :] = picked[k * count : (k + 1) * count, :].astype(jnp.bfloat16)


def first_send_kernel(partners, capacity, group, info, tokens_ref, ids, gain, *rest):
    outs, (given, state, arrived) = rest[-partners - 3 : -3], rest[-3:]

    @pl.when(info[0] == 0)
    def _():
        copy = pltpu.make_async_copy(tokens_ref, given, arrived.at[0])
        copy.start()
        copy.wait()
        micro_count, tokens, width = given.shape
        blocks = width // LANES
        for micro in range(micro_count):
            total = jnp.zeros((tokens, 1), jnp.float32)
            for b in range(blocks):
                part = given[micro, :, b * LANES : (b + 1) * LANES]
                state[b * tokens : (b + 1) * tokens, :] = part
                wide = part.astype(jnp.float32)
                total += jnp.sum(wide * wide, axis=1, keepdims=True)
            scale = lax.rsqrt(total * (1.0 / width) + EPS)
            size = blocks * capacity
            targets = [out.at[micro * size : (micro + 1) * size, :] for out in outs]
            send_rows(ids[0, micro] ^ info[1], state, scale, lambda b: gain_of(gain, b), targets, group, capacity, tokens)


def gain_of(gain, block):
    return gain[0:1, block * LANES : (block + 1) * LANES]


def mix_rows(picks, base_of, weights, returned, blocks, group, capacity, tokens):
    count, rows = group * capacity, group * tokens
    given = [
        jnp.concatenate([part[number * count : (number + 1) * count, :] for part in returned], axis=0)
        for number in range(blocks // group)
    ]
    for number, picked in enumerate(side_by_side(picks, given)):
        total = base_of(number).astype(jnp.float32)
        for choice in range(TOP):
            total += weights[choice] * picked[choice * rows : (choice + 1) * rows, :]
        yield number, total.astype(jnp.bfloat16)


def relay_kernel(micro, partners, capacity, group, info, *refs):
    @pl.when(info[0] == 0)
    def _():
        relay_rows(micro, partners, capacity, group, info, *refs)


def relay_rows(micro, partners, capacity, group, info, tokens_ref, ids, weights, next_ids, next_gain, *rest):
    returned, (state_out, carry), outs = rest[:partners], rest[-partners - 3 : -partners - 1], rest[-partners - 1 : -2]
    given, arrived = rest[-2:]
    carried = carry.at[1]
    copy = pltpu.make_async_copy(tokens_ref.at[micro], given, arrived.at[0])
    copy.start()
    tokens, width = given.shape
    blocks = width // LANES
    state = carried.at[blocks * capacity : blocks * (capacity + tokens), :]
    picks = picks_to_mix(ids[0, micro] ^ info[1], partners, capacity, group)
    shares = spread_columns(weights[0, micro], group * tokens)
    total = jnp.zeros((tokens, 1), jnp.float32)
    copy.wait()

    def base_of(number):
        return jnp.concatenate(
            [given[:, b * LANES : (b + 1) * LANES] for b in range(number * group, (number + 1) * group)], axis=0
        )

    for number, mixed in mix_rows(picks, base_of, shares, returned, blocks, group, capacity, tokens):
        state[number * group * tokens : (number + 1) * group * tokens, :] = mixed
        wide = mixed.astype(jnp.float32)
        square = jnp.sum(wide * wide, axis=1, keepdims=True)
        for j in range(group):
            b = number * group + j
            state_out[:, b * LANES : (b + 1) * LANES] = mixed[j * tokens : (j + 1) * tokens, :]
            total += square[j * tokens : (j + 1) * tokens, :]
    scale = lax.rsqrt(total * (1.0 / width) + EPS)
    send_rows(
        next_ids[0, micro] ^ info[1], state, scale, lambda b: gain_of(next_gain, b), [carried, *outs], group, capacity, tokens
    )


def last_kernel(micro, partners, capacity, group, info, first, carried, ids, weights, *rest):
    returned, (out, made, done) = rest[:partners], rest[-3:]
    tokens, width = made.shape
    blocks = width // LANES
    keep = pltpu.make_async_copy(made, out.at[0, micro], done.at[0])

    @pl.when(info[0] == 0)
    def _():
        copy = pltpu.make_async_copy(first, made, done.at[1])
        copy.start()
        copy.wait()

    @pl.when(info[0] != 0)
    def _():
        picks = picks_to_mix(ids[0, micro] ^ info[1], partners, capacity, group)
        shares = spread_columns(weights[0, micro], group * tokens)

        def base_of(number):
            start = blocks * capacity + number * group * tokens
            return carried[start : start + group * tokens, :]

        for number, mixed in mix_rows(picks, base_of, shares, returned, blocks, group, capacity, tokens):
            for j in range(group):
                b = number * group + j
                made[:, b * LANES : (b + 1) * LANES] = mixed[j * tokens : (j + 1) * tokens, :]

    keep.start()
    keep.wait()


def expert_kernel(section, partners, offsets, capacity, group, split, unroll, info, *refs):
    @pl.when(info[0] == section)
    def _():
        expert_rows(partners, offsets, capacity, group, split, unroll, *refs)


def expert_rows(partners, offsets, capacity, group, split, unroll, *refs):
    halves, first = [], 0
    for pieces in split:
        halves.append(refs[first : first + pieces])
        first += pieces
    sent, outs = refs[first : first + partners], refs[-10 - partners : -10]
    numbers, places, placed, weights, arrived, state, hidden, total, made, left = refs[-10:]
    blocks = state.shape[0]
    padded = state.shape[1] // partners
    columns = (weights.shape[1] - 1) // 3
    count = group * capacity
    sizes = [columns] * 3 + [1]

    def part_of(k, number):
        return sent[k][number * count : (number + 1) * count, :]

    def load(half, which):
        source, start = halves[half][0], which * columns
        if len(halves[half]) > 1:
            source, start = halves[half][min(which, 2)], columns if which == 3 else 0
        return pltpu.make_async_copy(
            source.at[pl.ds(start, sizes[which])],
            weights.at[half, pl.ds(which * columns, sizes[which])],
            arrived.at[half, which],
        )

    for which in (3,), (0, 1), (2,):
        for half in range(len(halves)):
            for piece in which:
                load(half, piece).start()

    shape = (group * padded, count)
    block, slot = split_by(iota((group * padded, 1), 0), padded)
    key = jnp.where(slot < capacity, block * capacity + slot, -1)
    spread = jnp.where(iota(shape, 1) == key, 1.0, 0.0).astype(jnp.bfloat16)
    for number in range(blocks // group):
        spaced = side_by_side(
            spread, [p[at + number * count : at + (number + 1) * count, :] for p, at in zip(sent, offsets)]
        )
        for j in range(group):
            rows = jnp.concatenate([s[j * padded : (j + 1) * padded, :] for s in spaced], axis=0)
            state[number * group + j] = rows.astype(jnp.bfloat16)
            total[number * group + j] = jnp.zeros(rows.shape, jnp.float32)

    for half in range(len(halves)):
        load(half, 3).wait()
        numbers[half] = weights[half, 3 * columns, :16, :].astype(jnp.float32)[:8, :].astype(jnp.int32)
    moves = [pltpu.make_async_copy(numbers.at[half], places.at[half], placed.at[half]) for half in range(len(halves))]
    for move in moves:
        move.start()
    for move in moves:
        move.wait()

    for half in range(len(halves)):
        load(half, 0).wait()
        load(half, 1).wait()

        def up_step(at, carry, half=half):
            for i in range(unroll):
                c = at * unroll + i
                rows = state[places[half, 0, c]]
                both = dot(rows, jnp.concatenate([weights[half, c], weights[half, columns + c]], axis=1))
                gate, up = both[:, :LANES], both[:, LANES:]
                hidden[half * columns + c] = (gate / (1.0 + jnp.exp(-gate)) * up).astype(jnp.bfloat16)
            return carry

        lax.fori_loop(0, columns // unroll, up_step, 0)

    for half in range(len(halves)):
        load(half, 2).wait()

        def down_step(at, carry, half=half):
            produced = []
            for i in range(unroll):
                c = at * unroll + i
                produced.append(dot(hidden[half * columns + c], weights[half, 2 * columns + c]))
            for i in range(unroll):
                to = places[half, 1, at * unroll + i]
                total[to] = total[to] + produced[i]
            return carry

        lax.fori_loop(0, columns // unroll, down_step, 0)

    block, slot = split_by(iota((count, 1), 0), capacity)
    packing = jnp.where(iota((count, group * padded), 1) == block * padded + slot, 1.0, 0.0).astype(jnp.bfloat16)
    copies = [pltpu.make_async_copy(made.at[k], outs[k], left.at[k]) for k in range(partners)]
    for number in range(blocks // group):
        spaced = [
            jnp.concatenate(
                [total[number * group + j, k * padded : (k + 1) * padded, :] for j in range(group)], axis=0
            ).astype(jnp.bfloat16)
            for k in range(partners)
        ]
        for k, rows in enumerate(side_by_side(packing, spaced)):
            made[k, number * count : (number + 1) * count, :] = rows.astype(jnp.bfloat16)
    for copy in copies:
        copy.start()
    for copy in copies:
        copy.wait()


def pack_kernel(info, in_rows, out_cols, *refs):
    stored, (out, kept, numbers, named, arrived, left) = refs[:3], refs[-6:]
    columns = stored[0].shape[0]
    names = [
        pltpu.make_async_copy(source, numbers.at[at], named.at[at]) for at, source in enumerate((in_rows, out_cols))
    ]

    def take(at):
        return pltpu.make_async_copy(stored[at], kept.at[pl.ds(at * columns, columns)], arrived.at[at])

    def give(at):
        span = pl.ds(at * columns, columns + at // 2)
        return pltpu.make_async_copy(kept.at[span], out.at[span], left.at[at])

    for name in names:
        name.start()
    for at in range(3):
        take(at).start()
    spread = jnp.where(iota((columns, LANES), 0) == iota((columns, LANES), 1), 1.0, 0.0).astype(jnp.bfloat16)
    row = iota((LANES, LANES), 0)
    for name in names:
        name.wait()
    rows, cols = (
        dot(jnp.broadcast_to(numbers[at].astype(jnp.float32), (LANES, columns)).astype(jnp.bfloat16), spread)
        for at in range(2)
    )
    kept[3 * columns] = jnp.where(row == 0, rows, jnp.where(row == 1, cols, 0.0)).astype(jnp.bfloat16)
    for at in range(3):
        take(at).wait()
        give(at).start()
    for at in range(3):
        give(at).wait()


def tie_kernel(*refs):
    pass


SMEM = pl.BlockSpec(memory_space=pltpu.SMEM)
VMEM = pl.BlockSpec(memory_space=pltpu.VMEM)
ANY = pl.BlockSpec(memory_space=pl.ANY)


def held(*arrays):
    return [pltpu.with_memory_space_constraint(a, pltpu.HBM) for a in arrays]


def pack(info, places, weights, after):
    columns, *block = weights[0].shape
    shape = (3 * columns + 1, *block)
    return pl.pallas_call(
        pack_kernel,
        out_shape=pltpu.HBM(shape, jnp.bfloat16),
        in_specs=[SMEM] + [ANY] * (5 + len(after)),
        out_specs=ANY,
        scratch_shapes=[
            pltpu.VMEM(shape, jnp.bfloat16),
            pltpu.VMEM((2, 1, columns), jnp.int32),
            pltpu.SemaphoreType.DMA((2,)),
            pltpu.SemaphoreType.DMA((3,)),
            pltpu.SemaphoreType.DMA((3,)),
        ],
        compiler_params=pltpu.CompilerParams(vmem_limit_bytes=8 * MIB),
        name="pack",
    )(info, *held(*places, *weights), *after)


def tie(array, *others):
    return pl.pallas_call(
        tie_kernel,
        out_shape=pltpu.HBM(array.shape, array.dtype),
        in_specs=[ANY] * (1 + len(others)),
        out_specs=ANY,
        input_output_aliases={0: 0},
        name="tie",
    )(*held(array), *others)


def body(tokens, norm_gain, route_ids, route_weights, gate_blocks, up_blocks, down_blocks, gate_rows, down_cols):
    partners = lax.axis_size("expert")
    sections = lax.axis_size("section")
    shards = lax.axis_size("shard")
    micro_count, row_count, width = tokens.shape
    assert sections == 2 and gate_blocks.shape[1] == 1 and partners & (partners - 1) == 0
    assert lax.axis_size("groups") == 2
    blocks = width // LANES
    capacity = min(row_count, max(row_count * 9 // 16, row_count * TOP // partners + 2))
    group = group_of(capacity)
    size = blocks * capacity
    padded = up_to(capacity, 8)
    bf16, f32 = jnp.bfloat16, jnp.float32
    rows_shape = jax.ShapeDtypeStruct((size, LANES), bf16)
    carry_shape = pltpu.HBM((sections, size + blocks * row_count, LANES), bf16)
    state_shape = jax.ShapeDtypeStruct((row_count, width), bf16)
    info = jnp.stack([lax.axis_index(a) for a in ("section", "expert")]).astype(jnp.int32)
    weights = [a.reshape(a.shape[2:3] + a.shape[4:]) for a in (gate_blocks, up_blocks, down_blocks)]
    places = [a.reshape(1, -1) for a in (gate_rows, down_cols)]
    ids, shares = jnp.swapaxes(route_ids, 2, 3), jnp.swapaxes(route_weights, 2, 3)
    axes = ("groups", "shard", "expert", "section")
    sizes = [lax.axis_size(a) for a in axes]

    def trade(array, *moves):
        pairs = []
        for place in itertools.product(*(range(n) for n in sizes)):
            if moves[place[3]]:
                target = moves[place[3]](*place)
                pairs.append(tuple(sum(p * math.prod(sizes[i + 1 :]) for i, p in enumerate(q)) for q in (place, target)))
        return lax.ppermute(array, axes, pairs)

    def idle(g, s, e, c):
        return g ^ 1, s, e, c

    def to_partner(k):
        return lambda g, s, e, c: (g, s, e ^ k, c)

    def to_next(k):
        return lambda g, s, e, c: (g, s, e ^ k, 1)

    def idle_back(g, s, e, c):
        return g ^ 1, s, e, 0

    def across(g, s, e, c):
        return g, s ^ 1, e, c

    def exchange(parts, *moves_of):
        moved = list(parts)
        for k in range(partners - 1, 0, -1):
            moved[k] = trade(parts[k], *(m(k) for m in moves_of))
        return moved

    def swap(array):
        return lax.ppermute(array, "section", [(0, 1), (1, 0)])

    def always(move):
        return lambda k: move

    paired = shards == 2
    if not paired:
        weights = [lax.all_gather(a, "shard", axis=0, tiled=True) for a in weights]
        places = [lax.all_gather(a, "shard", axis=1, tiled=True) for a in places]
    columns = weights[0].shape[0]
    assert columns <= LANES

    def call(kernel, name, out_shape, args, specs, scratch, limit, out_specs=None, aliases={}):
        return pl.pallas_call(
            kernel,
            out_shape=out_shape,
            in_specs=specs,
            out_specs=out_specs or [VMEM] * len(out_shape),
            scratch_shapes=scratch,
            input_output_aliases=aliases,
            compiler_params=pltpu.CompilerParams(vmem_limit_bytes=limit * MIB),
            name=name,
        )(*args)

    def expert(layer, sources, rows, offsets, after):
        return call(
            functools.partial(
                expert_kernel, layer, partners, offsets, capacity, group, [1] * len(sources), math.gcd(columns, 32)
            ),
            "expert",
            [pltpu.HBM(rows_shape.shape, bf16)] * partners,
            (info, *held(*sources), *rows, *after),
            [SMEM] + [ANY] * len(sources) + [VMEM] * partners + [ANY] * len(after),
            [
                pltpu.VMEM((len(sources), 8, LANES), jnp.int32),
                pltpu.SMEM((len(sources), 8, LANES), jnp.int32),
                pltpu.SemaphoreType.DMA((len(sources),)),
                pltpu.VMEM((len(sources), 3 * columns + 1) + weights[0].shape[1:], bf16),
                pltpu.SemaphoreType.DMA((len(sources), 4)),
                pltpu.VMEM((blocks, partners * padded, LANES), bf16),
                pltpu.VMEM((len(sources) * columns, partners * padded, LANES), bf16),
                pltpu.VMEM((blocks, partners * padded, LANES), f32),
                pltpu.VMEM((partners,) + rows_shape.shape, bf16),
                pltpu.SemaphoreType.DMA((partners,)),
            ],
            22,
            [ANY] * partners,
        )

    packed = pack(info, places, weights, [])
    next_ids, next_gain = swap(ids), swap(norm_gain)
    sent = call(
        functools.partial(first_send_kernel, partners, capacity, group),
        "first_send",
        [jax.ShapeDtypeStruct((micro_count * size, LANES), bf16)] * partners,
        (info, *held(tokens), ids, norm_gain, next_ids, next_gain),
        [SMEM, ANY, VMEM, VMEM, ANY, ANY],
        [
            pltpu.VMEM(tokens.shape, bf16),
            pltpu.VMEM((blocks * row_count, LANES), bf16),
            pltpu.SemaphoreType.DMA((1,)),
        ],
        16,
    )
    rows = exchange(sent, to_partner, always(None))
    sources = [[packed], [packed]]
    if paired:
        moved = tie(trade(packed, across, idle), *rows[1:])
        packed = tie(packed, moved)
        arrived = trade(packed, None, across)
        sources = [[packed, moved], [packed, arrived]]
    after = []
    back = []
    for micro in range(micro_count):
        done = expert(0, sources[0], rows, [micro * size] * partners, after)
        after = held(done[0])
        back.append(exchange(done, to_partner, always(idle)))
    firsts, carries, given_rows = [], [], []
    for micro in range(micro_count):
        first, carry, *sent = call(
            functools.partial(relay_kernel, micro, partners, capacity, group),
            "relay",
            [pltpu.HBM(state_shape.shape, bf16), carry_shape] + [rows_shape] * (partners - 1),
            (info, *held(tokens), ids, shares, next_ids, next_gain, *held(back[micro][0]), *back[micro][1:], *after),
            [SMEM, ANY] + [VMEM] * (4 + partners) + [ANY] * len(after),
            [pltpu.VMEM((row_count, width), bf16), pltpu.SemaphoreType.DMA((1,))],
            12,
        )
        after = held(first)
        firsts.append(first)
        carries.append(carry)
        given_rows.append(exchange([carry] + sent, to_next, always(idle_back)))
    carries = [
        lax.all_to_all(carry, "section", split_axis=0, concat_axis=0, tiled=True).reshape(-1, LANES) for carry in carries
    ]
    given_rows = [[carry] + parts[1:] for carry, parts in zip(carries, given_rows)]
    after = held(first)
    back = []
    for micro in range(micro_count):
        done = expert(1, sources[1], given_rows[micro], [0] * partners, after)
        after = [swap(done[0])]
        back.append(exchange(done, always(idle), to_partner))
    out = None
    for micro in range(micro_count):
        kept = [] if out is None else held(out)
        out = call(
            functools.partial(last_kernel, micro, partners, capacity, group),
            "last",
            pltpu.HBM((1, micro_count, row_count, width), bf16),
            (
                info,
                *held(firsts[micro]),
                carries[micro],
                ids,
                shares,
                *held(back[micro][0]),
                *back[micro][1:],
                *kept,
            ),
            [SMEM, ANY] + [VMEM] * (3 + partners) + [ANY] * len(kept),
            [pltpu.VMEM((row_count, width), bf16), pltpu.SemaphoreType.DMA((2,))],
            12,
            ANY,
            {5 + partners: 0} if kept else {},
        )
    return out


def solution(mesh):
    in_specs = (
        P(None, ("groups", "shard", "expert"), None),
        P("section", None),
        P("section", None, ("groups", "shard", "expert"), None),
        P("section", None, ("groups", "shard", "expert"), None),
        P("section", "expert", "shard", None, None, None),
        P("section", "expert", "shard", None, None, None),
        P("section", "expert", "shard", None, None, None),
        P("section", "expert", "shard", None),
        P("section", "expert", "shard", None),
    )
    out_specs = P("section", None, ("groups", "shard", "expert"), None)
    return jax.shard_map(body, mesh=mesh, in_specs=in_specs, out_specs=out_specs, check_vma=False)
```

time: 142 us -> 123 us (0.87)
  waiting for transfers between devices: 84 us -> 44.3 us
  starting transfers between devices: 22.8 us -> 49.5 us
  Pallas kernels: 32.5 us -> 27.9 us
    ppermute x21 -> x26, waiting for transfers between devices: 84 us -> 43.7 us  [the longest x23 42.6 us: trade(): return lax.ppermute(array, axes, pairs)]
    ppermute x21 -> x26, starting transfers between devices: 22.8 us -> 41.1 us  [the longest x23 40 us: trade(): return lax.ppermute(array, axes, pairs)]
    all_to_all x0 -> x2, starting transfers between devices: none -> 8.41 us  [body(): lax.all_to_all(carry, 'section', split_axis=0, concat_axis=0, tiled=True)]
    pallas_call x2 -> x1, Pallas kernels: 7.42 us -> 3.73 us  [pack(): pl.pallas_call(pack_kernel, out_shape=pltpu.HBM(shape, jnp.bfloat16), in_...]
    pallas_call x8 -> x9, Pallas kernels: 25.1 us -> 24.2 us  [call(): pl.pallas_call(kernel, out_shape=out_shape, in_specs=specs, out_specs=out...]
  transfers between devices with their start and end apart: 21 -> 28, of which waited for: 14 -> 9; matrix products, arithmetic and copies ran while one was open for 0% -> 0% of each run, Pallas kernels for 16% -> 18%
where the time goes in v3:
time: 123 us; the launch traced here: 122 us
  starting transfers between devices  49.5 us (40%)
  waiting for transfers between devices  44.3 us (36%)
  Pallas kernels  27.9 us (23%)
    ppermute x23, waiting for transfers between devices, trade(): return lax.ppermute(array, axes, pairs)  42.6 us
    ppermute x23, starting transfers between devices, trade(): return lax.ppermute(array, axes, pairs)  40 us
    pallas_call x9, Pallas kernels, call(): pl.pallas_call(kernel, out_shape=out_shape, in_specs=specs, out_specs=out...  24.2 us
    all_to_all x2, starting transfers between devices, body(): lax.all_to_all(carry, 'section', split_axis=0, concat_axis=0, tiled=True)  8.41 us
    pallas_call x1, Pallas kernels, pack(): pl.pallas_call(pack_kernel, out_shape=pltpu.HBM(shape, jnp.bfloat16), in_...  3.73 us
  transfers between devices with their start and end apart: 28, of which 9 were waited for; matrix products, arithmetic and copies ran while one was open for 0% of the time, Pallas kernels for 18%

profile of v3, /device:TPU:9, one launch (start us, length us, event | category | flops | bytes accessed | tf_op | source)
XLA Modules:
  0.0 122.2 jit_solution(7790601391587630304)
XLA Ops:
  0.1 3.7 %pack.1.refs_0_ = bf16[97,128,128]{2,1,0:T(8,128)(2,1)} custom-call(s32[2]{0:T(128)S(1)} %pad_add_fusion.info, s32[1,32]{1,0:T(1,128)} %bitcast.28, s32[1,32]{1,0:T(1,128)} %bitcast.29, bf16[32,128,128]{2,1,0:T(8,128)(2,1)} %bitcast.25, bf16[32,128,128]{2,1,0:T(8,128)(2,1)} %bitcast.26, bf16[32,128,128]{2,1,0:T(8,128)(2,1)} %bitcast.27), custom_call_target="tpu_custom_call" | custom-call | tf_op jit(solution)/shard_map/pack/pallas_call | solution.py:377
  3.8 1.3 %collective-permute-start.2 = (bf16[97,128,128]{2,1,0:T(8,128)(2,1)}, bf16[97,128,128]{2,1,0:T(8,128)(2,1)}, u32[]{:S(2)}, u32[]{:S(2)}) collective-permute-start(bf16[97,128,128]{2,1,0:T(8,128)(2,1)} %pack.1.refs_0_), channel_id=1, source_target_pairs={{0,8},{1,17},{2,10},{3,19},{4,12},{5,21},{6,14},{7,23},{8,0},{9,25... | collective-permute-start | bytes 9535496 | tf_op jit(solution)/shard_map/ppermute | solution.py:434
  5.1 0.9 collective-permute-start.1
  6.1 1.1 collective-permute-done.rest_0_.refs_3_
  8.5 0.7 collective-permute-start.4
  9.9 31.0 %collective-permute-done.2.refs_0_ = bf16[97,128,128]{2,1,0:T(8,128)(2,1)} collective-permute-done((bf16[97,128,128]{2,1,0:T(8,128)(2,1)}, bf16[97,128,128]{2,1,0:T(8,128)(2,1)}, u32[]{:S(2)}, u32[]{:S(2)}) %collective-permute-start.2) | collective-permute-done | bytes 3178528 | tf_op jit(solution)/shard_map/ppermute | solution.py:434
  41.0 3.2 %collective-permute-start.12 = (bf16[97,128,128]{2,1,0:T(8,128)(2,1)}, bf16[97,128,128]{2,1,0:T(8,128)(2,1)}, u32[]{:S(2)}, u32[]{:S(2)}) collective-permute-start(bf16[97,128,128]{2,1,0:T(8,128)(2,1)} %tie.3.refs_0_), channel_id=1, source_target_pairs={{1,9},{3,11},{5,13},{7,15},{9,1},{11,3},{13,5},{15,7},{17,25},{19,... | collective-permute-start | bytes 9535496 | tf_op jit(solution)/shard_map/ppermute | solution.py:434
  45.0 1.3 %collective-permute-start.9 = (bf16[864,128]{1,0:T(8,128)(2,1)}, bf16[864,128]{1,0:T(8,128)(2,1)S(1)}, u32[]{:S(2)}, u32[]{:S(2)}) collective-permute-start(bf16[864,128]{1,0:T(8,128)(2,1)} %get-tuple-element.44), channel_id=1, source_target_pairs={{0,2},{1,17},{2,0},{3,19},{4,6},{5,21},{6,4},{7,23},{8,10},{9,25},... | collective-permute-start | bytes 663560 | tf_op jit(solution)/shard_map/ppermute | solution.py:434
  46.5 1.2 %collective-permute-start.11 = (bf16[864,128]{1,0:T(8,128)(2,1)}, bf16[864,128]{1,0:T(8,128)(2,1)S(1)}, u32[]{:S(2)}, u32[]{:S(2)}) collective-permute-start(bf16[864,128]{1,0:T(8,128)(2,1)} %get-tuple-element.46), channel_id=1, source_target_pairs={{0,6},{1,17},{2,4},{3,19},{4,2},{5,21},{6,0},{7,23},{8,14},{9,25},... | collective-permute-start | bytes 663560 | tf_op jit(solution)/shard_map/ppermute | solution.py:434
  48.7 1.3 %collective-permute-done.9.refs_6_ = bf16[864,128]{1,0:T(8,128)(2,1)S(1)} collective-permute-done((bf16[864,128]{1,0:T(8,128)(2,1)}, bf16[864,128]{1,0:T(8,128)(2,1)S(1)}, u32[]{:S(2)}, u32[]{:S(2)}) %collective-permute-start.9) | collective-permute-done | bytes 221216 | tf_op jit(solution)/shard_map/ppermute | solution.py:434
  50.1 1.2 %collective-permute-start.7 = (bf16[864,128]{1,0:T(8,128)(2,1)}, bf16[864,128]{1,0:T(8,128)(2,1)S(1)}, u32[]{:S(2)}, u32[]{:S(2)}) collective-permute-start(bf16[864,128]{1,0:T(8,128)(2,1)} %get-tuple-element.42), channel_id=1, source_target_pairs={{0,4},{1,17},{2,6},{3,19},{4,0},{5,21},{6,2},{7,23},{8,12},{9,25},... | collective-permute-start | bytes 663560 | tf_op jit(solution)/shard_map/ppermute | solution.py:434
  51.3 1.1 collective-permute-done.10.refs_7_
  52.4 1.2 %collective-permute-start.8 = (bf16[864,128]{1,0:T(8,128)(2,1)}, bf16[864,128]{1,0:T(8,128)(2,1)S(1)}, u32[]{:S(2)}, u32[]{:S(2)}) collective-permute-start(bf16[864,128]{1,0:T(8,128)(2,1)} %get-tuple-element.43), channel_id=1, source_target_pairs={{0,6},{1,17},{2,4},{3,19},{4,2},{5,21},{6,0},{7,23},{8,14},{9,25},... | collective-permute-start | bytes 663560 | tf_op jit(solution)/shard_map/ppermute | solution.py:434
  53.7 1.4 %collective-permute-done.11.refs_8_ = bf16[864,128]{1,0:T(8,128)(2,1)S(1)} collective-permute-done((bf16[864,128]{1,0:T(8,128)(2,1)}, bf16[864,128]{1,0:T(8,128)(2,1)S(1)}, u32[]{:S(2)}, u32[]{:S(2)}) %collective-permute-start.11) | collective-permute-done | bytes 221216 | tf_op jit(solution)/shard_map/ppermute | solution.py:434
  55.1 2.2 %relay.2 = (bf16[32,6144]{1,0:T(8,128)(2,1)}, bf16[2,2400,128]{2,1,0:T(8,128)(2,1)}, bf16[864,128]{1,0:T(8,128)(2,1)S(1)}, bf16[864,128]{1,0:T(8,128)(2,1)S(1)}, bf16[864,128]{1,0:T(8,128)(2,1)S(1)}) custom-call(s32[2]{0:T(128)S(1)} %pad_add_fusion.info, bf16[2,32,6144]{2,1,0:T(8,128)(2,1)} %refs_0_.3, s32[1,2,2,32]{3,2,1,0:T(2,128)S(1)} %bitcast.17, ...), custom_call_target="tpu_custom_call" | custom-call | tf_op jit(solution)/shard_map/relay/pallas_call | solution.py:471
  57.3 14.8 %collective-permute-start.16 = (bf16[864,128]{1,0:T(8,128)(2,1)S(1)}, bf16[864,128]{1,0:T(8,128)(2,1)S(1)}, u32[]{:S(2)}, u32[]{:S(2)}) collective-permute-start(bf16[864,128]{1,0:T(8,128)(2,1)S(1)} %get-tuple-element.54), channel_id=1, source_target_pairs={{0,3},{1,16},{2,1},{3,18},{4,7},{5,20},{6,5},{7,22},{8,11},{9,24},... | collective-permute-start | bytes 663560 | tf_op jit(solution)/shard_map/ppermute | solution.py:434
  72.2 2.7 %collective-permute-start.18 = (bf16[864,128]{1,0:T(8,128)(2,1)S(1)}, bf16[864,128]{1,0:T(8,128)(2,1)S(1)}, u32[]{:S(2)}, u32[]{:S(2)}) collective-permute-start(bf16[864,128]{1,0:T(8,128)(2,1)S(1)} %get-tuple-element.56), channel_id=1, source_target_pairs={{0,7},{1,16},{2,5},{3,18},{4,3},{5,20},{6,1},{7,22},{8,15},{9,24},... | collective-permute-start | bytes 663560 | tf_op jit(solution)/shard_map/ppermute | solution.py:434
  74.9 3.6 %all-to-all-start.1 = ((bf16[2,2400,128]{2,1,0:T(8,128)(2,1)}), bf16[2,2400,128]{2,1,0:T(8,128)(2,1)S(1)}, u32[]{:S(2)}, u32[]{:S(2)}) async-start(bf16[2,2400,128]{2,1,0:T(8,128)(2,1)} %get-tuple-element.53), calls=%async_computation.1 | async-start | bytes 2457600 | tf_op jit(solution)/shard_map/all_to_all | solution.py:551
  78.5 2.5 %relay.3 = (bf16[32,6144]{1,0:T(8,128)(2,1)}, bf16[2,2400,128]{2,1,0:T(8,128)(2,1)}, bf16[864,128]{1,0:T(8,128)(2,1)}, bf16[864,128]{1,0:T(8,128)(2,1)}, bf16[864,128]{1,0:T(8,128)(2,1)}) custom-call(s32[2]{0:T(128)S(1)} %pad_add_fusion.info, bf16[2,32,6144]{2,1,0:T(8,128)(2,1)} %refs_0_.3, s32[1,2,2,32]{3,2,1,0:T(2,128)S(1)} %bitcast.18, ...), custom_call_target="tpu_custom_call" | custom-call | tf_op jit(solution)/shard_map/relay/pallas_call | solution.py:471
  81.1 2.9 %collective-permute-start.13 = (bf16[864,128]{1,0:T(8,128)(2,1)}, bf16[864,128]{1,0:T(8,128)(2,1)S(1)}, u32[]{:S(2)}, u32[]{:S(2)}) collective-permute-start(bf16[864,128]{1,0:T(8,128)(2,1)} %get-tuple-element.50), channel_id=1, source_target_pairs={{0,3},{1,16},{2,1},{3,18},{4,7},{5,20},{6,5},{7,22},{8,11},{9,24},... | collective-permute-start | bytes 663560 | tf_op jit(solution)/shard_map/ppermute | solution.py:434
  84.1 2.6 %collective-permute-start.15 = (bf16[864,128]{1,0:T(8,128)(2,1)}, bf16[864,128]{1,0:T(8,128)(2,1)S(1)}, u32[]{:S(2)}, u32[]{:S(2)}) collective-permute-start(bf16[864,128]{1,0:T(8,128)(2,1)} %get-tuple-element.52), channel_id=1, source_target_pairs={{0,7},{1,16},{2,5},{3,18},{4,3},{5,20},{6,1},{7,22},{8,15},{9,24},... | collective-permute-start | bytes 663560 | tf_op jit(solution)/shard_map/ppermute | solution.py:434
  86.7 5.9 %expert.6 = (bf16[864,128]{1,0:T(8,128)(2,1)}, bf16[864,128]{1,0:T(8,128)(2,1)}, bf16[864,128]{1,0:T(8,128)(2,1)}, bf16[864,128]{1,0:T(8,128)(2,1)}) custom-call(s32[2]{0:T(128)S(1)} %pad_add_fusion.info, bf16[97,128,128]{2,1,0:T(8,128)(2,1)} %tie.3.refs_0_, bf16[97,128,128]{2,1,0:T(8,128)(2,1)} %collective-permute-done.12.refs_1_, ...), custom_call_target="tpu_custom_call" | custom-call | tf_op jit(solution)/shard_map/expert/pallas_call | solution.py:471
  93.0 4.8 %all-to-all-start = ((bf16[2,2400,128]{2,1,0:T(8,128)(2,1)}), bf16[2,2400,128]{2,1,0:T(8,128)(2,1)S(1)}, u32[]{:S(2)}, u32[]{:S(2)}) async-start(bf16[2,2400,128]{2,1,0:T(8,128)(2,1)} %get-tuple-element.49), calls=%async_computation | async-start | bytes 2457600 | tf_op jit(solution)/shard_map/all_to_all | solution.py:551
  97.8 1.1 collective-permute-start.24
  99.7 5.8 %expert.7 = (bf16[864,128]{1,0:T(8,128)(2,1)}, bf16[864,128]{1,0:T(8,128)(2,1)}, bf16[864,128]{1,0:T(8,128)(2,1)}, bf16[864,128]{1,0:T(8,128)(2,1)}) custom-call(s32[2]{0:T(128)S(1)} %pad_add_fusion.info, bf16[97,128,128]{2,1,0:T(8,128)(2,1)} %tie.3.refs_0_, bf16[97,128,128]{2,1,0:T(8,128)(2,1)} %collective-permute-done.12.refs_1_, ...), custom_call_target="tpu_custom_call" | custom-call | tf_op jit(solution)/shard_map/expert/pallas_call | solution.py:471
  105.5 1.8 %collective-permute-start.20 = (bf16[864,128]{1,0:T(8,128)(2,1)}, bf16[864,128]{1,0:T(8,128)(2,1)S(1)}, u32[]{:S(2)}, u32[]{:S(2)}) collective-permute-start(bf16[864,128]{1,0:T(8,128)(2,1)} %get-tuple-element.59), channel_id=1, source_target_pairs={{0,16},{1,3},{2,18},{3,1},{4,20},{5,7},{6,22},{7,5},{8,24},{9,11},... | collective-permute-start | bytes 663560 | tf_op jit(solution)/shard_map/ppermute | solution.py:434
  107.8 0.7 collective-permute-start.22
  108.5 1.5 %collective-permute-done.25.rest_3_ = bf16[864,128]{1,0:T(8,128)(2,1)} collective-permute-done((bf16[864,128]{1,0:T(8,128)(2,1)}, bf16[864,128]{1,0:T(8,128)(2,1)}, u32[]{:S(2)}, u32[]{:S(2)}) %collective-permute-start.25) | collective-permute-done | bytes 221216 | tf_op jit(solution)/shard_map/ppermute | solution.py:434
  110.1 3.0 %last.2.rest_4_ = bf16[1,2,32,6144]{3,2,1,0:T(8,128)(2,1)} custom-call(s32[2]{0:T(128)S(1)} %pad_add_fusion.info, bf16[32,6144]{1,0:T(8,128)(2,1)} %get-tuple-element.47.refs_9_.first, bf16[4800,128]{1,0:T(8,128)(2,1)S(1)} %bitcast.12, s32[1,2,2,32]{3,2,1,0:T(2,128)S(1)} %bitcast.19, f32[1,2,2,32]{3,2,1,0:T(2,128)S(1)} %bitcast.23, ...), custom_call_target="tpu_custom_call" | custom-call | tf_op jit(solution)/shard_map/last/pallas_call | solution.py:471
  113.1 3.3 %collective-permute-done.21.rest_2_ = bf16[864,128]{1,0:T(8,128)(2,1)S(1)} collective-permute-done((bf16[864,128]{1,0:T(8,128)(2,1)}, bf16[864,128]{1,0:T(8,128)(2,1)S(1)}, u32[]{:S(2)}, u32[]{:S(2)}) %collective-permute-start.21) | collective-permute-done | bytes 221216 | tf_op jit(solution)/shard_map/ppermute | solution.py:434
  116.3 2.9 %collective-permute-done.22.rest_3_ = bf16[864,128]{1,0:T(8,128)(2,1)S(1)} collective-permute-done((bf16[864,128]{1,0:T(8,128)(2,1)}, bf16[864,128]{1,0:T(8,128)(2,1)S(1)}, u32[]{:S(2)}, u32[]{:S(2)}) %collective-permute-start.22) | collective-permute-done | bytes 221216 | tf_op jit(solution)/shard_map/ppermute | solution.py:434
  119.3 2.8 %last.3 = bf16[1,2,32,6144]{3,2,1,0:T(8,128)(2,1)} custom-call(s32[2]{0:T(128)S(1)} %pad_add_fusion.info, bf16[32,6144]{1,0:T(8,128)(2,1)} %get-tuple-element.48.refs_6_.first, bf16[4800,128]{1,0:T(8,128)(2,1)S(1)} %bitcast.14, s32[1,2,2,32]{3,2,1,0:T(2,128)S(1)} %bitcast.20, f32[1,2,2,32]{3,2,1,0:T(2,128)S(1)} %bitcast.24, ...), custom_call_target="tpu_custom_call", output_to_operand_aliasing={{}: (9, {})} | custom-call | tf_op jit(solution)/shard_map/last/pallas_call | solution.py:471
  (55 shorter events, 5.9 us)
Async XLA Ops:
  3.8 37.1 %collective-permute-start.2 = (bf16[97,128,128]{2,1,0:T(8,128)(2,1)}, bf16[97,128,128]{2,1,0:T(8,128)(2,1)}, u32[]{:S(2)}, u32[]{:S(2)}) collective-permute-start(bf16[97,128,128]{2,1,0:T(8,128)(2,1)} %pack.1.refs_0_), channel_id=1, source_target_pairs={{0,8},{1,17},{2,10},{3,19},{4,12},{5,21},{6,14},{7,23},{8,0},{9,25... | collective-permute-start | bytes 9535496 | tf_op jit(solution)/shard_map/ppermute | solution.py:434
  5.1 2.1 %collective-permute-start.1 = (f32[1,6144]{1,0:T(1,128)S(1)}, f32[1,6144]{1,0:T(1,128)S(1)}, u32[]{:S(2)}, u32[]{:S(2)}) collective-permute-start(f32[1,6144]{1,0:T(1,128)S(1)} %copy-done.8), channel_id=1, source_target_pairs={{0,1},{1,0},{2,3},{3,2},{4,5},{5,4},{6,7},{7,6},{8,9},{9,8},{10,11... | collective-permute-start | bytes 73736 | tf_op jit(solution)/shard_map/ppermute | solution.py:458
  6.1 1.2 collective-permute-start
  7.8 2.1 %collective-permute-start.3 = (bf16[1728,128]{1,0:T(8,128)(2,1)S(1)}, bf16[1728,128]{1,0:T(8,128)(2,1)S(1)}, u32[]{:S(2)}, u32[]{:S(2)}) collective-permute-start(bf16[1728,128]{1,0:T(8,128)(2,1)S(1)} %get-tuple-element.35), channel_id=1, source_target_pairs={{0,2},{2,0},{4,6},{6,4},{8,10},{10,8},{12,14},{14,12},{16,18},{18,... | collective-permute-start | bytes 1327112 | tf_op jit(solution)/shard_map/ppermute | solution.py:434
  8.5 1.4 %collective-permute-start.4 = (bf16[1728,128]{1,0:T(8,128)(2,1)S(1)}, bf16[1728,128]{1,0:T(8,128)(2,1)S(1)}, u32[]{:S(2)}, u32[]{:S(2)}) collective-permute-start(bf16[1728,128]{1,0:T(8,128)(2,1)S(1)} %get-tuple-element.36), channel_id=1, source_target_pairs={{0,4},{2,6},{4,0},{6,2},{8,12},{10,14},{12,8},{14,10},{16,20},{18,... | collective-permute-start | bytes 1327112 | tf_op jit(solution)/shard_map/ppermute | solution.py:434
  9.2 0.7 collective-permute-start.5
  9.9 31.1 %copy-start = (bf16[1728,128]{1,0:T(8,128)(2,1)}, bf16[1728,128]{1,0:T(8,128)(2,1)S(1)}, u32[]{:S(2)}) copy-start(bf16[1728,128]{1,0:T(8,128)(2,1)S(1)} %collective-permute-done.3.refs_1_.refs_3_) | copy-start | bytes 1327108
  9.9 31.1 %copy-start.2 = (bf16[1728,128]{1,0:T(8,128)(2,1)}, bf16[1728,128]{1,0:T(8,128)(2,1)S(1)}, u32[]{:S(2)}) copy-start(bf16[1728,128]{1,0:T(8,128)(2,1)S(1)} %collective-permute-done.4.refs_2_.refs_4_) | copy-start | bytes 1327108
  9.9 31.0 %copy-start.4 = (bf16[1728,128]{1,0:T(8,128)(2,1)}, bf16[1728,128]{1,0:T(8,128)(2,1)S(1)}, u32[]{:S(2)}) copy-start(bf16[1728,128]{1,0:T(8,128)(2,1)S(1)} %collective-permute-done.5.refs_3_.refs_5_) | copy-start | bytes 1327108
  41.0 45.7 %collective-permute-start.12 = (bf16[97,128,128]{2,1,0:T(8,128)(2,1)}, bf16[97,128,128]{2,1,0:T(8,128)(2,1)}, u32[]{:S(2)}, u32[]{:S(2)}) collective-permute-start(bf16[97,128,128]{2,1,0:T(8,128)(2,1)} %tie.3.refs_0_), channel_id=1, source_target_pairs={{1,9},{3,11},{5,13},{7,15},{9,1},{11,3},{13,5},{15,7},{17,25},{19,... | collective-permute-start | bytes 9535496 | tf_op jit(solution)/shard_map/ppermute | solution.py:434
  45.0 5.1 %collective-permute-start.9 = (bf16[864,128]{1,0:T(8,128)(2,1)}, bf16[864,128]{1,0:T(8,128)(2,1)S(1)}, u32[]{:S(2)}, u32[]{:S(2)}) collective-permute-start(bf16[864,128]{1,0:T(8,128)(2,1)} %get-tuple-element.44), channel_id=1, source_target_pairs={{0,2},{1,17},{2,0},{3,19},{4,6},{5,21},{6,4},{7,23},{8,10},{9,25},... | collective-permute-start | bytes 663560 | tf_op jit(solution)/shard_map/ppermute | solution.py:434
  46.3 6.1 %collective-permute-start.10 = (bf16[864,128]{1,0:T(8,128)(2,1)}, bf16[864,128]{1,0:T(8,128)(2,1)S(1)}, u32[]{:S(2)}, u32[]{:S(2)}) collective-permute-start(bf16[864,128]{1,0:T(8,128)(2,1)} %get-tuple-element.45), channel_id=1, source_target_pairs={{0,4},{1,17},{2,6},{3,19},{4,0},{5,21},{6,2},{7,23},{8,12},{9,25},... | collective-permute-start | bytes 663560 | tf_op jit(solution)/shard_map/ppermute | solution.py:434
  46.5 8.6 %collective-permute-start.11 = (bf16[864,128]{1,0:T(8,128)(2,1)}, bf16[864,128]{1,0:T(8,128)(2,1)S(1)}, u32[]{:S(2)}, u32[]{:S(2)}) collective-permute-start(bf16[864,128]{1,0:T(8,128)(2,1)} %get-tuple-element.46), channel_id=1, source_target_pairs={{0,6},{1,17},{2,4},{3,19},{4,2},{5,21},{6,0},{7,23},{8,14},{9,25},... | collective-permute-start | bytes 663560 | tf_op jit(solution)/shard_map/ppermute | solution.py:434
  47.8 7.3 %copy-start.7 = (f32[1,2,32,2]{2,3,1,0:T(2,128)S(1)}, f32[1,2,32,2]{2,3,1,0:T(2,128)}, u32[]{:S(2)}) copy-start(f32[1,2,32,2]{2,3,1,0:T(2,128)} %param.12) | copy-start | bytes 1540
  48.5 23.6 %collective-permute-start.6 = (bf16[864,128]{1,0:T(8,128)(2,1)}, bf16[864,128]{1,0:T(8,128)(2,1)S(1)}, u32[]{:S(2)}, u32[]{:S(2)}) collective-permute-start(bf16[864,128]{1,0:T(8,128)(2,1)} %get-tuple-element.41), channel_id=1, source_target_pairs={{0,2},{1,17},{2,0},{3,19},{4,6},{5,21},{6,4},{7,23},{8,10},{9,25},... | collective-permute-start | bytes 663560 | tf_op jit(solution)/shard_map/ppermute | solution.py:434
  50.1 22.1 %collective-permute-start.7 = (bf16[864,128]{1,0:T(8,128)(2,1)}, bf16[864,128]{1,0:T(8,128)(2,1)S(1)}, u32[]{:S(2)}, u32[]{:S(2)}) collective-permute-start(bf16[864,128]{1,0:T(8,128)(2,1)} %get-tuple-element.42), channel_id=1, source_target_pairs={{0,4},{1,17},{2,6},{3,19},{4,0},{5,21},{6,2},{7,23},{8,12},{9,25},... | collective-permute-start | bytes 663560 | tf_op jit(solution)/shard_map/ppermute | solution.py:434
  52.4 26.1 %collective-permute-start.8 = (bf16[864,128]{1,0:T(8,128)(2,1)}, bf16[864,128]{1,0:T(8,128)(2,1)S(1)}, u32[]{:S(2)}, u32[]{:S(2)}) collective-permute-start(bf16[864,128]{1,0:T(8,128)(2,1)} %get-tuple-element.43), channel_id=1, source_target_pairs={{0,6},{1,17},{2,4},{3,19},{4,2},{5,21},{6,0},{7,23},{8,14},{9,25},... | collective-permute-start | bytes 663560 | tf_op jit(solution)/shard_map/ppermute | solution.py:434
  57.3 26.7 %collective-permute-start.16 = (bf16[864,128]{1,0:T(8,128)(2,1)S(1)}, bf16[864,128]{1,0:T(8,128)(2,1)S(1)}, u32[]{:S(2)}, u32[]{:S(2)}) collective-permute-start(bf16[864,128]{1,0:T(8,128)(2,1)S(1)} %get-tuple-element.54), channel_id=1, source_target_pairs={{0,3},{1,16},{2,1},{3,18},{4,7},{5,20},{6,5},{7,22},{8,11},{9,24},... | collective-permute-start | bytes 663560 | tf_op jit(solution)/shard_map/ppermute | solution.py:434
  72.1 12.0 %collective-permute-start.17 = (bf16[864,128]{1,0:T(8,128)(2,1)S(1)}, bf16[864,128]{1,0:T(8,128)(2,1)S(1)}, u32[]{:S(2)}, u32[]{:S(2)}) collective-permute-start(bf16[864,128]{1,0:T(8,128)(2,1)S(1)} %get-tuple-element.55), channel_id=1, source_target_pairs={{0,5},{1,16},{2,7},{3,18},{4,1},{5,20},{6,3},{7,22},{8,13},{9,24},... | collective-permute-start | bytes 663560 | tf_op jit(solution)/shard_map/ppermute | solution.py:434
  72.2 14.5 %collective-permute-start.18 = (bf16[864,128]{1,0:T(8,128)(2,1)S(1)}, bf16[864,128]{1,0:T(8,128)(2,1)S(1)}, u32[]{:S(2)}, u32[]{:S(2)}) collective-permute-start(bf16[864,128]{1,0:T(8,128)(2,1)S(1)} %get-tuple-element.56), channel_id=1, source_target_pairs={{0,7},{1,16},{2,5},{3,18},{4,3},{5,20},{6,1},{7,22},{8,15},{9,24},... | collective-permute-start | bytes 663560 | tf_op jit(solution)/shard_map/ppermute | solution.py:434
  74.9 11.8 %all-to-all-start.1 = ((bf16[2,2400,128]{2,1,0:T(8,128)(2,1)}), bf16[2,2400,128]{2,1,0:T(8,128)(2,1)S(1)}, u32[]{:S(2)}, u32[]{:S(2)}) async-start(bf16[2,2400,128]{2,1,0:T(8,128)(2,1)} %get-tuple-element.53), calls=%async_computation.1 | async-start | bytes 2457600 | tf_op jit(solution)/shard_map/all_to_all | solution.py:551
  81.1 16.7 %collective-permute-start.13 = (bf16[864,128]{1,0:T(8,128)(2,1)}, bf16[864,128]{1,0:T(8,128)(2,1)S(1)}, u32[]{:S(2)}, u32[]{:S(2)}) collective-permute-start(bf16[864,128]{1,0:T(8,128)(2,1)} %get-tuple-element.50), channel_id=1, source_target_pairs={{0,3},{1,16},{2,1},{3,18},{4,7},{5,20},{6,5},{7,22},{8,11},{9,24},... | collective-permute-start | bytes 663560 | tf_op jit(solution)/shard_map/ppermute | solution.py:434
  84.0 14.9 %collective-permute-start.14 = (bf16[864,128]{1,0:T(8,128)(2,1)}, bf16[864,128]{1,0:T(8,128)(2,1)S(1)}, u32[]{:S(2)}, u32[]{:S(2)}) collective-permute-start(bf16[864,128]{1,0:T(8,128)(2,1)} %get-tuple-element.51), channel_id=1, source_target_pairs={{0,5},{1,16},{2,7},{3,18},{4,1},{5,20},{6,3},{7,22},{8,13},{9,24},... | collective-permute-start | bytes 663560 | tf_op jit(solution)/shard_map/ppermute | solution.py:434
  84.1 15.6 %collective-permute-start.15 = (bf16[864,128]{1,0:T(8,128)(2,1)}, bf16[864,128]{1,0:T(8,128)(2,1)S(1)}, u32[]{:S(2)}, u32[]{:S(2)}) collective-permute-start(bf16[864,128]{1,0:T(8,128)(2,1)} %get-tuple-element.52), channel_id=1, source_target_pairs={{0,7},{1,16},{2,5},{3,18},{4,3},{5,20},{6,1},{7,22},{8,15},{9,24},... | collective-permute-start | bytes 663560 | tf_op jit(solution)/shard_map/ppermute | solution.py:434
  92.6 7.0 %collective-permute-start.19 = (bf16[864,128]{1,0:T(8,128)(2,1)}, bf16[864,128]{1,0:T(8,128)(2,1)}, u32[]{:S(2)}, u32[]{:S(2)}) collective-permute-start(bf16[864,128]{1,0:T(8,128)(2,1)} %get-tuple-element.57.rest_0_), channel_id=1, source_target_pairs={{0,1},{1,0},{2,3},{3,2},{4,5},{5,4},{6,7},{7,6},{8,9},{9,8},{10,11... | collective-permute-start | bytes 663560 | tf_op jit(solution)/shard_map/ppermute | solution.py:458
  92.7 15.1 %collective-permute-start.23 = (bf16[864,128]{1,0:T(8,128)(2,1)}, bf16[864,128]{1,0:T(8,128)(2,1)S(1)}, u32[]{:S(2)}, u32[]{:S(2)}) collective-permute-start(bf16[864,128]{1,0:T(8,128)(2,1)} %get-tuple-element.62), channel_id=1, source_target_pairs={{0,16},{1,3},{2,18},{3,1},{4,20},{5,7},{6,22},{7,5},{8,24},{9,11},... | collective-permute-start | bytes 663560 | tf_op jit(solution)/shard_map/ppermute | solution.py:434
  93.0 6.7 %all-to-all-start = ((bf16[2,2400,128]{2,1,0:T(8,128)(2,1)}), bf16[2,2400,128]{2,1,0:T(8,128)(2,1)S(1)}, u32[]{:S(2)}, u32[]{:S(2)}) async-start(bf16[2,2400,128]{2,1,0:T(8,128)(2,1)} %get-tuple-element.49), calls=%async_computation | async-start | bytes 2457600 | tf_op jit(solution)/shard_map/all_to_all | solution.py:551
  97.8 10.7 %collective-permute-start.24 = (bf16[864,128]{1,0:T(8,128)(2,1)}, bf16[864,128]{1,0:T(8,128)(2,1)}, u32[]{:S(2)}, u32[]{:S(2)}) collective-permute-start(bf16[864,128]{1,0:T(8,128)(2,1)} %get-tuple-element.63), channel_id=1, source_target_pairs={{0,16},{1,5},{2,18},{3,7},{4,20},{5,1},{6,22},{7,3},{8,24},{9,13},... | collective-permute-start | bytes 663560 | tf_op jit(solution)/shard_map/ppermute | solution.py:434
  98.9 11.2 %collective-permute-start.25 = (bf16[864,128]{1,0:T(8,128)(2,1)}, bf16[864,128]{1,0:T(8,128)(2,1)}, u32[]{:S(2)}, u32[]{:S(2)}) collective-permute-start(bf16[864,128]{1,0:T(8,128)(2,1)} %get-tuple-element.64), channel_id=1, source_target_pairs={{0,16},{1,7},{2,18},{3,5},{4,20},{5,3},{6,22},{7,1},{8,24},{9,15},... | collective-permute-start | bytes 663560 | tf_op jit(solution)/shard_map/ppermute | solution.py:434
  105.5 7.5 %collective-permute-start.20 = (bf16[864,128]{1,0:T(8,128)(2,1)}, bf16[864,128]{1,0:T(8,128)(2,1)S(1)}, u32[]{:S(2)}, u32[]{:S(2)}) collective-permute-start(bf16[864,128]{1,0:T(8,128)(2,1)} %get-tuple-element.59), channel_id=1, source_target_pairs={{0,16},{1,3},{2,18},{3,1},{4,20},{5,7},{6,22},{7,5},{8,24},{9,11},... | collective-permute-start | bytes 663560 | tf_op jit(solution)/shard_map/ppermute | solution.py:434
  107.3 9.1 %collective-permute-start.21 = (bf16[864,128]{1,0:T(8,128)(2,1)}, bf16[864,128]{1,0:T(8,128)(2,1)S(1)}, u32[]{:S(2)}, u32[]{:S(2)}) collective-permute-start(bf16[864,128]{1,0:T(8,128)(2,1)} %get-tuple-element.60), channel_id=1, source_target_pairs={{0,16},{1,5},{2,18},{3,7},{4,20},{5,1},{6,22},{7,3},{8,24},{9,13},... | collective-permute-start | bytes 663560 | tf_op jit(solution)/shard_map/ppermute | solution.py:434
  107.8 11.4 %collective-permute-start.22 = (bf16[864,128]{1,0:T(8,128)(2,1)}, bf16[864,128]{1,0:T(8,128)(2,1)S(1)}, u32[]{:S(2)}, u32[]{:S(2)}) collective-permute-start(bf16[864,128]{1,0:T(8,128)(2,1)} %get-tuple-element.61), channel_id=1, source_target_pairs={{0,16},{1,7},{2,18},{3,5},{4,20},{5,3},{6,22},{7,1},{8,24},{9,15},... | collective-permute-start | bytes 663560 | tf_op jit(solution)/shard_map/ppermute | solution.py:434
  (5 other events, 21.1 us)

commit v4 on v3

--- a/solution.py
+++ b/solution.py
@@ -155,9 +155,8 @@
 
 
 def relay_rows(micro, partners, capacity, group, info, tokens_ref, ids, weights, next_ids, next_gain, *rest):
-    returned, (state_out, carry), outs = rest[:partners], rest[-partners - 3 : -partners - 1], rest[-partners - 1 : -2]
-    given, arrived = rest[-2:]
-    carried = carry.at[1]
+    returned, (state_to, carry_to), outs = rest[:partners], rest[-partners - 7 : -partners - 5], rest[-partners - 5 : -6]
+    given, arrived, state_out, carried, made, left = rest[-6:]
     copy = pltpu.make_async_copy(tokens_ref.at[micro], given, arrived.at[0])
     copy.start()
     tokens, width = given.shape
@@ -182,9 +181,21 @@
             state_out[:, b * LANES : (b + 1) * LANES] = mixed[j * tokens : (j + 1) * tokens, :]
             total += square[j * tokens : (j + 1) * tokens, :]
     scale = lax.rsqrt(total * (1.0 / width) + EPS)
+    own = blocks * capacity
+    copies = [pltpu.make_async_copy(state_out, state_to, left.at[0])]
+    copies += [pltpu.make_async_copy(carried.at[pl.ds(own, state.shape[0])], carry_to.at[1, pl.ds(own, state.shape[0])], left.at[1])]
+    for copy in copies:
+        copy.start()
+    targets = [carried] + [made.at[k] for k in range(partners - 1)]
     send_rows(
-        next_ids[0, micro] ^ info[1], state, scale, lambda b: gain_of(next_gain, b), [carried, *outs], group, capacity, tokens
+        next_ids[0, micro] ^ info[1], state, scale, lambda b: gain_of(next_gain, b), targets, group, capacity, tokens
     )
+    sends = [pltpu.make_async_copy(made.at[k], outs[k], left.at[3 + k]) for k in range(partners - 1)]
+    sends += [pltpu.make_async_copy(carried.at[pl.ds(0, own)], carry_to.at[1, pl.ds(0, own)], left.at[2])]
+    for copy in sends:
+        copy.start()
+    for copy in copies + sends:
+        copy.wait()
 
 
 def last_kernel(micro, partners, capacity, group, info, first, carried, ids, weights, *rest):
@@ -537,11 +548,19 @@
         first, carry, *sent = call(
             functools.partial(relay_kernel, micro, partners, capacity, group),
             "relay",
-            [pltpu.HBM(state_shape.shape, bf16), carry_shape] + [rows_shape] * (partners - 1),
+            [pltpu.HBM(state_shape.shape, bf16), carry_shape] + [pltpu.HBM(rows_shape.shape, bf16)] * (partners - 1),
             (info, *held(tokens), ids, shares, next_ids, next_gain, *held(back[micro][0]), *back[micro][1:], *after),
             [SMEM, ANY] + [VMEM] * (4 + partners) + [ANY] * len(after),
-            [pltpu.VMEM((row_count, width), bf16), pltpu.SemaphoreType.DMA((1,))],
+            [
+                pltpu.VMEM((row_count, width), bf16),
+                pltpu.SemaphoreType.DMA((1,)),
+                pltpu.VMEM((row_count, width), bf16),
+                pltpu.VMEM(carry_shape.shape[1:], bf16),
+                pltpu.VMEM((partners - 1,) + rows_shape.shape, bf16),
+                pltpu.SemaphoreType.DMA((partners + 2,)),
+            ],
             12,
+            [ANY] * (partners + 1),
         )
         after = held(first)
         firsts.append(first)

time: 123 us -> 122 us (level)
  Pallas kernels: 27.9 us -> 25.3 us
  starting transfers between devices: 49.5 us -> 51.3 us
    pallas_call x9, Pallas kernels: 24.2 us -> 21.6 us  [call(): pl.pallas_call(kernel, out_shape=out_shape, in_specs=specs, out_specs=out...]
    ppermute x23, starting transfers between devices: 40 us -> 41.5 us  [trade(): return lax.ppermute(array, axes, pairs)]
  transfers between devices with their start and end apart: 28 -> 28, of which waited for: 9 -> 9; matrix products, arithmetic and copies ran while one was open for 0% -> 0% of each run, Pallas kernels for 18% -> 15%
where the time goes in v4:
time: 122 us
  starting transfers between devices  51.3 us (42%)
  waiting for transfers between devices  44.5 us (36%)
  Pallas kernels  25.3 us (21%)
    ppermute x23, waiting for transfers between devices, trade(): return lax.ppermute(array, axes, pairs)  42.6 us
    ppermute x23, starting transfers between devices, trade(): return lax.ppermute(array, axes, pairs)  41.5 us
    pallas_call x9, Pallas kernels, call(): pl.pallas_call(kernel, out_shape=out_shape, in_specs=specs, out_specs=out...  21.6 us
    all_to_all x2, starting transfers between devices, body(): lax.all_to_all(carry, 'section', split_axis=0, concat_axis=0, tiled=True)  8.69 us
    pallas_call x1, Pallas kernels, pack(): pl.pallas_call(pack_kernel, out_shape=pltpu.HBM(shape, jnp.bfloat16), in_...  3.73 us
  transfers between devices with their start and end apart: 28, of which 9 were waited for; matrix products, arithmetic and copies ran while one was open for 0% of the time, Pallas kernels for 15%

profile of v4, /device:TPU:9, one launch (start us, length us, event | category | flops | bytes accessed | tf_op | source)
XLA Modules:
  0.0 121.7 jit_solution(10737980009067877833)
XLA Ops:
  0.1 3.7 %pack.1.refs_0_ = bf16[97,128,128]{2,1,0:T(8,128)(2,1)} custom-call(s32[2]{0:T(128)S(1)} %pad_add_fusion.info, s32[1,32]{1,0:T(1,128)} %bitcast.28, s32[1,32]{1,0:T(1,128)} %bitcast.29, bf16[32,128,128]{2,1,0:T(8,128)(2,1)} %bitcast.25, bf16[32,128,128]{2,1,0:T(8,128)(2,1)} %bitcast.26, bf16[32,128,128]{2,1,0:T(8,128)(2,1)} %bitcast.27), custom_call_target="tpu_custom_call" | custom-call | tf_op jit(solution)/shard_map/pack/pallas_call | solution.py:388
  3.8 1.3 %collective-permute-start.2 = (bf16[97,128,128]{2,1,0:T(8,128)(2,1)}, bf16[97,128,128]{2,1,0:T(8,128)(2,1)}, u32[]{:S(2)}, u32[]{:S(2)}) collective-permute-start(bf16[97,128,128]{2,1,0:T(8,128)(2,1)} %pack.1.refs_0_), channel_id=1, source_target_pairs={{0,8},{1,17},{2,10},{3,19},{4,12},{5,21},{6,14},{7,23},{8,0},{9,25... | collective-permute-start | bytes 9535496 | tf_op jit(solution)/shard_map/ppermute | solution.py:445
  5.1 0.9 collective-permute-start.1
  6.1 1.1 collective-permute-done.rest_0_.refs_3_
  9.9 31.0 %collective-permute-done.2.refs_0_ = bf16[97,128,128]{2,1,0:T(8,128)(2,1)} collective-permute-done((bf16[97,128,128]{2,1,0:T(8,128)(2,1)}, bf16[97,128,128]{2,1,0:T(8,128)(2,1)}, u32[]{:S(2)}, u32[]{:S(2)}) %collective-permute-start.2) | collective-permute-done | bytes 3178528 | tf_op jit(solution)/shard_map/ppermute | solution.py:445
  41.0 3.2 %collective-permute-start.12 = (bf16[97,128,128]{2,1,0:T(8,128)(2,1)}, bf16[97,128,128]{2,1,0:T(8,128)(2,1)}, u32[]{:S(2)}, u32[]{:S(2)}) collective-permute-start(bf16[97,128,128]{2,1,0:T(8,128)(2,1)} %tie.3.refs_0_), channel_id=1, source_target_pairs={{1,9},{3,11},{5,13},{7,15},{9,1},{11,3},{13,5},{15,7},{17,25},{19,... | collective-permute-start | bytes 9535496 | tf_op jit(solution)/shard_map/ppermute | solution.py:445
  45.0 1.3 %collective-permute-start.9 = (bf16[864,128]{1,0:T(8,128)(2,1)}, bf16[864,128]{1,0:T(8,128)(2,1)S(1)}, u32[]{:S(2)}, u32[]{:S(2)}) collective-permute-start(bf16[864,128]{1,0:T(8,128)(2,1)} %get-tuple-element.44), channel_id=1, source_target_pairs={{0,2},{1,17},{2,0},{3,19},{4,6},{5,21},{6,4},{7,23},{8,10},{9,25},... | collective-permute-start | bytes 663560 | tf_op jit(solution)/shard_map/ppermute | solution.py:445
  46.5 1.2 %collective-permute-start.11 = (bf16[864,128]{1,0:T(8,128)(2,1)}, bf16[864,128]{1,0:T(8,128)(2,1)S(1)}, u32[]{:S(2)}, u32[]{:S(2)}) collective-permute-start(bf16[864,128]{1,0:T(8,128)(2,1)} %get-tuple-element.46), channel_id=1, source_target_pairs={{0,6},{1,17},{2,4},{3,19},{4,2},{5,21},{6,0},{7,23},{8,14},{9,25},... | collective-permute-start | bytes 663560 | tf_op jit(solution)/shard_map/ppermute | solution.py:445
  48.7 1.3 %collective-permute-done.9.refs_6_ = bf16[864,128]{1,0:T(8,128)(2,1)S(1)} collective-permute-done((bf16[864,128]{1,0:T(8,128)(2,1)}, bf16[864,128]{1,0:T(8,128)(2,1)S(1)}, u32[]{:S(2)}, u32[]{:S(2)}) %collective-permute-start.9) | collective-permute-done | bytes 221216 | tf_op jit(solution)/shard_map/ppermute | solution.py:445
  50.1 1.2 %collective-permute-start.7 = (bf16[864,128]{1,0:T(8,128)(2,1)}, bf16[864,128]{1,0:T(8,128)(2,1)S(1)}, u32[]{:S(2)}, u32[]{:S(2)}) collective-permute-start(bf16[864,128]{1,0:T(8,128)(2,1)} %get-tuple-element.42), channel_id=1, source_target_pairs={{0,4},{1,17},{2,6},{3,19},{4,0},{5,21},{6,2},{7,23},{8,12},{9,25},... | collective-permute-start | bytes 663560 | tf_op jit(solution)/shard_map/ppermute | solution.py:445
  51.3 1.1 collective-permute-done.10.refs_7_
  52.4 1.2 %collective-permute-start.8 = (bf16[864,128]{1,0:T(8,128)(2,1)}, bf16[864,128]{1,0:T(8,128)(2,1)S(1)}, u32[]{:S(2)}, u32[]{:S(2)}) collective-permute-start(bf16[864,128]{1,0:T(8,128)(2,1)} %get-tuple-element.43), channel_id=1, source_target_pairs={{0,6},{1,17},{2,4},{3,19},{4,2},{5,21},{6,0},{7,23},{8,14},{9,25},... | collective-permute-start | bytes 663560 | tf_op jit(solution)/shard_map/ppermute | solution.py:445
  53.7 1.4 %collective-permute-done.11.refs_8_ = bf16[864,128]{1,0:T(8,128)(2,1)S(1)} collective-permute-done((bf16[864,128]{1,0:T(8,128)(2,1)}, bf16[864,128]{1,0:T(8,128)(2,1)S(1)}, u32[]{:S(2)}, u32[]{:S(2)}) %collective-permute-start.11) | collective-permute-done | bytes 221216 | tf_op jit(solution)/shard_map/ppermute | solution.py:445
  55.1 1.0 relay.2
  56.1 15.7 %collective-permute-start.16 = (bf16[864,128]{1,0:T(8,128)(2,1)}, bf16[864,128]{1,0:T(8,128)(2,1)S(1)}, u32[]{:S(2)}, u32[]{:S(2)}) collective-permute-start(bf16[864,128]{1,0:T(8,128)(2,1)} %get-tuple-element.54), channel_id=1, source_target_pairs={{0,3},{1,16},{2,1},{3,18},{4,7},{5,20},{6,5},{7,22},{8,11},{9,24},... | collective-permute-start | bytes 663560 | tf_op jit(solution)/shard_map/ppermute | solution.py:445
  71.9 2.8 %collective-permute-start.18 = (bf16[864,128]{1,0:T(8,128)(2,1)}, bf16[864,128]{1,0:T(8,128)(2,1)S(1)}, u32[]{:S(2)}, u32[]{:S(2)}) collective-permute-start(bf16[864,128]{1,0:T(8,128)(2,1)} %get-tuple-element.56), channel_id=1, source_target_pairs={{0,7},{1,16},{2,5},{3,18},{4,3},{5,20},{6,1},{7,22},{8,15},{9,24},... | collective-permute-start | bytes 663560 | tf_op jit(solution)/shard_map/ppermute | solution.py:445
  74.7 3.6 %all-to-all-start.1 = ((bf16[2,2400,128]{2,1,0:T(8,128)(2,1)}), bf16[2,2400,128]{2,1,0:T(8,128)(2,1)S(1)}, u32[]{:S(2)}, u32[]{:S(2)}) async-start(bf16[2,2400,128]{2,1,0:T(8,128)(2,1)} %get-tuple-element.53), calls=%async_computation.1 | async-start | bytes 2457600 | tf_op jit(solution)/shard_map/all_to_all | solution.py:570
  78.3 1.2 relay.3
  79.5 3.8 %collective-permute-start.13 = (bf16[864,128]{1,0:T(8,128)(2,1)}, bf16[864,128]{1,0:T(8,128)(2,1)S(1)}, u32[]{:S(2)}, u32[]{:S(2)}) collective-permute-start(bf16[864,128]{1,0:T(8,128)(2,1)} %get-tuple-element.50), channel_id=1, source_target_pairs={{0,3},{1,16},{2,1},{3,18},{4,7},{5,20},{6,5},{7,22},{8,11},{9,24},... | collective-permute-start | bytes 663560 | tf_op jit(solution)/shard_map/ppermute | solution.py:445
  83.4 2.6 %collective-permute-start.15 = (bf16[864,128]{1,0:T(8,128)(2,1)}, bf16[864,128]{1,0:T(8,128)(2,1)S(1)}, u32[]{:S(2)}, u32[]{:S(2)}) collective-permute-start(bf16[864,128]{1,0:T(8,128)(2,1)} %get-tuple-element.52), channel_id=1, source_target_pairs={{0,7},{1,16},{2,5},{3,18},{4,3},{5,20},{6,1},{7,22},{8,15},{9,24},... | collective-permute-start | bytes 663560 | tf_op jit(solution)/shard_map/ppermute | solution.py:445
  86.0 5.9 %expert.6 = (bf16[864,128]{1,0:T(8,128)(2,1)}, bf16[864,128]{1,0:T(8,128)(2,1)}, bf16[864,128]{1,0:T(8,128)(2,1)}, bf16[864,128]{1,0:T(8,128)(2,1)}) custom-call(s32[2]{0:T(128)S(1)} %pad_add_fusion.info, bf16[97,128,128]{2,1,0:T(8,128)(2,1)} %tie.3.refs_0_, bf16[97,128,128]{2,1,0:T(8,128)(2,1)} %collective-permute-done.12.refs_1_, ...), custom_call_target="tpu_custom_call" | custom-call | tf_op jit(solution)/shard_map/expert/pallas_call | solution.py:482
  92.3 5.1 %all-to-all-start = ((bf16[2,2400,128]{2,1,0:T(8,128)(2,1)}), bf16[2,2400,128]{2,1,0:T(8,128)(2,1)S(1)}, u32[]{:S(2)}, u32[]{:S(2)}) async-start(bf16[2,2400,128]{2,1,0:T(8,128)(2,1)} %get-tuple-element.49), calls=%async_computation | async-start | bytes 2457600 | tf_op jit(solution)/shard_map/all_to_all | solution.py:570
  97.4 0.8 collective-permute-start.24
  98.4 0.8 all-to-all-done
  99.3 5.8 %expert.7 = (bf16[864,128]{1,0:T(8,128)(2,1)}, bf16[864,128]{1,0:T(8,128)(2,1)}, bf16[864,128]{1,0:T(8,128)(2,1)}, bf16[864,128]{1,0:T(8,128)(2,1)}) custom-call(s32[2]{0:T(128)S(1)} %pad_add_fusion.info, bf16[97,128,128]{2,1,0:T(8,128)(2,1)} %tie.3.refs_0_, bf16[97,128,128]{2,1,0:T(8,128)(2,1)} %collective-permute-done.12.refs_1_, ...), custom_call_target="tpu_custom_call" | custom-call | tf_op jit(solution)/shard_map/expert/pallas_call | solution.py:482
  105.1 1.8 %collective-permute-start.20 = (bf16[864,128]{1,0:T(8,128)(2,1)}, bf16[864,128]{1,0:T(8,128)(2,1)S(1)}, u32[]{:S(2)}, u32[]{:S(2)}) collective-permute-start(bf16[864,128]{1,0:T(8,128)(2,1)} %get-tuple-element.59), channel_id=1, source_target_pairs={{0,16},{1,3},{2,18},{3,1},{4,20},{5,7},{6,22},{7,5},{8,24},{9,11},... | collective-permute-start | bytes 663560 | tf_op jit(solution)/shard_map/ppermute | solution.py:445
  107.2 1.0 collective-permute-start.22
  108.1 1.2 collective-permute-done.25.rest_3_
  109.3 3.0 %last.2.rest_4_ = bf16[1,2,32,6144]{3,2,1,0:T(8,128)(2,1)} custom-call(s32[2]{0:T(128)S(1)} %pad_add_fusion.info, bf16[32,6144]{1,0:T(8,128)(2,1)} %get-tuple-element.47.refs_9_.first, bf16[4800,128]{1,0:T(8,128)(2,1)S(1)} %bitcast.12, s32[1,2,2,32]{3,2,1,0:T(2,128)S(1)} %bitcast.19, f32[1,2,2,32]{3,2,1,0:T(2,128)S(1)} %bitcast.23, ...), custom_call_target="tpu_custom_call" | custom-call | tf_op jit(solution)/shard_map/last/pallas_call | solution.py:482
  112.3 3.3 %collective-permute-done.21.rest_2_ = bf16[864,128]{1,0:T(8,128)(2,1)S(1)} collective-permute-done((bf16[864,128]{1,0:T(8,128)(2,1)}, bf16[864,128]{1,0:T(8,128)(2,1)S(1)}, u32[]{:S(2)}, u32[]{:S(2)}) %collective-permute-start.21) | collective-permute-done | bytes 221216 | tf_op jit(solution)/shard_map/ppermute | solution.py:445
  115.7 3.1 %collective-permute-done.22.rest_3_ = bf16[864,128]{1,0:T(8,128)(2,1)S(1)} collective-permute-done((bf16[864,128]{1,0:T(8,128)(2,1)}, bf16[864,128]{1,0:T(8,128)(2,1)S(1)}, u32[]{:S(2)}, u32[]{:S(2)}) %collective-permute-start.22) | collective-permute-done | bytes 221216 | tf_op jit(solution)/shard_map/ppermute | solution.py:445
  118.8 2.8 %last.3 = bf16[1,2,32,6144]{3,2,1,0:T(8,128)(2,1)} custom-call(s32[2]{0:T(128)S(1)} %pad_add_fusion.info, bf16[32,6144]{1,0:T(8,128)(2,1)} %get-tuple-element.48.refs_6_.first, bf16[4800,128]{1,0:T(8,128)(2,1)S(1)} %bitcast.14, s32[1,2,2,32]{3,2,1,0:T(2,128)S(1)} %bitcast.20, f32[1,2,2,32]{3,2,1,0:T(2,128)S(1)} %bitcast.24, ...), custom_call_target="tpu_custom_call", output_to_operand_aliasing={{}: (9, {})} | custom-call | tf_op jit(solution)/shard_map/last/pallas_call | solution.py:482
  (55 shorter events, 5.7 us)
Async XLA Ops:
  3.8 37.1 %collective-permute-start.2 = (bf16[97,128,128]{2,1,0:T(8,128)(2,1)}, bf16[97,128,128]{2,1,0:T(8,128)(2,1)}, u32[]{:S(2)}, u32[]{:S(2)}) collective-permute-start(bf16[97,128,128]{2,1,0:T(8,128)(2,1)} %pack.1.refs_0_), channel_id=1, source_target_pairs={{0,8},{1,17},{2,10},{3,19},{4,12},{5,21},{6,14},{7,23},{8,0},{9,25... | collective-permute-start | bytes 9535496 | tf_op jit(solution)/shard_map/ppermute | solution.py:445
  5.1 2.1 %collective-permute-start.1 = (f32[1,6144]{1,0:T(1,128)S(1)}, f32[1,6144]{1,0:T(1,128)S(1)}, u32[]{:S(2)}, u32[]{:S(2)}) collective-permute-start(f32[1,6144]{1,0:T(1,128)S(1)} %copy-done.8), channel_id=1, source_target_pairs={{0,1},{1,0},{2,3},{3,2},{4,5},{5,4},{6,7},{7,6},{8,9},{9,8},{10,11... | collective-permute-start | bytes 73736 | tf_op jit(solution)/shard_map/ppermute | solution.py:469
  6.1 1.2 collective-permute-start
  7.8 2.1 %collective-permute-start.3 = (bf16[1728,128]{1,0:T(8,128)(2,1)S(1)}, bf16[1728,128]{1,0:T(8,128)(2,1)S(1)}, u32[]{:S(2)}, u32[]{:S(2)}) collective-permute-start(bf16[1728,128]{1,0:T(8,128)(2,1)S(1)} %get-tuple-element.35), channel_id=1, source_target_pairs={{0,2},{2,0},{4,6},{6,4},{8,10},{10,8},{12,14},{14,12},{16,18},{18,... | collective-permute-start | bytes 1327112 | tf_op jit(solution)/shard_map/ppermute | solution.py:445
  8.5 1.4 %collective-permute-start.4 = (bf16[1728,128]{1,0:T(8,128)(2,1)S(1)}, bf16[1728,128]{1,0:T(8,128)(2,1)S(1)}, u32[]{:S(2)}, u32[]{:S(2)}) collective-permute-start(bf16[1728,128]{1,0:T(8,128)(2,1)S(1)} %get-tuple-element.36), channel_id=1, source_target_pairs={{0,4},{2,6},{4,0},{6,2},{8,12},{10,14},{12,8},{14,10},{16,20},{18,... | collective-permute-start | bytes 1327112 | tf_op jit(solution)/shard_map/ppermute | solution.py:445
  9.2 0.7 collective-permute-start.5
  9.9 31.1 %copy-start = (bf16[1728,128]{1,0:T(8,128)(2,1)}, bf16[1728,128]{1,0:T(8,128)(2,1)S(1)}, u32[]{:S(2)}) copy-start(bf16[1728,128]{1,0:T(8,128)(2,1)S(1)} %collective-permute-done.3.refs_1_.refs_3_) | copy-start | bytes 1327108
  9.9 31.1 %copy-start.2 = (bf16[1728,128]{1,0:T(8,128)(2,1)}, bf16[1728,128]{1,0:T(8,128)(2,1)S(1)}, u32[]{:S(2)}) copy-start(bf16[1728,128]{1,0:T(8,128)(2,1)S(1)} %collective-permute-done.4.refs_2_.refs_4_) | copy-start | bytes 1327108
  9.9 31.0 %copy-start.4 = (bf16[1728,128]{1,0:T(8,128)(2,1)}, bf16[1728,128]{1,0:T(8,128)(2,1)S(1)}, u32[]{:S(2)}) copy-start(bf16[1728,128]{1,0:T(8,128)(2,1)S(1)} %collective-permute-done.5.refs_3_.refs_5_) | copy-start | bytes 1327108
  41.0 45.0 %collective-permute-start.12 = (bf16[97,128,128]{2,1,0:T(8,128)(2,1)}, bf16[97,128,128]{2,1,0:T(8,128)(2,1)}, u32[]{:S(2)}, u32[]{:S(2)}) collective-permute-start(bf16[97,128,128]{2,1,0:T(8,128)(2,1)} %tie.3.refs_0_), channel_id=1, source_target_pairs={{1,9},{3,11},{5,13},{7,15},{9,1},{11,3},{13,5},{15,7},{17,25},{19,... | collective-permute-start | bytes 9535496 | tf_op jit(solution)/shard_map/ppermute | solution.py:445
  45.0 5.1 %collective-permute-start.9 = (bf16[864,128]{1,0:T(8,128)(2,1)}, bf16[864,128]{1,0:T(8,128)(2,1)S(1)}, u32[]{:S(2)}, u32[]{:S(2)}) collective-permute-start(bf16[864,128]{1,0:T(8,128)(2,1)} %get-tuple-element.44), channel_id=1, source_target_pairs={{0,2},{1,17},{2,0},{3,19},{4,6},{5,21},{6,4},{7,23},{8,10},{9,25},... | collective-permute-start | bytes 663560 | tf_op jit(solution)/shard_map/ppermute | solution.py:445
  46.3 6.1 %collective-permute-start.10 = (bf16[864,128]{1,0:T(8,128)(2,1)}, bf16[864,128]{1,0:T(8,128)(2,1)S(1)}, u32[]{:S(2)}, u32[]{:S(2)}) collective-permute-start(bf16[864,128]{1,0:T(8,128)(2,1)} %get-tuple-element.45), channel_id=1, source_target_pairs={{0,4},{1,17},{2,6},{3,19},{4,0},{5,21},{6,2},{7,23},{8,12},{9,25},... | collective-permute-start | bytes 663560 | tf_op jit(solution)/shard_map/ppermute | solution.py:445
  46.5 8.6 %collective-permute-start.11 = (bf16[864,128]{1,0:T(8,128)(2,1)}, bf16[864,128]{1,0:T(8,128)(2,1)S(1)}, u32[]{:S(2)}, u32[]{:S(2)}) collective-permute-start(bf16[864,128]{1,0:T(8,128)(2,1)} %get-tuple-element.46), channel_id=1, source_target_pairs={{0,6},{1,17},{2,4},{3,19},{4,2},{5,21},{6,0},{7,23},{8,14},{9,25},... | collective-permute-start | bytes 663560 | tf_op jit(solution)/shard_map/ppermute | solution.py:445
  47.8 7.3 %copy-start.7 = (f32[1,2,32,2]{2,3,1,0:T(2,128)S(1)}, f32[1,2,32,2]{2,3,1,0:T(2,128)}, u32[]{:S(2)}) copy-start(f32[1,2,32,2]{2,3,1,0:T(2,128)} %param.12) | copy-start | bytes 1540
  48.5 23.4 %collective-permute-start.6 = (bf16[864,128]{1,0:T(8,128)(2,1)}, bf16[864,128]{1,0:T(8,128)(2,1)S(1)}, u32[]{:S(2)}, u32[]{:S(2)}) collective-permute-start(bf16[864,128]{1,0:T(8,128)(2,1)} %get-tuple-element.41), channel_id=1, source_target_pairs={{0,2},{1,17},{2,0},{3,19},{4,6},{5,21},{6,4},{7,23},{8,10},{9,25},... | collective-permute-start | bytes 663560 | tf_op jit(solution)/shard_map/ppermute | solution.py:445
  50.1 21.8 %collective-permute-start.7 = (bf16[864,128]{1,0:T(8,128)(2,1)}, bf16[864,128]{1,0:T(8,128)(2,1)S(1)}, u32[]{:S(2)}, u32[]{:S(2)}) collective-permute-start(bf16[864,128]{1,0:T(8,128)(2,1)} %get-tuple-element.42), channel_id=1, source_target_pairs={{0,4},{1,17},{2,6},{3,19},{4,0},{5,21},{6,2},{7,23},{8,12},{9,25},... | collective-permute-start | bytes 663560 | tf_op jit(solution)/shard_map/ppermute | solution.py:445
  52.4 25.9 %collective-permute-start.8 = (bf16[864,128]{1,0:T(8,128)(2,1)}, bf16[864,128]{1,0:T(8,128)(2,1)S(1)}, u32[]{:S(2)}, u32[]{:S(2)}) collective-permute-start(bf16[864,128]{1,0:T(8,128)(2,1)} %get-tuple-element.43), channel_id=1, source_target_pairs={{0,6},{1,17},{2,4},{3,19},{4,2},{5,21},{6,0},{7,23},{8,14},{9,25},... | collective-permute-start | bytes 663560 | tf_op jit(solution)/shard_map/ppermute | solution.py:445
  56.1 27.2 %collective-permute-start.16 = (bf16[864,128]{1,0:T(8,128)(2,1)}, bf16[864,128]{1,0:T(8,128)(2,1)S(1)}, u32[]{:S(2)}, u32[]{:S(2)}) collective-permute-start(bf16[864,128]{1,0:T(8,128)(2,1)} %get-tuple-element.54), channel_id=1, source_target_pairs={{0,3},{1,16},{2,1},{3,18},{4,7},{5,20},{6,5},{7,22},{8,11},{9,24},... | collective-permute-start | bytes 663560 | tf_op jit(solution)/shard_map/ppermute | solution.py:445
  71.8 11.6 %collective-permute-start.17 = (bf16[864,128]{1,0:T(8,128)(2,1)}, bf16[864,128]{1,0:T(8,128)(2,1)S(1)}, u32[]{:S(2)}, u32[]{:S(2)}) collective-permute-start(bf16[864,128]{1,0:T(8,128)(2,1)} %get-tuple-element.55), channel_id=1, source_target_pairs={{0,5},{1,16},{2,7},{3,18},{4,1},{5,20},{6,3},{7,22},{8,13},{9,24},... | collective-permute-start | bytes 663560 | tf_op jit(solution)/shard_map/ppermute | solution.py:445
  71.9 14.1 %collective-permute-start.18 = (bf16[864,128]{1,0:T(8,128)(2,1)}, bf16[864,128]{1,0:T(8,128)(2,1)S(1)}, u32[]{:S(2)}, u32[]{:S(2)}) collective-permute-start(bf16[864,128]{1,0:T(8,128)(2,1)} %get-tuple-element.56), channel_id=1, source_target_pairs={{0,7},{1,16},{2,5},{3,18},{4,3},{5,20},{6,1},{7,22},{8,15},{9,24},... | collective-permute-start | bytes 663560 | tf_op jit(solution)/shard_map/ppermute | solution.py:445
  74.7 11.3 %all-to-all-start.1 = ((bf16[2,2400,128]{2,1,0:T(8,128)(2,1)}), bf16[2,2400,128]{2,1,0:T(8,128)(2,1)S(1)}, u32[]{:S(2)}, u32[]{:S(2)}) async-start(bf16[2,2400,128]{2,1,0:T(8,128)(2,1)} %get-tuple-element.53), calls=%async_computation.1 | async-start | bytes 2457600 | tf_op jit(solution)/shard_map/all_to_all | solution.py:570
  79.5 17.9 %collective-permute-start.13 = (bf16[864,128]{1,0:T(8,128)(2,1)}, bf16[864,128]{1,0:T(8,128)(2,1)S(1)}, u32[]{:S(2)}, u32[]{:S(2)}) collective-permute-start(bf16[864,128]{1,0:T(8,128)(2,1)} %get-tuple-element.50), channel_id=1, source_target_pairs={{0,3},{1,16},{2,1},{3,18},{4,7},{5,20},{6,5},{7,22},{8,11},{9,24},... | collective-permute-start | bytes 663560 | tf_op jit(solution)/shard_map/ppermute | solution.py:445
  83.3 14.9 %collective-permute-start.14 = (bf16[864,128]{1,0:T(8,128)(2,1)}, bf16[864,128]{1,0:T(8,128)(2,1)S(1)}, u32[]{:S(2)}, u32[]{:S(2)}) collective-permute-start(bf16[864,128]{1,0:T(8,128)(2,1)} %get-tuple-element.51), channel_id=1, source_target_pairs={{0,5},{1,16},{2,7},{3,18},{4,1},{5,20},{6,3},{7,22},{8,13},{9,24},... | collective-permute-start | bytes 663560 | tf_op jit(solution)/shard_map/ppermute | solution.py:445
  83.4 15.9 %collective-permute-start.15 = (bf16[864,128]{1,0:T(8,128)(2,1)}, bf16[864,128]{1,0:T(8,128)(2,1)S(1)}, u32[]{:S(2)}, u32[]{:S(2)}) collective-permute-start(bf16[864,128]{1,0:T(8,128)(2,1)} %get-tuple-element.52), channel_id=1, source_target_pairs={{0,7},{1,16},{2,5},{3,18},{4,3},{5,20},{6,1},{7,22},{8,15},{9,24},... | collective-permute-start | bytes 663560 | tf_op jit(solution)/shard_map/ppermute | solution.py:445
  91.9 7.3 %collective-permute-start.19 = (bf16[864,128]{1,0:T(8,128)(2,1)}, bf16[864,128]{1,0:T(8,128)(2,1)}, u32[]{:S(2)}, u32[]{:S(2)}) collective-permute-start(bf16[864,128]{1,0:T(8,128)(2,1)} %get-tuple-element.57.rest_0_), channel_id=1, source_target_pairs={{0,1},{1,0},{2,3},{3,2},{4,5},{5,4},{6,7},{7,6},{8,9},{9,8},{10,11... | collective-permute-start | bytes 663560 | tf_op jit(solution)/shard_map/ppermute | solution.py:469
  92.0 15.2 %collective-permute-start.23 = (bf16[864,128]{1,0:T(8,128)(2,1)}, bf16[864,128]{1,0:T(8,128)(2,1)S(1)}, u32[]{:S(2)}, u32[]{:S(2)}) collective-permute-start(bf16[864,128]{1,0:T(8,128)(2,1)} %get-tuple-element.62), channel_id=1, source_target_pairs={{0,16},{1,3},{2,18},{3,1},{4,20},{5,7},{6,22},{7,5},{8,24},{9,11},... | collective-permute-start | bytes 663560 | tf_op jit(solution)/shard_map/ppermute | solution.py:445
  92.3 7.0 %all-to-all-start = ((bf16[2,2400,128]{2,1,0:T(8,128)(2,1)}), bf16[2,2400,128]{2,1,0:T(8,128)(2,1)S(1)}, u32[]{:S(2)}, u32[]{:S(2)}) async-start(bf16[2,2400,128]{2,1,0:T(8,128)(2,1)} %get-tuple-element.49), calls=%async_computation | async-start | bytes 2457600 | tf_op jit(solution)/shard_map/all_to_all | solution.py:570
  97.4 10.7 %collective-permute-start.24 = (bf16[864,128]{1,0:T(8,128)(2,1)}, bf16[864,128]{1,0:T(8,128)(2,1)}, u32[]{:S(2)}, u32[]{:S(2)}) collective-permute-start(bf16[864,128]{1,0:T(8,128)(2,1)} %get-tuple-element.63), channel_id=1, source_target_pairs={{0,16},{1,5},{2,18},{3,7},{4,20},{5,1},{6,22},{7,3},{8,24},{9,13},... | collective-permute-start | bytes 663560 | tf_op jit(solution)/shard_map/ppermute | solution.py:445
  98.2 11.1 %collective-permute-start.25 = (bf16[864,128]{1,0:T(8,128)(2,1)}, bf16[864,128]{1,0:T(8,128)(2,1)}, u32[]{:S(2)}, u32[]{:S(2)}) collective-permute-start(bf16[864,128]{1,0:T(8,128)(2,1)} %get-tuple-element.64), channel_id=1, source_target_pairs={{0,16},{1,7},{2,18},{3,5},{4,20},{5,3},{6,22},{7,1},{8,24},{9,15},... | collective-permute-start | bytes 663560 | tf_op jit(solution)/shard_map/ppermute | solution.py:445
  105.1 7.2 %collective-permute-start.20 = (bf16[864,128]{1,0:T(8,128)(2,1)}, bf16[864,128]{1,0:T(8,128)(2,1)S(1)}, u32[]{:S(2)}, u32[]{:S(2)}) collective-permute-start(bf16[864,128]{1,0:T(8,128)(2,1)} %get-tuple-element.59), channel_id=1, source_target_pairs={{0,16},{1,3},{2,18},{3,1},{4,20},{5,7},{6,22},{7,5},{8,24},{9,11},... | collective-permute-start | bytes 663560 | tf_op jit(solution)/shard_map/ppermute | solution.py:445
  106.9 8.8 %collective-permute-start.21 = (bf16[864,128]{1,0:T(8,128)(2,1)}, bf16[864,128]{1,0:T(8,128)(2,1)S(1)}, u32[]{:S(2)}, u32[]{:S(2)}) collective-permute-start(bf16[864,128]{1,0:T(8,128)(2,1)} %get-tuple-element.60), channel_id=1, source_target_pairs={{0,16},{1,5},{2,18},{3,7},{4,20},{5,1},{6,22},{7,3},{8,24},{9,13},... | collective-permute-start | bytes 663560 | tf_op jit(solution)/shard_map/ppermute | solution.py:445
  107.2 11.7 %collective-permute-start.22 = (bf16[864,128]{1,0:T(8,128)(2,1)}, bf16[864,128]{1,0:T(8,128)(2,1)S(1)}, u32[]{:S(2)}, u32[]{:S(2)}) collective-permute-start(bf16[864,128]{1,0:T(8,128)(2,1)} %get-tuple-element.61), channel_id=1, source_target_pairs={{0,16},{1,7},{2,18},{3,5},{4,20},{5,3},{6,22},{7,1},{8,24},{9,15},... | collective-permute-start | bytes 663560 | tf_op jit(solution)/shard_map/ppermute | solution.py:445
  (5 other events, 21.1 us)

commit v5 on v4

--- a/solution.py
+++ b/solution.py
@@ -155,8 +155,9 @@
 
 
 def relay_rows(micro, partners, capacity, group, info, tokens_ref, ids, weights, next_ids, next_gain, *rest):
-    returned, (state_to, carry_to), outs = rest[:partners], rest[-partners - 7 : -partners - 5], rest[-partners - 5 : -6]
+    returned, outs, (state_to, *carry_to) = rest[:partners], rest[-partners - 5 : -6], rest[-partners - 8 : -partners - 5]
     given, arrived, state_out, carried, made, left = rest[-6:]
+    own_to, kept_to = carry_to
     copy = pltpu.make_async_copy(tokens_ref.at[micro], given, arrived.at[0])
     copy.start()
     tokens, width = given.shape
@@ -183,7 +184,7 @@
     scale = lax.rsqrt(total * (1.0 / width) + EPS)
     own = blocks * capacity
     copies = [pltpu.make_async_copy(state_out, state_to, left.at[0])]
-    copies += [pltpu.make_async_copy(carried.at[pl.ds(own, state.shape[0])], carry_to.at[1, pl.ds(own, state.shape[0])], left.at[1])]
+    copies += [pltpu.make_async_copy(carried.at[pl.ds(own, state.shape[0])], kept_to, left.at[1])]
     for copy in copies:
         copy.start()
     targets = [carried] + [made.at[k] for k in range(partners - 1)]
@@ -191,7 +192,7 @@
         next_ids[0, micro] ^ info[1], state, scale, lambda b: gain_of(next_gain, b), targets, group, capacity, tokens
     )
     sends = [pltpu.make_async_copy(made.at[k], outs[k], left.at[3 + k]) for k in range(partners - 1)]
-    sends += [pltpu.make_async_copy(carried.at[pl.ds(0, own)], carry_to.at[1, pl.ds(0, own)], left.at[2])]
+    sends += [pltpu.make_async_copy(carried.at[pl.ds(0, own)], own_to, left.at[2])]
     for copy in sends:
         copy.start()
     for copy in copies + sends:
@@ -216,8 +217,7 @@
         shares = spread_columns(weights[0, micro], group * tokens)
 
         def base_of(number):
-            start = blocks * capacity + number * group * tokens
-            return carried[start : start + group * tokens, :]
+            return carried[number * group * tokens : (number + 1) * group * tokens, :]
 
         for number, mixed in mix_rows(picks, base_of, shares, returned, blocks, group, capacity, tokens):
             for j in range(group):
@@ -427,7 +427,8 @@
     padded = up_to(capacity, 8)
     bf16, f32 = jnp.bfloat16, jnp.float32
     rows_shape = jax.ShapeDtypeStruct((size, LANES), bf16)
-    carry_shape = pltpu.HBM((sections, size + blocks * row_count, LANES), bf16)
+    carry_rows = size + blocks * row_count
+    carry_shapes = [pltpu.HBM((size, LANES), bf16), pltpu.HBM((carry_rows - size, LANES), bf16)]
     state_shape = jax.ShapeDtypeStruct((row_count, width), bf16)
     info = jnp.stack([lax.axis_index(a) for a in ("section", "expert")]).astype(jnp.int32)
     weights = [a.reshape(a.shape[2:3] + a.shape[4:]) for a in (gate_blocks, up_blocks, down_blocks)]
@@ -545,36 +546,36 @@
         back.append(exchange(done, to_partner, always(idle)))
     firsts, carries, given_rows = [], [], []
     for micro in range(micro_count):
-        first, carry, *sent = call(
+        first, *sent = call(
             functools.partial(relay_kernel, micro, partners, capacity, group),
             "relay",
-            [pltpu.HBM(state_shape.shape, bf16), carry_shape] + [pltpu.HBM(rows_shape.shape, bf16)] * (partners - 1),
+            [pltpu.HBM(state_shape.shape, bf16), *carry_shapes] + [pltpu.HBM(rows_shape.shape, bf16)] * (partners - 1),
             (info, *held(tokens), ids, shares, next_ids, next_gain, *held(back[micro][0]), *back[micro][1:], *after),
             [SMEM, ANY] + [VMEM] * (4 + partners) + [ANY] * len(after),
             [
                 pltpu.VMEM((row_count, width), bf16),
                 pltpu.SemaphoreType.DMA((1,)),
                 pltpu.VMEM((row_count, width), bf16),
-                pltpu.VMEM(carry_shape.shape[1:], bf16),
+                pltpu.VMEM((carry_rows, LANES), bf16),
                 pltpu.VMEM((partners - 1,) + rows_shape.shape, bf16),
                 pltpu.SemaphoreType.DMA((partners + 2,)),
             ],
             12,
-            [ANY] * (partners + 1),
+            [ANY] * (partners + 2),
         )
         after = held(first)
         firsts.append(first)
-        carries.append(carry)
-        given_rows.append(exchange([carry] + sent, to_next, always(idle_back)))
-    carries = [
-        lax.all_to_all(carry, "section", split_axis=0, concat_axis=0, tiled=True).reshape(-1, LANES) for carry in carries
-    ]
-    given_rows = [[carry] + parts[1:] for carry, parts in zip(carries, given_rows)]
+        carries.append(sent[: 1 - partners])
+        given_rows.append(exchange([None] + sent[1 - partners :], to_next, always(idle_back)))
+    carries[0][0] = swap(carries[0][0])
     after = held(first)
     back = []
     for micro in range(micro_count):
-        done = expert(1, sources[1], given_rows[micro], [0] * partners, after)
-        after = [swap(done[0])]
+        if micro:
+            carries[micro][0] = swap(tie(carries[micro][0], done[0]))
+        done = expert(1, sources[1], [carries[micro][0]] + given_rows[micro][1:], [0] * partners, after)
+        after = []
+        carries[micro][1] = swap(tie(carries[micro][1], done[0]))
         back.append(exchange(done, always(idle), to_partner))
     out = None
     for micro in range(micro_count):
@@ -586,7 +587,7 @@
             (
                 info,
                 *held(firsts[micro]),
-                carries[micro],
+                carries[micro][1],
                 ids,
                 shares,
                 *held(back[micro][0]),

time: 122 us -> 120 us (0.984)
  starting transfers between devices: 51.3 us -> 47.4 us
  local copies, waits for them, and re-layouts: 0.04 us -> 1.69 us
    ppermute x3 -> x6, starting transfers between devices: 1.08 us -> 14.9 us  [swap(): return lax.ppermute(array, 'section', [(0, 1), (1, 0)])]
    ppermute x23, starting transfers between devices: 41.5 us -> 32.5 us  [trade(): return lax.ppermute(array, axes, pairs)]
    all_to_all x2 -> x0, starting transfers between devices: 8.69 us -> none  [body(): lax.all_to_all(carry, 'section', split_axis=0, concat_axis=0, tiled=True)]
    unnamed x18 -> x20, local copies, waits for them, and re-layouts: 0.04 us -> 1.69 us
  transfers between devices with their start and end apart: 28 -> 29, of which waited for: 9 -> 10; matrix products, arithmetic and copies ran while one was open for 0% -> 0% of each run, Pallas kernels for 15% -> 16%
where the time goes in v5:
time: 120 us; the launch traced here: 119 us
  starting transfers between devices  47.4 us (40%)
  waiting for transfers between devices  44.6 us (37%)
  Pallas kernels  25.1 us (21%)
  local copies, waits for them, and re-layouts  1.69 us (1%)
    ppermute x23, waiting for transfers between devices, trade(): return lax.ppermute(array, axes, pairs)  43.5 us
    ppermute x23, starting transfers between devices, trade(): return lax.ppermute(array, axes, pairs)  32.5 us
    pallas_call x9, Pallas kernels, call(): pl.pallas_call(kernel, out_shape=out_shape, in_specs=specs, out_specs=out...  21.4 us
    ppermute x6, starting transfers between devices, swap(): return lax.ppermute(array, 'section', [(0, 1), (1, 0)])  14.9 us
    pallas_call x1, Pallas kernels, pack(): pl.pallas_call(pack_kernel, out_shape=pltpu.HBM(shape, jnp.bfloat16), in_...  3.73 us
  transfers between devices with their start and end apart: 29, of which 10 were waited for; matrix products, arithmetic and copies ran while one was open for 0% of the time, Pallas kernels for 16%

profile of v5, /device:TPU:9, one launch (start us, length us, event | category | flops | bytes accessed | tf_op | source)
XLA Modules:
  0.0 119.4 jit_solution(7768740997890852174)
XLA Ops:
  0.1 3.7 %pack.1.refs_0_ = bf16[97,128,128]{2,1,0:T(8,128)(2,1)} custom-call(s32[2]{0:T(128)S(1)} %pad_add_fusion.info, s32[1,32]{1,0:T(1,128)} %bitcast.22, s32[1,32]{1,0:T(1,128)} %bitcast.23, bf16[32,128,128]{2,1,0:T(8,128)(2,1)} %bitcast.19, bf16[32,128,128]{2,1,0:T(8,128)(2,1)} %bitcast.20, bf16[32,128,128]{2,1,0:T(8,128)(2,1)} %bitcast.21), custom_call_target="tpu_custom_call" | custom-call | tf_op jit(solution)/shard_map/pack/pallas_call | solution.py:388
  3.8 1.3 %collective-permute-start.2 = (bf16[97,128,128]{2,1,0:T(8,128)(2,1)}, bf16[97,128,128]{2,1,0:T(8,128)(2,1)}, u32[]{:S(2)}, u32[]{:S(2)}) collective-permute-start(bf16[97,128,128]{2,1,0:T(8,128)(2,1)} %pack.1.refs_0_), channel_id=1, source_target_pairs={{0,8},{1,17},{2,10},{3,19},{4,12},{5,21},{6,14},{7,23},{8,0},{9,25... | collective-permute-start | bytes 9535496 | tf_op jit(solution)/shard_map/ppermute | solution.py:446
  5.1 0.9 collective-permute-start.1
  6.1 1.1 collective-permute-done.rest_0_.refs_3_
  9.9 31.0 %collective-permute-done.2.refs_0_ = bf16[97,128,128]{2,1,0:T(8,128)(2,1)} collective-permute-done((bf16[97,128,128]{2,1,0:T(8,128)(2,1)}, bf16[97,128,128]{2,1,0:T(8,128)(2,1)}, u32[]{:S(2)}, u32[]{:S(2)}) %collective-permute-start.2) | collective-permute-done | bytes 3178528 | tf_op jit(solution)/shard_map/ppermute | solution.py:446
  41.0 3.2 %collective-permute-start.12 = (bf16[97,128,128]{2,1,0:T(8,128)(2,1)}, bf16[97,128,128]{2,1,0:T(8,128)(2,1)S(1)}, u32[]{:S(2)}, u32[]{:S(2)}) collective-permute-start(bf16[97,128,128]{2,1,0:T(8,128)(2,1)} %tie.6.refs_0_), channel_id=1, source_target_pairs={{1,9},{3,11},{5,13},{7,15},{9,1},{11,3},{13,5},{15,7},{17,25},{19,... | collective-permute-start | bytes 9535496 | tf_op jit(solution)/shard_map/ppermute | solution.py:446
  45.0 1.3 %collective-permute-start.9 = (bf16[864,128]{1,0:T(8,128)(2,1)}, bf16[864,128]{1,0:T(8,128)(2,1)S(1)}, u32[]{:S(2)}, u32[]{:S(2)}) collective-permute-start(bf16[864,128]{1,0:T(8,128)(2,1)} %get-tuple-element.46), channel_id=1, source_target_pairs={{0,2},{1,17},{2,0},{3,19},{4,6},{5,21},{6,4},{7,23},{8,10},{9,25},... | collective-permute-start | bytes 663560 | tf_op jit(solution)/shard_map/ppermute | solution.py:446
  46.5 1.2 %collective-permute-start.11 = (bf16[864,128]{1,0:T(8,128)(2,1)}, bf16[864,128]{1,0:T(8,128)(2,1)S(1)}, u32[]{:S(2)}, u32[]{:S(2)}) collective-permute-start(bf16[864,128]{1,0:T(8,128)(2,1)} %get-tuple-element.48), channel_id=1, source_target_pairs={{0,6},{1,17},{2,4},{3,19},{4,2},{5,21},{6,0},{7,23},{8,14},{9,25},... | collective-permute-start | bytes 663560 | tf_op jit(solution)/shard_map/ppermute | solution.py:446
  48.7 1.3 %collective-permute-done.9.refs_6_ = bf16[864,128]{1,0:T(8,128)(2,1)S(1)} collective-permute-done((bf16[864,128]{1,0:T(8,128)(2,1)}, bf16[864,128]{1,0:T(8,128)(2,1)S(1)}, u32[]{:S(2)}, u32[]{:S(2)}) %collective-permute-start.9) | collective-permute-done | bytes 221216 | tf_op jit(solution)/shard_map/ppermute | solution.py:446
  50.1 1.2 %collective-permute-start.7 = (bf16[864,128]{1,0:T(8,128)(2,1)}, bf16[864,128]{1,0:T(8,128)(2,1)S(1)}, u32[]{:S(2)}, u32[]{:S(2)}) collective-permute-start(bf16[864,128]{1,0:T(8,128)(2,1)} %get-tuple-element.44), channel_id=1, source_target_pairs={{0,4},{1,17},{2,6},{3,19},{4,0},{5,21},{6,2},{7,23},{8,12},{9,25},... | collective-permute-start | bytes 663560 | tf_op jit(solution)/shard_map/ppermute | solution.py:446
  51.3 1.1 collective-permute-done.10.refs_7_
  52.4 1.2 %collective-permute-start.8 = (bf16[864,128]{1,0:T(8,128)(2,1)}, bf16[864,128]{1,0:T(8,128)(2,1)S(1)}, u32[]{:S(2)}, u32[]{:S(2)}) collective-permute-start(bf16[864,128]{1,0:T(8,128)(2,1)} %get-tuple-element.45), channel_id=1, source_target_pairs={{0,6},{1,17},{2,4},{3,19},{4,2},{5,21},{6,0},{7,23},{8,14},{9,25},... | collective-permute-start | bytes 663560 | tf_op jit(solution)/shard_map/ppermute | solution.py:446
  53.7 1.4 %collective-permute-done.11.refs_8_ = bf16[864,128]{1,0:T(8,128)(2,1)S(1)} collective-permute-done((bf16[864,128]{1,0:T(8,128)(2,1)}, bf16[864,128]{1,0:T(8,128)(2,1)S(1)}, u32[]{:S(2)}, u32[]{:S(2)}) %collective-permute-start.11) | collective-permute-done | bytes 221216 | tf_op jit(solution)/shard_map/ppermute | solution.py:446
  55.1 1.0 relay.2
  56.1 13.4 %collective-permute-start.13 = (bf16[864,128]{1,0:T(8,128)(2,1)}, bf16[864,128]{1,0:T(8,128)(2,1)S(1)}, u32[]{:S(2)}, u32[]{:S(2)}) collective-permute-start(bf16[864,128]{1,0:T(8,128)(2,1)} %get-tuple-element.53), channel_id=1, source_target_pairs={{0,1},{1,0},{2,3},{3,2},{4,5},{5,4},{6,7},{7,6},{8,9},{9,8},{10,11... | collective-permute-start | bytes 663560 | tf_op jit(solution)/shard_map/ppermute | solution.py:470
  69.6 1.2 %collective-permute-start.14 = (bf16[864,128]{1,0:T(8,128)(2,1)}, bf16[864,128]{1,0:T(8,128)(2,1)S(1)}, u32[]{:S(2)}, u32[]{:S(2)}) collective-permute-start(bf16[864,128]{1,0:T(8,128)(2,1)} %get-tuple-element.54), channel_id=1, source_target_pairs={{0,3},{1,16},{2,1},{3,18},{4,7},{5,20},{6,5},{7,22},{8,11},{9,24},... | collective-permute-start | bytes 663560 | tf_op jit(solution)/shard_map/ppermute | solution.py:446
  70.8 1.7 %collective-permute-start.15 = (bf16[864,128]{1,0:T(8,128)(2,1)}, bf16[864,128]{1,0:T(8,128)(2,1)S(1)}, u32[]{:S(2)}, u32[]{:S(2)}) collective-permute-start(bf16[864,128]{1,0:T(8,128)(2,1)} %get-tuple-element.55), channel_id=1, source_target_pairs={{0,5},{1,16},{2,7},{3,18},{4,1},{5,20},{6,3},{7,22},{8,13},{9,24},... | collective-permute-start | bytes 663560 | tf_op jit(solution)/shard_map/ppermute | solution.py:446
  72.5 3.2 %collective-permute-start.16 = (bf16[864,128]{1,0:T(8,128)(2,1)}, bf16[864,128]{1,0:T(8,128)(2,1)S(1)}, u32[]{:S(2)}, u32[]{:S(2)}) collective-permute-start(bf16[864,128]{1,0:T(8,128)(2,1)} %get-tuple-element.56), channel_id=1, source_target_pairs={{0,7},{1,16},{2,5},{3,18},{4,3},{5,20},{6,1},{7,22},{8,15},{9,24},... | collective-permute-start | bytes 663560 | tf_op jit(solution)/shard_map/ppermute | solution.py:446
  75.7 1.2 %relay.3 = (bf16[32,6144]{1,0:T(8,128)(2,1)}, bf16[864,128]{1,0:T(8,128)(2,1)}, bf16[1536,128]{1,0:T(8,128)(2,1)}, bf16[864,128]{1,0:T(8,128)(2,1)}, bf16[864,128]{1,0:T(8,128)(2,1)}, /*index=5*/bf16[864,128]{1,0:T(8,128)(2,1)}) custom-call(s32[2]{0:T(128)S(1)} %pad_add_fusion.info, bf16[2,32,6144]{2,1,0:T(8,128)(2,1)} %refs_0_.3, ...), custom_call_target="tpu_custom_call" | custom-call | tf_op jit(solution)/shard_map/relay/pallas_call | solution.py:483
  76.9 3.8 %collective-permute-start.18 = (bf16[864,128]{1,0:T(8,128)(2,1)}, bf16[864,128]{1,0:T(8,128)(2,1)S(1)}, u32[]{:S(2)}, u32[]{:S(2)}) collective-permute-start(bf16[864,128]{1,0:T(8,128)(2,1)} %get-tuple-element.58), channel_id=1, source_target_pairs={{0,3},{1,16},{2,1},{3,18},{4,7},{5,20},{6,5},{7,22},{8,11},{9,24},... | collective-permute-start | bytes 663560 | tf_op jit(solution)/shard_map/ppermute | solution.py:446
  80.8 2.9 %collective-permute-start.20 = (bf16[864,128]{1,0:T(8,128)(2,1)}, bf16[864,128]{1,0:T(8,128)(2,1)S(1)}, u32[]{:S(2)}, u32[]{:S(2)}) collective-permute-start(bf16[864,128]{1,0:T(8,128)(2,1)} %get-tuple-element.60), channel_id=1, source_target_pairs={{0,7},{1,16},{2,5},{3,18},{4,3},{5,20},{6,1},{7,22},{8,15},{9,24},... | collective-permute-start | bytes 663560 | tf_op jit(solution)/shard_map/ppermute | solution.py:446
  83.6 1.2 collective-permute-done.16.refs_5_
  84.8 1.7 %copy-done.9 = bf16[97,128,128]{2,1,0:T(8,128)(2,1)} copy-done((bf16[97,128,128]{2,1,0:T(8,128)(2,1)}, bf16[97,128,128]{2,1,0:T(8,128)(2,1)S(1)}, u32[]{:S(2)}) %copy-start.9) | copy-done | bytes 3178520
  86.5 5.9 %expert.6 = (bf16[864,128]{1,0:T(8,128)(2,1)}, bf16[864,128]{1,0:T(8,128)(2,1)}, bf16[864,128]{1,0:T(8,128)(2,1)}, bf16[864,128]{1,0:T(8,128)(2,1)}) custom-call(s32[2]{0:T(128)S(1)} %pad_add_fusion.info, bf16[97,128,128]{2,1,0:T(8,128)(2,1)} %tie.6.refs_0_, bf16[97,128,128]{2,1,0:T(8,128)(2,1)} %copy-done.9, ...), custom_call_target="tpu_custom_call" | custom-call | tf_op jit(solution)/shard_map/expert/pallas_call | solution.py:483
  92.5 2.4 %collective-permute-start.27 = (bf16[864,128]{1,0:T(8,128)(2,1)}, bf16[864,128]{1,0:T(8,128)(2,1)S(1)}, u32[]{:S(2)}, u32[]{:S(2)}) collective-permute-start(bf16[864,128]{1,0:T(8,128)(2,1)} %get-tuple-element.67), channel_id=1, source_target_pairs={{0,16},{1,5},{2,18},{3,7},{4,20},{5,1},{6,22},{7,3},{8,24},{9,13},... | collective-permute-start | bytes 663560 | tf_op jit(solution)/shard_map/ppermute | solution.py:446
  95.5 5.8 %expert.7 = (bf16[864,128]{1,0:T(8,128)(2,1)}, bf16[864,128]{1,0:T(8,128)(2,1)}, bf16[864,128]{1,0:T(8,128)(2,1)}, bf16[864,128]{1,0:T(8,128)(2,1)}) custom-call(s32[2]{0:T(128)S(1)} %pad_add_fusion.info, bf16[97,128,128]{2,1,0:T(8,128)(2,1)} %tie.6.refs_0_, bf16[97,128,128]{2,1,0:T(8,128)(2,1)} %copy-done.9, ...), custom_call_target="tpu_custom_call" | custom-call | tf_op jit(solution)/shard_map/expert/pallas_call | solution.py:483
  102.9 2.7 %collective-permute-start.23 = (bf16[864,128]{1,0:T(8,128)(2,1)}, bf16[864,128]{1,0:T(8,128)(2,1)S(1)}, u32[]{:S(2)}, u32[]{:S(2)}) collective-permute-start(bf16[864,128]{1,0:T(8,128)(2,1)} %get-tuple-element.63), channel_id=1, source_target_pairs={{0,16},{1,5},{2,18},{3,7},{4,20},{5,1},{6,22},{7,3},{8,24},{9,13},... | collective-permute-start | bytes 663560 | tf_op jit(solution)/shard_map/ppermute | solution.py:446
  106.1 1.3 %collective-permute-start.24 = (bf16[864,128]{1,0:T(8,128)(2,1)}, bf16[864,128]{1,0:T(8,128)(2,1)S(1)}, u32[]{:S(2)}, u32[]{:S(2)}) collective-permute-start(bf16[864,128]{1,0:T(8,128)(2,1)} %get-tuple-element.64), channel_id=1, source_target_pairs={{0,16},{1,7},{2,18},{3,5},{4,20},{5,3},{6,22},{7,1},{8,24},{9,15},... | collective-permute-start | bytes 663560 | tf_op jit(solution)/shard_map/ppermute | solution.py:446
  107.4 2.8 %last.2.rest_4_ = bf16[1,2,32,6144]{3,2,1,0:T(8,128)(2,1)} custom-call(s32[2]{0:T(128)S(1)} %pad_add_fusion.info, bf16[32,6144]{1,0:T(8,128)(2,1)} %get-tuple-element.49.refs_9_.first, bf16[1536,128]{1,0:T(8,128)(2,1)S(1)} %collective-permute-done.25.carried, s32[1,2,2,32]{3,2,1,0:T(2,128)S(1)} %bitcast.13, f32[1,2,2,32]{3,2,1,0:T(2,128)S(1)} %bitcast.17, ...), custom_call_target="tpu_custom_call" | custom-call | tf_op jit(solution)/shard_map/last/pallas_call | solution.py:483
  110.2 2.8 %collective-permute-done.23.rest_2_ = bf16[864,128]{1,0:T(8,128)(2,1)S(1)} collective-permute-done((bf16[864,128]{1,0:T(8,128)(2,1)}, bf16[864,128]{1,0:T(8,128)(2,1)S(1)}, u32[]{:S(2)}, u32[]{:S(2)}) %collective-permute-start.23) | collective-permute-done | bytes 221216 | tf_op jit(solution)/shard_map/ppermute | solution.py:446
  113.0 3.4 %collective-permute-done.24.rest_3_ = bf16[864,128]{1,0:T(8,128)(2,1)S(1)} collective-permute-done((bf16[864,128]{1,0:T(8,128)(2,1)}, bf16[864,128]{1,0:T(8,128)(2,1)S(1)}, u32[]{:S(2)}, u32[]{:S(2)}) %collective-permute-start.24) | collective-permute-done | bytes 221216 | tf_op jit(solution)/shard_map/ppermute | solution.py:446
  116.4 2.8 %last.3 = bf16[1,2,32,6144]{3,2,1,0:T(8,128)(2,1)} custom-call(s32[2]{0:T(128)S(1)} %pad_add_fusion.info, bf16[32,6144]{1,0:T(8,128)(2,1)} %get-tuple-element.50.refs_6_.first, bf16[1536,128]{1,0:T(8,128)(2,1)S(1)} %collective-permute-done.21.carried, s32[1,2,2,32]{3,2,1,0:T(2,128)S(1)} %bitcast.14, ...), custom_call_target="tpu_custom_call", output_to_operand_aliasing={{}: (9, {})} | custom-call | tf_op jit(solution)/shard_map/last/pallas_call | solution.py:483
  (62 shorter events, 7.5 us)
Async XLA Ops:
  3.8 37.1 %collective-permute-start.2 = (bf16[97,128,128]{2,1,0:T(8,128)(2,1)}, bf16[97,128,128]{2,1,0:T(8,128)(2,1)}, u32[]{:S(2)}, u32[]{:S(2)}) collective-permute-start(bf16[97,128,128]{2,1,0:T(8,128)(2,1)} %pack.1.refs_0_), channel_id=1, source_target_pairs={{0,8},{1,17},{2,10},{3,19},{4,12},{5,21},{6,14},{7,23},{8,0},{9,25... | collective-permute-start | bytes 9535496 | tf_op jit(solution)/shard_map/ppermute | solution.py:446
  5.1 2.1 %collective-permute-start.1 = (f32[1,6144]{1,0:T(1,128)S(1)}, f32[1,6144]{1,0:T(1,128)S(1)}, u32[]{:S(2)}, u32[]{:S(2)}) collective-permute-start(f32[1,6144]{1,0:T(1,128)S(1)} %copy-done.8), channel_id=1, source_target_pairs={{0,1},{1,0},{2,3},{3,2},{4,5},{5,4},{6,7},{7,6},{8,9},{9,8},{10,11... | collective-permute-start | bytes 73736 | tf_op jit(solution)/shard_map/ppermute | solution.py:470
  6.1 1.2 collective-permute-start
  7.8 2.1 %collective-permute-start.3 = (bf16[1728,128]{1,0:T(8,128)(2,1)S(1)}, bf16[1728,128]{1,0:T(8,128)(2,1)S(1)}, u32[]{:S(2)}, u32[]{:S(2)}) collective-permute-start(bf16[1728,128]{1,0:T(8,128)(2,1)S(1)} %get-tuple-element.37), channel_id=1, source_target_pairs={{0,2},{2,0},{4,6},{6,4},{8,10},{10,8},{12,14},{14,12},{16,18},{18,... | collective-permute-start | bytes 1327112 | tf_op jit(solution)/shard_map/ppermute | solution.py:446
  8.5 1.4 %collective-permute-start.4 = (bf16[1728,128]{1,0:T(8,128)(2,1)S(1)}, bf16[1728,128]{1,0:T(8,128)(2,1)S(1)}, u32[]{:S(2)}, u32[]{:S(2)}) collective-permute-start(bf16[1728,128]{1,0:T(8,128)(2,1)S(1)} %get-tuple-element.38), channel_id=1, source_target_pairs={{0,4},{2,6},{4,0},{6,2},{8,12},{10,14},{12,8},{14,10},{16,20},{18,... | collective-permute-start | bytes 1327112 | tf_op jit(solution)/shard_map/ppermute | solution.py:446
  9.2 0.7 collective-permute-start.5
  9.9 31.1 %copy-start = (bf16[1728,128]{1,0:T(8,128)(2,1)}, bf16[1728,128]{1,0:T(8,128)(2,1)S(1)}, u32[]{:S(2)}) copy-start(bf16[1728,128]{1,0:T(8,128)(2,1)S(1)} %collective-permute-done.3.refs_1_.refs_3_) | copy-start | bytes 1327108
  9.9 31.1 %copy-start.2 = (bf16[1728,128]{1,0:T(8,128)(2,1)}, bf16[1728,128]{1,0:T(8,128)(2,1)S(1)}, u32[]{:S(2)}) copy-start(bf16[1728,128]{1,0:T(8,128)(2,1)S(1)} %collective-permute-done.4.refs_2_.refs_4_) | copy-start | bytes 1327108
  9.9 31.0 %copy-start.4 = (bf16[1728,128]{1,0:T(8,128)(2,1)}, bf16[1728,128]{1,0:T(8,128)(2,1)S(1)}, u32[]{:S(2)}) copy-start(bf16[1728,128]{1,0:T(8,128)(2,1)S(1)} %collective-permute-done.5.refs_3_.refs_5_) | copy-start | bytes 1327108
  41.0 43.8 %collective-permute-start.12 = (bf16[97,128,128]{2,1,0:T(8,128)(2,1)}, bf16[97,128,128]{2,1,0:T(8,128)(2,1)S(1)}, u32[]{:S(2)}, u32[]{:S(2)}) collective-permute-start(bf16[97,128,128]{2,1,0:T(8,128)(2,1)} %tie.6.refs_0_), channel_id=1, source_target_pairs={{1,9},{3,11},{5,13},{7,15},{9,1},{11,3},{13,5},{15,7},{17,25},{19,... | collective-permute-start | bytes 9535496 | tf_op jit(solution)/shard_map/ppermute | solution.py:446
  45.0 5.1 %collective-permute-start.9 = (bf16[864,128]{1,0:T(8,128)(2,1)}, bf16[864,128]{1,0:T(8,128)(2,1)S(1)}, u32[]{:S(2)}, u32[]{:S(2)}) collective-permute-start(bf16[864,128]{1,0:T(8,128)(2,1)} %get-tuple-element.46), channel_id=1, source_target_pairs={{0,2},{1,17},{2,0},{3,19},{4,6},{5,21},{6,4},{7,23},{8,10},{9,25},... | collective-permute-start | bytes 663560 | tf_op jit(solution)/shard_map/ppermute | solution.py:446
  46.3 6.1 %collective-permute-start.10 = (bf16[864,128]{1,0:T(8,128)(2,1)}, bf16[864,128]{1,0:T(8,128)(2,1)S(1)}, u32[]{:S(2)}, u32[]{:S(2)}) collective-permute-start(bf16[864,128]{1,0:T(8,128)(2,1)} %get-tuple-element.47), channel_id=1, source_target_pairs={{0,4},{1,17},{2,6},{3,19},{4,0},{5,21},{6,2},{7,23},{8,12},{9,25},... | collective-permute-start | bytes 663560 | tf_op jit(solution)/shard_map/ppermute | solution.py:446
  46.5 8.6 %collective-permute-start.11 = (bf16[864,128]{1,0:T(8,128)(2,1)}, bf16[864,128]{1,0:T(8,128)(2,1)S(1)}, u32[]{:S(2)}, u32[]{:S(2)}) collective-permute-start(bf16[864,128]{1,0:T(8,128)(2,1)} %get-tuple-element.48), channel_id=1, source_target_pairs={{0,6},{1,17},{2,4},{3,19},{4,2},{5,21},{6,0},{7,23},{8,14},{9,25},... | collective-permute-start | bytes 663560 | tf_op jit(solution)/shard_map/ppermute | solution.py:446
  48.5 21.1 %collective-permute-start.6 = (bf16[864,128]{1,0:T(8,128)(2,1)}, bf16[864,128]{1,0:T(8,128)(2,1)S(1)}, u32[]{:S(2)}, u32[]{:S(2)}) collective-permute-start(bf16[864,128]{1,0:T(8,128)(2,1)} %get-tuple-element.43), channel_id=1, source_target_pairs={{0,2},{1,17},{2,0},{3,19},{4,6},{5,21},{6,4},{7,23},{8,10},{9,25},... | collective-permute-start | bytes 663560 | tf_op jit(solution)/shard_map/ppermute | solution.py:446
  50.1 20.7 %collective-permute-start.7 = (bf16[864,128]{1,0:T(8,128)(2,1)}, bf16[864,128]{1,0:T(8,128)(2,1)S(1)}, u32[]{:S(2)}, u32[]{:S(2)}) collective-permute-start(bf16[864,128]{1,0:T(8,128)(2,1)} %get-tuple-element.44), channel_id=1, source_target_pairs={{0,4},{1,17},{2,6},{3,19},{4,0},{5,21},{6,2},{7,23},{8,12},{9,25},... | collective-permute-start | bytes 663560 | tf_op jit(solution)/shard_map/ppermute | solution.py:446
  52.4 20.0 %collective-permute-start.8 = (bf16[864,128]{1,0:T(8,128)(2,1)}, bf16[864,128]{1,0:T(8,128)(2,1)S(1)}, u32[]{:S(2)}, u32[]{:S(2)}) collective-permute-start(bf16[864,128]{1,0:T(8,128)(2,1)} %get-tuple-element.45), channel_id=1, source_target_pairs={{0,6},{1,17},{2,4},{3,19},{4,2},{5,21},{6,0},{7,23},{8,14},{9,25},... | collective-permute-start | bytes 663560 | tf_op jit(solution)/shard_map/ppermute | solution.py:446
  56.1 20.7 %collective-permute-start.13 = (bf16[864,128]{1,0:T(8,128)(2,1)}, bf16[864,128]{1,0:T(8,128)(2,1)S(1)}, u32[]{:S(2)}, u32[]{:S(2)}) collective-permute-start(bf16[864,128]{1,0:T(8,128)(2,1)} %get-tuple-element.53), channel_id=1, source_target_pairs={{0,1},{1,0},{2,3},{3,2},{4,5},{5,4},{6,7},{7,6},{8,9},{9,8},{10,11... | collective-permute-start | bytes 663560 | tf_op jit(solution)/shard_map/ppermute | solution.py:470
  69.6 11.2 %collective-permute-start.14 = (bf16[864,128]{1,0:T(8,128)(2,1)}, bf16[864,128]{1,0:T(8,128)(2,1)S(1)}, u32[]{:S(2)}, u32[]{:S(2)}) collective-permute-start(bf16[864,128]{1,0:T(8,128)(2,1)} %get-tuple-element.54), channel_id=1, source_target_pairs={{0,3},{1,16},{2,1},{3,18},{4,7},{5,20},{6,5},{7,22},{8,11},{9,24},... | collective-permute-start | bytes 663560 | tf_op jit(solution)/shard_map/ppermute | solution.py:446
  70.8 10.0 %collective-permute-start.15 = (bf16[864,128]{1,0:T(8,128)(2,1)}, bf16[864,128]{1,0:T(8,128)(2,1)S(1)}, u32[]{:S(2)}, u32[]{:S(2)}) collective-permute-start(bf16[864,128]{1,0:T(8,128)(2,1)} %get-tuple-element.55), channel_id=1, source_target_pairs={{0,5},{1,16},{2,7},{3,18},{4,1},{5,20},{6,3},{7,22},{8,13},{9,24},... | collective-permute-start | bytes 663560 | tf_op jit(solution)/shard_map/ppermute | solution.py:446
  72.5 12.3 %collective-permute-start.16 = (bf16[864,128]{1,0:T(8,128)(2,1)}, bf16[864,128]{1,0:T(8,128)(2,1)S(1)}, u32[]{:S(2)}, u32[]{:S(2)}) collective-permute-start(bf16[864,128]{1,0:T(8,128)(2,1)} %get-tuple-element.56), channel_id=1, source_target_pairs={{0,7},{1,16},{2,5},{3,18},{4,3},{5,20},{6,1},{7,22},{8,15},{9,24},... | collective-permute-start | bytes 663560 | tf_op jit(solution)/shard_map/ppermute | solution.py:446
  76.9 15.7 %collective-permute-start.18 = (bf16[864,128]{1,0:T(8,128)(2,1)}, bf16[864,128]{1,0:T(8,128)(2,1)S(1)}, u32[]{:S(2)}, u32[]{:S(2)}) collective-permute-start(bf16[864,128]{1,0:T(8,128)(2,1)} %get-tuple-element.58), channel_id=1, source_target_pairs={{0,3},{1,16},{2,1},{3,18},{4,7},{5,20},{6,5},{7,22},{8,11},{9,24},... | collective-permute-start | bytes 663560 | tf_op jit(solution)/shard_map/ppermute | solution.py:446
  80.7 14.3 %collective-permute-start.19 = (bf16[864,128]{1,0:T(8,128)(2,1)}, bf16[864,128]{1,0:T(8,128)(2,1)S(1)}, u32[]{:S(2)}, u32[]{:S(2)}) collective-permute-start(bf16[864,128]{1,0:T(8,128)(2,1)} %get-tuple-element.59), channel_id=1, source_target_pairs={{0,5},{1,16},{2,7},{3,18},{4,1},{5,20},{6,3},{7,22},{8,13},{9,24},... | collective-permute-start | bytes 663560 | tf_op jit(solution)/shard_map/ppermute | solution.py:446
  80.8 14.4 %collective-permute-start.20 = (bf16[864,128]{1,0:T(8,128)(2,1)}, bf16[864,128]{1,0:T(8,128)(2,1)S(1)}, u32[]{:S(2)}, u32[]{:S(2)}) collective-permute-start(bf16[864,128]{1,0:T(8,128)(2,1)} %get-tuple-element.60), channel_id=1, source_target_pairs={{0,7},{1,16},{2,5},{3,18},{4,3},{5,20},{6,1},{7,22},{8,15},{9,24},... | collective-permute-start | bytes 663560 | tf_op jit(solution)/shard_map/ppermute | solution.py:446
  92.4 3.1 %collective-permute-start.17 = (bf16[864,128]{1,0:T(8,128)(2,1)}, bf16[864,128]{1,0:T(8,128)(2,1)S(1)}, u32[]{:S(2)}, u32[]{:S(2)}) collective-permute-start(bf16[864,128]{1,0:T(8,128)(2,1)} %tie.7), channel_id=1, source_target_pairs={{0,1},{1,0},{2,3},{3,2},{4,5},{5,4},{6,7},{7,6},{8,9},{9,8},{10,11... | collective-permute-start | bytes 663560 | tf_op jit(solution)/shard_map/ppermute | solution.py:470
  92.4 9.0 %collective-permute-start.26 = (bf16[864,128]{1,0:T(8,128)(2,1)}, bf16[864,128]{1,0:T(8,128)(2,1)S(1)}, u32[]{:S(2)}, u32[]{:S(2)}) collective-permute-start(bf16[864,128]{1,0:T(8,128)(2,1)} %get-tuple-element.66), channel_id=1, source_target_pairs={{0,16},{1,3},{2,18},{3,1},{4,20},{5,7},{6,22},{7,5},{8,24},{9,11},... | collective-permute-start | bytes 663560 | tf_op jit(solution)/shard_map/ppermute | solution.py:446
  92.5 10.4 %collective-permute-start.27 = (bf16[864,128]{1,0:T(8,128)(2,1)}, bf16[864,128]{1,0:T(8,128)(2,1)S(1)}, u32[]{:S(2)}, u32[]{:S(2)}) collective-permute-start(bf16[864,128]{1,0:T(8,128)(2,1)} %get-tuple-element.67), channel_id=1, source_target_pairs={{0,16},{1,5},{2,18},{3,7},{4,20},{5,1},{6,22},{7,3},{8,24},{9,13},... | collective-permute-start | bytes 663560 | tf_op jit(solution)/shard_map/ppermute | solution.py:446
  95.0 11.1 %collective-permute-start.28 = (bf16[864,128]{1,0:T(8,128)(2,1)}, bf16[864,128]{1,0:T(8,128)(2,1)S(1)}, u32[]{:S(2)}, u32[]{:S(2)}) collective-permute-start(bf16[864,128]{1,0:T(8,128)(2,1)} %get-tuple-element.68), channel_id=1, source_target_pairs={{0,16},{1,7},{2,18},{3,5},{4,20},{5,3},{6,22},{7,1},{8,24},{9,15},... | collective-permute-start | bytes 663560 | tf_op jit(solution)/shard_map/ppermute | solution.py:446
  95.2 12.2 %collective-permute-start.25 = (bf16[1536,128]{1,0:T(8,128)(2,1)}, bf16[1536,128]{1,0:T(8,128)(2,1)S(1)}, u32[]{:S(2)}, u32[]{:S(2)}) collective-permute-start(bf16[1536,128]{1,0:T(8,128)(2,1)} %tie.9), channel_id=1, source_target_pairs={{0,1},{1,0},{2,3},{3,2},{4,5},{5,4},{6,7},{7,6},{8,9},{9,8},{10,11... | collective-permute-start | bytes 1179656 | tf_op jit(solution)/shard_map/ppermute | solution.py:470
  101.4 15.1 %collective-permute-start.21 = (bf16[1536,128]{1,0:T(8,128)(2,1)}, bf16[1536,128]{1,0:T(8,128)(2,1)S(1)}, u32[]{:S(2)}, u32[]{:S(2)}) collective-permute-start(bf16[1536,128]{1,0:T(8,128)(2,1)} %tie.8), channel_id=1, source_target_pairs={{0,1},{1,0},{2,3},{3,2},{4,5},{5,4},{6,7},{7,6},{8,9},{9,8},{10,11... | collective-permute-start | bytes 1179656 | tf_op jit(solution)/shard_map/ppermute | solution.py:470
  101.4 8.7 %collective-permute-start.22 = (bf16[864,128]{1,0:T(8,128)(2,1)}, bf16[864,128]{1,0:T(8,128)(2,1)S(1)}, u32[]{:S(2)}, u32[]{:S(2)}) collective-permute-start(bf16[864,128]{1,0:T(8,128)(2,1)} %get-tuple-element.62), channel_id=1, source_target_pairs={{0,16},{1,3},{2,18},{3,1},{4,20},{5,7},{6,22},{7,5},{8,24},{9,11},... | collective-permute-start | bytes 663560 | tf_op jit(solution)/shard_map/ppermute | solution.py:446
  102.9 10.1 %collective-permute-start.23 = (bf16[864,128]{1,0:T(8,128)(2,1)}, bf16[864,128]{1,0:T(8,128)(2,1)S(1)}, u32[]{:S(2)}, u32[]{:S(2)}) collective-permute-start(bf16[864,128]{1,0:T(8,128)(2,1)} %get-tuple-element.63), channel_id=1, source_target_pairs={{0,16},{1,5},{2,18},{3,7},{4,20},{5,1},{6,22},{7,3},{8,24},{9,13},... | collective-permute-start | bytes 663560 | tf_op jit(solution)/shard_map/ppermute | solution.py:446
  106.1 10.3 %collective-permute-start.24 = (bf16[864,128]{1,0:T(8,128)(2,1)}, bf16[864,128]{1,0:T(8,128)(2,1)S(1)}, u32[]{:S(2)}, u32[]{:S(2)}) collective-permute-start(bf16[864,128]{1,0:T(8,128)(2,1)} %get-tuple-element.64), channel_id=1, source_target_pairs={{0,16},{1,7},{2,18},{3,5},{4,20},{5,3},{6,22},{7,1},{8,24},{9,15},... | collective-permute-start | bytes 663560 | tf_op jit(solution)/shard_map/ppermute | solution.py:446
  (7 other events, 30.0 us)

commit v6 on v5

--- a/solution.py
+++ b/solution.py
@@ -353,6 +353,9 @@
         name.start()
     for at in range(3):
         take(at).start()
+    for at in range(2):
+        take(at).wait()
+        give(at).start()
     spread = jnp.where(iota((columns, LANES), 0) == iota((columns, LANES), 1), 1.0, 0.0).astype(jnp.bfloat16)
     row = iota((LANES, LANES), 0)
     for name in names:
@@ -362,9 +365,8 @@
         for at in range(2)
     )
     kept[3 * columns] = jnp.where(row == 0, rows, jnp.where(row == 1, cols, 0.0)).astype(jnp.bfloat16)
-    for at in range(3):
-        take(at).wait()
-        give(at).start()
+    take(2).wait()
+    give(2).start()
     for at in range(3):
         give(at).wait()
 

time: 120 us -> 120 us (level)
  no operation moved by 1% of the time
where the time goes in v6:
time: 120 us; the launch traced here: 119 us
  starting transfers between devices  47.3 us (39%)
  waiting for transfers between devices  44.6 us (37%)
  Pallas kernels  25 us (21%)
  local copies, waits for them, and re-layouts  1.69 us (1%)
    ppermute x23, waiting for transfers between devices, trade(): return lax.ppermute(array, axes, pairs)  43.5 us
    ppermute x23, starting transfers between devices, trade(): return lax.ppermute(array, axes, pairs)  32.5 us
    pallas_call x9, Pallas kernels, call(): pl.pallas_call(kernel, out_shape=out_shape, in_specs=specs, out_specs=out...  21.4 us
    ppermute x6, starting transfers between devices, swap(): return lax.ppermute(array, 'section', [(0, 1), (1, 0)])  14.9 us
    pallas_call x1, Pallas kernels, pack(): pl.pallas_call(pack_kernel, out_shape=pltpu.HBM(shape, jnp.bfloat16), in_...  3.53 us
  transfers between devices with their start and end apart: 29, of which 10 were waited for; matrix products, arithmetic and copies ran while one was open for 0% of the time, Pallas kernels for 16%

profile of v6, /device:TPU:9, one launch (start us, length us, event | category | flops | bytes accessed | tf_op | source)
XLA Modules:
  0.0 119.2 jit_solution(6206599885279250379)
XLA Ops:
  0.1 3.5 %pack.1.refs_0_ = bf16[97,128,128]{2,1,0:T(8,128)(2,1)} custom-call(s32[2]{0:T(128)S(1)} %pad_add_fusion.info, s32[1,32]{1,0:T(1,128)} %bitcast.22, s32[1,32]{1,0:T(1,128)} %bitcast.23, bf16[32,128,128]{2,1,0:T(8,128)(2,1)} %bitcast.19, bf16[32,128,128]{2,1,0:T(8,128)(2,1)} %bitcast.20, bf16[32,128,128]{2,1,0:T(8,128)(2,1)} %bitcast.21), custom_call_target="tpu_custom_call" | custom-call | tf_op jit(solution)/shard_map/pack/pallas_call | solution.py:390
  3.6 1.3 %collective-permute-start.2 = (bf16[97,128,128]{2,1,0:T(8,128)(2,1)}, bf16[97,128,128]{2,1,0:T(8,128)(2,1)}, u32[]{:S(2)}, u32[]{:S(2)}) collective-permute-start(bf16[97,128,128]{2,1,0:T(8,128)(2,1)} %pack.1.refs_0_), channel_id=1, source_target_pairs={{0,8},{1,17},{2,10},{3,19},{4,12},{5,21},{6,14},{7,23},{8,0},{9,25... | collective-permute-start | bytes 9535496 | tf_op jit(solution)/shard_map/ppermute | solution.py:448
  4.9 0.9 collective-permute-start.1
  5.9 1.1 collective-permute-done.rest_0_.refs_3_
  9.7 31.0 %collective-permute-done.2.refs_0_ = bf16[97,128,128]{2,1,0:T(8,128)(2,1)} collective-permute-done((bf16[97,128,128]{2,1,0:T(8,128)(2,1)}, bf16[97,128,128]{2,1,0:T(8,128)(2,1)}, u32[]{:S(2)}, u32[]{:S(2)}) %collective-permute-start.2) | collective-permute-done | bytes 3178528 | tf_op jit(solution)/shard_map/ppermute | solution.py:448
  40.8 3.3 %collective-permute-start.12 = (bf16[97,128,128]{2,1,0:T(8,128)(2,1)}, bf16[97,128,128]{2,1,0:T(8,128)(2,1)S(1)}, u32[]{:S(2)}, u32[]{:S(2)}) collective-permute-start(bf16[97,128,128]{2,1,0:T(8,128)(2,1)} %tie.6.refs_0_), channel_id=1, source_target_pairs={{1,9},{3,11},{5,13},{7,15},{9,1},{11,3},{13,5},{15,7},{17,25},{19,... | collective-permute-start | bytes 9535496 | tf_op jit(solution)/shard_map/ppermute | solution.py:448
  44.8 1.3 %collective-permute-start.9 = (bf16[864,128]{1,0:T(8,128)(2,1)}, bf16[864,128]{1,0:T(8,128)(2,1)S(1)}, u32[]{:S(2)}, u32[]{:S(2)}) collective-permute-start(bf16[864,128]{1,0:T(8,128)(2,1)} %get-tuple-element.46), channel_id=1, source_target_pairs={{0,2},{1,17},{2,0},{3,19},{4,6},{5,21},{6,4},{7,23},{8,10},{9,25},... | collective-permute-start | bytes 663560 | tf_op jit(solution)/shard_map/ppermute | solution.py:448
  46.3 1.2 %collective-permute-start.11 = (bf16[864,128]{1,0:T(8,128)(2,1)}, bf16[864,128]{1,0:T(8,128)(2,1)S(1)}, u32[]{:S(2)}, u32[]{:S(2)}) collective-permute-start(bf16[864,128]{1,0:T(8,128)(2,1)} %get-tuple-element.48), channel_id=1, source_target_pairs={{0,6},{1,17},{2,4},{3,19},{4,2},{5,21},{6,0},{7,23},{8,14},{9,25},... | collective-permute-start | bytes 663560 | tf_op jit(solution)/shard_map/ppermute | solution.py:448
  48.6 1.3 %collective-permute-done.9.refs_6_ = bf16[864,128]{1,0:T(8,128)(2,1)S(1)} collective-permute-done((bf16[864,128]{1,0:T(8,128)(2,1)}, bf16[864,128]{1,0:T(8,128)(2,1)S(1)}, u32[]{:S(2)}, u32[]{:S(2)}) %collective-permute-start.9) | collective-permute-done | bytes 221216 | tf_op jit(solution)/shard_map/ppermute | solution.py:448
  49.9 1.2 %collective-permute-start.7 = (bf16[864,128]{1,0:T(8,128)(2,1)}, bf16[864,128]{1,0:T(8,128)(2,1)S(1)}, u32[]{:S(2)}, u32[]{:S(2)}) collective-permute-start(bf16[864,128]{1,0:T(8,128)(2,1)} %get-tuple-element.44), channel_id=1, source_target_pairs={{0,4},{1,17},{2,6},{3,19},{4,0},{5,21},{6,2},{7,23},{8,12},{9,25},... | collective-permute-start | bytes 663560 | tf_op jit(solution)/shard_map/ppermute | solution.py:448
  51.1 1.1 collective-permute-done.10.refs_7_
  52.2 1.2 %collective-permute-start.8 = (bf16[864,128]{1,0:T(8,128)(2,1)}, bf16[864,128]{1,0:T(8,128)(2,1)S(1)}, u32[]{:S(2)}, u32[]{:S(2)}) collective-permute-start(bf16[864,128]{1,0:T(8,128)(2,1)} %get-tuple-element.45), channel_id=1, source_target_pairs={{0,6},{1,17},{2,4},{3,19},{4,2},{5,21},{6,0},{7,23},{8,14},{9,25},... | collective-permute-start | bytes 663560 | tf_op jit(solution)/shard_map/ppermute | solution.py:448
  53.5 1.4 %collective-permute-done.11.refs_8_ = bf16[864,128]{1,0:T(8,128)(2,1)S(1)} collective-permute-done((bf16[864,128]{1,0:T(8,128)(2,1)}, bf16[864,128]{1,0:T(8,128)(2,1)S(1)}, u32[]{:S(2)}, u32[]{:S(2)}) %collective-permute-start.11) | collective-permute-done | bytes 221216 | tf_op jit(solution)/shard_map/ppermute | solution.py:448
  54.9 1.0 relay.2
  55.9 13.4 %collective-permute-start.13 = (bf16[864,128]{1,0:T(8,128)(2,1)}, bf16[864,128]{1,0:T(8,128)(2,1)S(1)}, u32[]{:S(2)}, u32[]{:S(2)}) collective-permute-start(bf16[864,128]{1,0:T(8,128)(2,1)} %get-tuple-element.53), channel_id=1, source_target_pairs={{0,1},{1,0},{2,3},{3,2},{4,5},{5,4},{6,7},{7,6},{8,9},{9,8},{10,11... | collective-permute-start | bytes 663560 | tf_op jit(solution)/shard_map/ppermute | solution.py:472
  69.3 1.2 %collective-permute-start.14 = (bf16[864,128]{1,0:T(8,128)(2,1)}, bf16[864,128]{1,0:T(8,128)(2,1)S(1)}, u32[]{:S(2)}, u32[]{:S(2)}) collective-permute-start(bf16[864,128]{1,0:T(8,128)(2,1)} %get-tuple-element.54), channel_id=1, source_target_pairs={{0,3},{1,16},{2,1},{3,18},{4,7},{5,20},{6,5},{7,22},{8,11},{9,24},... | collective-permute-start | bytes 663560 | tf_op jit(solution)/shard_map/ppermute | solution.py:448
  70.5 1.7 %collective-permute-start.15 = (bf16[864,128]{1,0:T(8,128)(2,1)}, bf16[864,128]{1,0:T(8,128)(2,1)S(1)}, u32[]{:S(2)}, u32[]{:S(2)}) collective-permute-start(bf16[864,128]{1,0:T(8,128)(2,1)} %get-tuple-element.55), channel_id=1, source_target_pairs={{0,5},{1,16},{2,7},{3,18},{4,1},{5,20},{6,3},{7,22},{8,13},{9,24},... | collective-permute-start | bytes 663560 | tf_op jit(solution)/shard_map/ppermute | solution.py:448
  72.3 3.2 %collective-permute-start.16 = (bf16[864,128]{1,0:T(8,128)(2,1)}, bf16[864,128]{1,0:T(8,128)(2,1)S(1)}, u32[]{:S(2)}, u32[]{:S(2)}) collective-permute-start(bf16[864,128]{1,0:T(8,128)(2,1)} %get-tuple-element.56), channel_id=1, source_target_pairs={{0,7},{1,16},{2,5},{3,18},{4,3},{5,20},{6,1},{7,22},{8,15},{9,24},... | collective-permute-start | bytes 663560 | tf_op jit(solution)/shard_map/ppermute | solution.py:448
  75.5 1.2 %relay.3 = (bf16[32,6144]{1,0:T(8,128)(2,1)}, bf16[864,128]{1,0:T(8,128)(2,1)}, bf16[1536,128]{1,0:T(8,128)(2,1)}, bf16[864,128]{1,0:T(8,128)(2,1)}, bf16[864,128]{1,0:T(8,128)(2,1)}, /*index=5*/bf16[864,128]{1,0:T(8,128)(2,1)}) custom-call(s32[2]{0:T(128)S(1)} %pad_add_fusion.info, bf16[2,32,6144]{2,1,0:T(8,128)(2,1)} %refs_0_.3, ...), custom_call_target="tpu_custom_call" | custom-call | tf_op jit(solution)/shard_map/relay/pallas_call | solution.py:485
  76.7 3.8 %collective-permute-start.18 = (bf16[864,128]{1,0:T(8,128)(2,1)}, bf16[864,128]{1,0:T(8,128)(2,1)S(1)}, u32[]{:S(2)}, u32[]{:S(2)}) collective-permute-start(bf16[864,128]{1,0:T(8,128)(2,1)} %get-tuple-element.58), channel_id=1, source_target_pairs={{0,3},{1,16},{2,1},{3,18},{4,7},{5,20},{6,5},{7,22},{8,11},{9,24},... | collective-permute-start | bytes 663560 | tf_op jit(solution)/shard_map/ppermute | solution.py:448
  80.6 2.8 %collective-permute-start.20 = (bf16[864,128]{1,0:T(8,128)(2,1)}, bf16[864,128]{1,0:T(8,128)(2,1)S(1)}, u32[]{:S(2)}, u32[]{:S(2)}) collective-permute-start(bf16[864,128]{1,0:T(8,128)(2,1)} %get-tuple-element.60), channel_id=1, source_target_pairs={{0,7},{1,16},{2,5},{3,18},{4,3},{5,20},{6,1},{7,22},{8,15},{9,24},... | collective-permute-start | bytes 663560 | tf_op jit(solution)/shard_map/ppermute | solution.py:448
  83.5 1.2 collective-permute-done.16.refs_5_
  84.6 1.7 %copy-done.9 = bf16[97,128,128]{2,1,0:T(8,128)(2,1)} copy-done((bf16[97,128,128]{2,1,0:T(8,128)(2,1)}, bf16[97,128,128]{2,1,0:T(8,128)(2,1)S(1)}, u32[]{:S(2)}) %copy-start.9) | copy-done | bytes 3178520
  86.3 5.9 %expert.6 = (bf16[864,128]{1,0:T(8,128)(2,1)}, bf16[864,128]{1,0:T(8,128)(2,1)}, bf16[864,128]{1,0:T(8,128)(2,1)}, bf16[864,128]{1,0:T(8,128)(2,1)}) custom-call(s32[2]{0:T(128)S(1)} %pad_add_fusion.info, bf16[97,128,128]{2,1,0:T(8,128)(2,1)} %tie.6.refs_0_, bf16[97,128,128]{2,1,0:T(8,128)(2,1)} %copy-done.9, ...), custom_call_target="tpu_custom_call" | custom-call | tf_op jit(solution)/shard_map/expert/pallas_call | solution.py:485
  92.3 2.4 %collective-permute-start.27 = (bf16[864,128]{1,0:T(8,128)(2,1)}, bf16[864,128]{1,0:T(8,128)(2,1)S(1)}, u32[]{:S(2)}, u32[]{:S(2)}) collective-permute-start(bf16[864,128]{1,0:T(8,128)(2,1)} %get-tuple-element.67), channel_id=1, source_target_pairs={{0,16},{1,5},{2,18},{3,7},{4,20},{5,1},{6,22},{7,3},{8,24},{9,13},... | collective-permute-start | bytes 663560 | tf_op jit(solution)/shard_map/ppermute | solution.py:448
  95.3 5.8 %expert.7 = (bf16[864,128]{1,0:T(8,128)(2,1)}, bf16[864,128]{1,0:T(8,128)(2,1)}, bf16[864,128]{1,0:T(8,128)(2,1)}, bf16[864,128]{1,0:T(8,128)(2,1)}) custom-call(s32[2]{0:T(128)S(1)} %pad_add_fusion.info, bf16[97,128,128]{2,1,0:T(8,128)(2,1)} %tie.6.refs_0_, bf16[97,128,128]{2,1,0:T(8,128)(2,1)} %copy-done.9, ...), custom_call_target="tpu_custom_call" | custom-call | tf_op jit(solution)/shard_map/expert/pallas_call | solution.py:485
  102.7 2.7 %collective-permute-start.23 = (bf16[864,128]{1,0:T(8,128)(2,1)}, bf16[864,128]{1,0:T(8,128)(2,1)S(1)}, u32[]{:S(2)}, u32[]{:S(2)}) collective-permute-start(bf16[864,128]{1,0:T(8,128)(2,1)} %get-tuple-element.63), channel_id=1, source_target_pairs={{0,16},{1,5},{2,18},{3,7},{4,20},{5,1},{6,22},{7,3},{8,24},{9,13},... | collective-permute-start | bytes 663560 | tf_op jit(solution)/shard_map/ppermute | solution.py:448
  105.9 1.2 %collective-permute-start.24 = (bf16[864,128]{1,0:T(8,128)(2,1)}, bf16[864,128]{1,0:T(8,128)(2,1)S(1)}, u32[]{:S(2)}, u32[]{:S(2)}) collective-permute-start(bf16[864,128]{1,0:T(8,128)(2,1)} %get-tuple-element.64), channel_id=1, source_target_pairs={{0,16},{1,7},{2,18},{3,5},{4,20},{5,3},{6,22},{7,1},{8,24},{9,15},... | collective-permute-start | bytes 663560 | tf_op jit(solution)/shard_map/ppermute | solution.py:448
  107.2 2.8 %last.2.rest_4_ = bf16[1,2,32,6144]{3,2,1,0:T(8,128)(2,1)} custom-call(s32[2]{0:T(128)S(1)} %pad_add_fusion.info, bf16[32,6144]{1,0:T(8,128)(2,1)} %get-tuple-element.49.refs_9_.first, bf16[1536,128]{1,0:T(8,128)(2,1)S(1)} %collective-permute-done.25.carried, s32[1,2,2,32]{3,2,1,0:T(2,128)S(1)} %bitcast.13, f32[1,2,2,32]{3,2,1,0:T(2,128)S(1)} %bitcast.17, ...), custom_call_target="tpu_custom_call" | custom-call | tf_op jit(solution)/shard_map/last/pallas_call | solution.py:485
  109.9 2.9 %collective-permute-done.23.rest_2_ = bf16[864,128]{1,0:T(8,128)(2,1)S(1)} collective-permute-done((bf16[864,128]{1,0:T(8,128)(2,1)}, bf16[864,128]{1,0:T(8,128)(2,1)S(1)}, u32[]{:S(2)}, u32[]{:S(2)}) %collective-permute-start.23) | collective-permute-done | bytes 221216 | tf_op jit(solution)/shard_map/ppermute | solution.py:448
  112.8 3.4 %collective-permute-done.24.rest_3_ = bf16[864,128]{1,0:T(8,128)(2,1)S(1)} collective-permute-done((bf16[864,128]{1,0:T(8,128)(2,1)}, bf16[864,128]{1,0:T(8,128)(2,1)S(1)}, u32[]{:S(2)}, u32[]{:S(2)}) %collective-permute-start.24) | collective-permute-done | bytes 221216 | tf_op jit(solution)/shard_map/ppermute | solution.py:448
  116.2 2.8 %last.3 = bf16[1,2,32,6144]{3,2,1,0:T(8,128)(2,1)} custom-call(s32[2]{0:T(128)S(1)} %pad_add_fusion.info, bf16[32,6144]{1,0:T(8,128)(2,1)} %get-tuple-element.50.refs_6_.first, bf16[1536,128]{1,0:T(8,128)(2,1)S(1)} %collective-permute-done.21.carried, s32[1,2,2,32]{3,2,1,0:T(2,128)S(1)} %bitcast.14, ...), custom_call_target="tpu_custom_call", output_to_operand_aliasing={{}: (9, {})} | custom-call | tf_op jit(solution)/shard_map/last/pallas_call | solution.py:485
  (62 shorter events, 7.5 us)
Async XLA Ops:
  3.6 37.1 %collective-permute-start.2 = (bf16[97,128,128]{2,1,0:T(8,128)(2,1)}, bf16[97,128,128]{2,1,0:T(8,128)(2,1)}, u32[]{:S(2)}, u32[]{:S(2)}) collective-permute-start(bf16[97,128,128]{2,1,0:T(8,128)(2,1)} %pack.1.refs_0_), channel_id=1, source_target_pairs={{0,8},{1,17},{2,10},{3,19},{4,12},{5,21},{6,14},{7,23},{8,0},{9,25... | collective-permute-start | bytes 9535496 | tf_op jit(solution)/shard_map/ppermute | solution.py:448
  4.9 2.1 %collective-permute-start.1 = (f32[1,6144]{1,0:T(1,128)S(1)}, f32[1,6144]{1,0:T(1,128)S(1)}, u32[]{:S(2)}, u32[]{:S(2)}) collective-permute-start(f32[1,6144]{1,0:T(1,128)S(1)} %copy-done.8), channel_id=1, source_target_pairs={{0,1},{1,0},{2,3},{3,2},{4,5},{5,4},{6,7},{7,6},{8,9},{9,8},{10,11... | collective-permute-start | bytes 73736 | tf_op jit(solution)/shard_map/ppermute | solution.py:472
  5.9 1.2 collective-permute-start
  7.6 2.1 %collective-permute-start.3 = (bf16[1728,128]{1,0:T(8,128)(2,1)S(1)}, bf16[1728,128]{1,0:T(8,128)(2,1)S(1)}, u32[]{:S(2)}, u32[]{:S(2)}) collective-permute-start(bf16[1728,128]{1,0:T(8,128)(2,1)S(1)} %get-tuple-element.37), channel_id=1, source_target_pairs={{0,2},{2,0},{4,6},{6,4},{8,10},{10,8},{12,14},{14,12},{16,18},{18,... | collective-permute-start | bytes 1327112 | tf_op jit(solution)/shard_map/ppermute | solution.py:448
  8.3 1.4 %collective-permute-start.4 = (bf16[1728,128]{1,0:T(8,128)(2,1)S(1)}, bf16[1728,128]{1,0:T(8,128)(2,1)S(1)}, u32[]{:S(2)}, u32[]{:S(2)}) collective-permute-start(bf16[1728,128]{1,0:T(8,128)(2,1)S(1)} %get-tuple-element.38), channel_id=1, source_target_pairs={{0,4},{2,6},{4,0},{6,2},{8,12},{10,14},{12,8},{14,10},{16,20},{18,... | collective-permute-start | bytes 1327112 | tf_op jit(solution)/shard_map/ppermute | solution.py:448
  9.0 0.7 collective-permute-start.5
  9.7 31.1 %copy-start = (bf16[1728,128]{1,0:T(8,128)(2,1)}, bf16[1728,128]{1,0:T(8,128)(2,1)S(1)}, u32[]{:S(2)}) copy-start(bf16[1728,128]{1,0:T(8,128)(2,1)S(1)} %collective-permute-done.3.refs_1_.refs_3_) | copy-start | bytes 1327108
  9.7 31.1 %copy-start.2 = (bf16[1728,128]{1,0:T(8,128)(2,1)}, bf16[1728,128]{1,0:T(8,128)(2,1)S(1)}, u32[]{:S(2)}) copy-start(bf16[1728,128]{1,0:T(8,128)(2,1)S(1)} %collective-permute-done.4.refs_2_.refs_4_) | copy-start | bytes 1327108
  9.7 31.0 %copy-start.4 = (bf16[1728,128]{1,0:T(8,128)(2,1)}, bf16[1728,128]{1,0:T(8,128)(2,1)S(1)}, u32[]{:S(2)}) copy-start(bf16[1728,128]{1,0:T(8,128)(2,1)S(1)} %collective-permute-done.5.refs_3_.refs_5_) | copy-start | bytes 1327108
  40.8 43.8 %collective-permute-start.12 = (bf16[97,128,128]{2,1,0:T(8,128)(2,1)}, bf16[97,128,128]{2,1,0:T(8,128)(2,1)S(1)}, u32[]{:S(2)}, u32[]{:S(2)}) collective-permute-start(bf16[97,128,128]{2,1,0:T(8,128)(2,1)} %tie.6.refs_0_), channel_id=1, source_target_pairs={{1,9},{3,11},{5,13},{7,15},{9,1},{11,3},{13,5},{15,7},{17,25},{19,... | collective-permute-start | bytes 9535496 | tf_op jit(solution)/shard_map/ppermute | solution.py:448
  44.8 5.1 %collective-permute-start.9 = (bf16[864,128]{1,0:T(8,128)(2,1)}, bf16[864,128]{1,0:T(8,128)(2,1)S(1)}, u32[]{:S(2)}, u32[]{:S(2)}) collective-permute-start(bf16[864,128]{1,0:T(8,128)(2,1)} %get-tuple-element.46), channel_id=1, source_target_pairs={{0,2},{1,17},{2,0},{3,19},{4,6},{5,21},{6,4},{7,23},{8,10},{9,25},... | collective-permute-start | bytes 663560 | tf_op jit(solution)/shard_map/ppermute | solution.py:448
  46.1 6.1 %collective-permute-start.10 = (bf16[864,128]{1,0:T(8,128)(2,1)}, bf16[864,128]{1,0:T(8,128)(2,1)S(1)}, u32[]{:S(2)}, u32[]{:S(2)}) collective-permute-start(bf16[864,128]{1,0:T(8,128)(2,1)} %get-tuple-element.47), channel_id=1, source_target_pairs={{0,4},{1,17},{2,6},{3,19},{4,0},{5,21},{6,2},{7,23},{8,12},{9,25},... | collective-permute-start | bytes 663560 | tf_op jit(solution)/shard_map/ppermute | solution.py:448
  46.3 8.6 %collective-permute-start.11 = (bf16[864,128]{1,0:T(8,128)(2,1)}, bf16[864,128]{1,0:T(8,128)(2,1)S(1)}, u32[]{:S(2)}, u32[]{:S(2)}) collective-permute-start(bf16[864,128]{1,0:T(8,128)(2,1)} %get-tuple-element.48), channel_id=1, source_target_pairs={{0,6},{1,17},{2,4},{3,19},{4,2},{5,21},{6,0},{7,23},{8,14},{9,25},... | collective-permute-start | bytes 663560 | tf_op jit(solution)/shard_map/ppermute | solution.py:448
  48.3 21.1 %collective-permute-start.6 = (bf16[864,128]{1,0:T(8,128)(2,1)}, bf16[864,128]{1,0:T(8,128)(2,1)S(1)}, u32[]{:S(2)}, u32[]{:S(2)}) collective-permute-start(bf16[864,128]{1,0:T(8,128)(2,1)} %get-tuple-element.43), channel_id=1, source_target_pairs={{0,2},{1,17},{2,0},{3,19},{4,6},{5,21},{6,4},{7,23},{8,10},{9,25},... | collective-permute-start | bytes 663560 | tf_op jit(solution)/shard_map/ppermute | solution.py:448
  49.9 20.7 %collective-permute-start.7 = (bf16[864,128]{1,0:T(8,128)(2,1)}, bf16[864,128]{1,0:T(8,128)(2,1)S(1)}, u32[]{:S(2)}, u32[]{:S(2)}) collective-permute-start(bf16[864,128]{1,0:T(8,128)(2,1)} %get-tuple-element.44), channel_id=1, source_target_pairs={{0,4},{1,17},{2,6},{3,19},{4,0},{5,21},{6,2},{7,23},{8,12},{9,25},... | collective-permute-start | bytes 663560 | tf_op jit(solution)/shard_map/ppermute | solution.py:448
  52.2 20.1 %collective-permute-start.8 = (bf16[864,128]{1,0:T(8,128)(2,1)}, bf16[864,128]{1,0:T(8,128)(2,1)S(1)}, u32[]{:S(2)}, u32[]{:S(2)}) collective-permute-start(bf16[864,128]{1,0:T(8,128)(2,1)} %get-tuple-element.45), channel_id=1, source_target_pairs={{0,6},{1,17},{2,4},{3,19},{4,2},{5,21},{6,0},{7,23},{8,14},{9,25},... | collective-permute-start | bytes 663560 | tf_op jit(solution)/shard_map/ppermute | solution.py:448
  55.9 20.8 %collective-permute-start.13 = (bf16[864,128]{1,0:T(8,128)(2,1)}, bf16[864,128]{1,0:T(8,128)(2,1)S(1)}, u32[]{:S(2)}, u32[]{:S(2)}) collective-permute-start(bf16[864,128]{1,0:T(8,128)(2,1)} %get-tuple-element.53), channel_id=1, source_target_pairs={{0,1},{1,0},{2,3},{3,2},{4,5},{5,4},{6,7},{7,6},{8,9},{9,8},{10,11... | collective-permute-start | bytes 663560 | tf_op jit(solution)/shard_map/ppermute | solution.py:472
  69.3 11.2 %collective-permute-start.14 = (bf16[864,128]{1,0:T(8,128)(2,1)}, bf16[864,128]{1,0:T(8,128)(2,1)S(1)}, u32[]{:S(2)}, u32[]{:S(2)}) collective-permute-start(bf16[864,128]{1,0:T(8,128)(2,1)} %get-tuple-element.54), channel_id=1, source_target_pairs={{0,3},{1,16},{2,1},{3,18},{4,7},{5,20},{6,5},{7,22},{8,11},{9,24},... | collective-permute-start | bytes 663560 | tf_op jit(solution)/shard_map/ppermute | solution.py:448
  70.5 10.1 %collective-permute-start.15 = (bf16[864,128]{1,0:T(8,128)(2,1)}, bf16[864,128]{1,0:T(8,128)(2,1)S(1)}, u32[]{:S(2)}, u32[]{:S(2)}) collective-permute-start(bf16[864,128]{1,0:T(8,128)(2,1)} %get-tuple-element.55), channel_id=1, source_target_pairs={{0,5},{1,16},{2,7},{3,18},{4,1},{5,20},{6,3},{7,22},{8,13},{9,24},... | collective-permute-start | bytes 663560 | tf_op jit(solution)/shard_map/ppermute | solution.py:448
  72.3 12.3 %collective-permute-start.16 = (bf16[864,128]{1,0:T(8,128)(2,1)}, bf16[864,128]{1,0:T(8,128)(2,1)S(1)}, u32[]{:S(2)}, u32[]{:S(2)}) collective-permute-start(bf16[864,128]{1,0:T(8,128)(2,1)} %get-tuple-element.56), channel_id=1, source_target_pairs={{0,7},{1,16},{2,5},{3,18},{4,3},{5,20},{6,1},{7,22},{8,15},{9,24},... | collective-permute-start | bytes 663560 | tf_op jit(solution)/shard_map/ppermute | solution.py:448
  76.7 15.6 %collective-permute-start.18 = (bf16[864,128]{1,0:T(8,128)(2,1)}, bf16[864,128]{1,0:T(8,128)(2,1)S(1)}, u32[]{:S(2)}, u32[]{:S(2)}) collective-permute-start(bf16[864,128]{1,0:T(8,128)(2,1)} %get-tuple-element.58), channel_id=1, source_target_pairs={{0,3},{1,16},{2,1},{3,18},{4,7},{5,20},{6,5},{7,22},{8,11},{9,24},... | collective-permute-start | bytes 663560 | tf_op jit(solution)/shard_map/ppermute | solution.py:448
  80.5 14.2 %collective-permute-start.19 = (bf16[864,128]{1,0:T(8,128)(2,1)}, bf16[864,128]{1,0:T(8,128)(2,1)S(1)}, u32[]{:S(2)}, u32[]{:S(2)}) collective-permute-start(bf16[864,128]{1,0:T(8,128)(2,1)} %get-tuple-element.59), channel_id=1, source_target_pairs={{0,5},{1,16},{2,7},{3,18},{4,1},{5,20},{6,3},{7,22},{8,13},{9,24},... | collective-permute-start | bytes 663560 | tf_op jit(solution)/shard_map/ppermute | solution.py:448
  80.6 14.4 %collective-permute-start.20 = (bf16[864,128]{1,0:T(8,128)(2,1)}, bf16[864,128]{1,0:T(8,128)(2,1)S(1)}, u32[]{:S(2)}, u32[]{:S(2)}) collective-permute-start(bf16[864,128]{1,0:T(8,128)(2,1)} %get-tuple-element.60), channel_id=1, source_target_pairs={{0,7},{1,16},{2,5},{3,18},{4,3},{5,20},{6,1},{7,22},{8,15},{9,24},... | collective-permute-start | bytes 663560 | tf_op jit(solution)/shard_map/ppermute | solution.py:448
  92.2 3.1 %collective-permute-start.17 = (bf16[864,128]{1,0:T(8,128)(2,1)}, bf16[864,128]{1,0:T(8,128)(2,1)S(1)}, u32[]{:S(2)}, u32[]{:S(2)}) collective-permute-start(bf16[864,128]{1,0:T(8,128)(2,1)} %tie.7), channel_id=1, source_target_pairs={{0,1},{1,0},{2,3},{3,2},{4,5},{5,4},{6,7},{7,6},{8,9},{9,8},{10,11... | collective-permute-start | bytes 663560 | tf_op jit(solution)/shard_map/ppermute | solution.py:472
  92.3 9.0 %collective-permute-start.26 = (bf16[864,128]{1,0:T(8,128)(2,1)}, bf16[864,128]{1,0:T(8,128)(2,1)S(1)}, u32[]{:S(2)}, u32[]{:S(2)}) collective-permute-start(bf16[864,128]{1,0:T(8,128)(2,1)} %get-tuple-element.66), channel_id=1, source_target_pairs={{0,16},{1,3},{2,18},{3,1},{4,20},{5,7},{6,22},{7,5},{8,24},{9,11},... | collective-permute-start | bytes 663560 | tf_op jit(solution)/shard_map/ppermute | solution.py:448
  92.3 10.3 %collective-permute-start.27 = (bf16[864,128]{1,0:T(8,128)(2,1)}, bf16[864,128]{1,0:T(8,128)(2,1)S(1)}, u32[]{:S(2)}, u32[]{:S(2)}) collective-permute-start(bf16[864,128]{1,0:T(8,128)(2,1)} %get-tuple-element.67), channel_id=1, source_target_pairs={{0,16},{1,5},{2,18},{3,7},{4,20},{5,1},{6,22},{7,3},{8,24},{9,13},... | collective-permute-start | bytes 663560 | tf_op jit(solution)/shard_map/ppermute | solution.py:448
  94.8 11.1 %collective-permute-start.28 = (bf16[864,128]{1,0:T(8,128)(2,1)}, bf16[864,128]{1,0:T(8,128)(2,1)S(1)}, u32[]{:S(2)}, u32[]{:S(2)}) collective-permute-start(bf16[864,128]{1,0:T(8,128)(2,1)} %get-tuple-element.68), channel_id=1, source_target_pairs={{0,16},{1,7},{2,18},{3,5},{4,20},{5,3},{6,22},{7,1},{8,24},{9,15},... | collective-permute-start | bytes 663560 | tf_op jit(solution)/shard_map/ppermute | solution.py:448
  95.0 12.2 %collective-permute-start.25 = (bf16[1536,128]{1,0:T(8,128)(2,1)}, bf16[1536,128]{1,0:T(8,128)(2,1)S(1)}, u32[]{:S(2)}, u32[]{:S(2)}) collective-permute-start(bf16[1536,128]{1,0:T(8,128)(2,1)} %tie.9), channel_id=1, source_target_pairs={{0,1},{1,0},{2,3},{3,2},{4,5},{5,4},{6,7},{7,6},{8,9},{9,8},{10,11... | collective-permute-start | bytes 1179656 | tf_op jit(solution)/shard_map/ppermute | solution.py:472
  101.2 15.1 %collective-permute-start.21 = (bf16[1536,128]{1,0:T(8,128)(2,1)}, bf16[1536,128]{1,0:T(8,128)(2,1)S(1)}, u32[]{:S(2)}, u32[]{:S(2)}) collective-permute-start(bf16[1536,128]{1,0:T(8,128)(2,1)} %tie.8), channel_id=1, source_target_pairs={{0,1},{1,0},{2,3},{3,2},{4,5},{5,4},{6,7},{7,6},{8,9},{9,8},{10,11... | collective-permute-start | bytes 1179656 | tf_op jit(solution)/shard_map/ppermute | solution.py:472
  101.3 8.7 %collective-permute-start.22 = (bf16[864,128]{1,0:T(8,128)(2,1)}, bf16[864,128]{1,0:T(8,128)(2,1)S(1)}, u32[]{:S(2)}, u32[]{:S(2)}) collective-permute-start(bf16[864,128]{1,0:T(8,128)(2,1)} %get-tuple-element.62), channel_id=1, source_target_pairs={{0,16},{1,3},{2,18},{3,1},{4,20},{5,7},{6,22},{7,5},{8,24},{9,11},... | collective-permute-start | bytes 663560 | tf_op jit(solution)/shard_map/ppermute | solution.py:448
  102.7 10.1 %collective-permute-start.23 = (bf16[864,128]{1,0:T(8,128)(2,1)}, bf16[864,128]{1,0:T(8,128)(2,1)S(1)}, u32[]{:S(2)}, u32[]{:S(2)}) collective-permute-start(bf16[864,128]{1,0:T(8,128)(2,1)} %get-tuple-element.63), channel_id=1, source_target_pairs={{0,16},{1,5},{2,18},{3,7},{4,20},{5,1},{6,22},{7,3},{8,24},{9,13},... | collective-permute-start | bytes 663560 | tf_op jit(solution)/shard_map/ppermute | solution.py:448
  105.9 10.3 %collective-permute-start.24 = (bf16[864,128]{1,0:T(8,128)(2,1)}, bf16[864,128]{1,0:T(8,128)(2,1)S(1)}, u32[]{:S(2)}, u32[]{:S(2)}) collective-permute-start(bf16[864,128]{1,0:T(8,128)(2,1)} %get-tuple-element.64), channel_id=1, source_target_pairs={{0,16},{1,7},{2,18},{3,5},{4,20},{5,3},{6,22},{7,1},{8,24},{9,15},... | collective-permute-start | bytes 663560 | tf_op jit(solution)/shard_map/ppermute | solution.py:448
  (7 other events, 29.7 us)

commit v7 on v6

--- a/solution.py
+++ b/solution.py
@@ -203,13 +203,16 @@
     returned, (out, made, done) = rest[:partners], rest[-3:]
     tokens, width = made.shape
     blocks = width // LANES
-    keep = pltpu.make_async_copy(made, out.at[0, micro], done.at[0])
+    cut = blocks // group // 2 * group * LANES
+    spans = pl.ds(0, cut), pl.ds(cut, width - cut)
+    keeps = [pltpu.make_async_copy(made.at[:, p], out.at[0, micro, :, p], done.at[i]) for i, p in enumerate(spans)]
 
     @pl.when(info[0] == 0)
     def _():
         copy = pltpu.make_async_copy(first, made, done.at[1])
         copy.start()
         copy.wait()
+        keeps[0].start()
 
     @pl.when(info[0] != 0)
     def _():
@@ -223,9 +226,12 @@
             for j in range(group):
                 b = number * group + j
                 made[:, b * LANES : (b + 1) * LANES] = mixed[j * tokens : (j + 1) * tokens, :]
-
-    keep.start()
-    keep.wait()
+            if (number + 1) * group * LANES == cut:
+                keeps[0].start()
+
+    keeps[1].start()
+    for keep in keeps:
+        keep.wait()
 
 
 def expert_kernel(section, partners, offsets, capacity, group, split, unroll, info, *refs):

time: 120 us -> 120 us (level)
  no operation moved by 1% of the time
where the time goes in v7:
time: 120 us; the launch traced here: 119 us
  starting transfers between devices  47.4 us (40%)
  waiting for transfers between devices  44.6 us (37%)
  Pallas kernels  24.9 us (21%)
  local copies, waits for them, and re-layouts  1.69 us (1%)
    ppermute x23, waiting for transfers between devices, trade(): return lax.ppermute(array, axes, pairs)  43.5 us
    ppermute x23, starting transfers between devices, trade(): return lax.ppermute(array, axes, pairs)  32.5 us
    pallas_call x9, Pallas kernels, call(): pl.pallas_call(kernel, out_shape=out_shape, in_specs=specs, out_specs=out...  21.4 us
    ppermute x6, starting transfers between devices, swap(): return lax.ppermute(array, 'section', [(0, 1), (1, 0)])  14.9 us
    pallas_call x1, Pallas kernels, pack(): pl.pallas_call(pack_kernel, out_shape=pltpu.HBM(shape, jnp.bfloat16), in_...  3.53 us
  transfers between devices with their start and end apart: 29, of which 10 were waited for; matrix products, arithmetic and copies ran while one was open for 0% of the time, Pallas kernels for 16%

profile of v7, /device:TPU:9, one launch (start us, length us, event | category | flops | bytes accessed | tf_op | source)
XLA Modules:
  0.0 119.2 jit_solution(18147368755452857178)
XLA Ops:
  0.1 3.5 %pack.1.refs_0_ = bf16[97,128,128]{2,1,0:T(8,128)(2,1)} custom-call(s32[2]{0:T(128)S(1)} %pad_add_fusion.info, s32[1,32]{1,0:T(1,128)} %bitcast.22, s32[1,32]{1,0:T(1,128)} %bitcast.23, bf16[32,128,128]{2,1,0:T(8,128)(2,1)} %bitcast.19, bf16[32,128,128]{2,1,0:T(8,128)(2,1)} %bitcast.20, bf16[32,128,128]{2,1,0:T(8,128)(2,1)} %bitcast.21), custom_call_target="tpu_custom_call" | custom-call | tf_op jit(solution)/shard_map/pack/pallas_call | solution.py:396
  3.6 1.3 %collective-permute-start.2 = (bf16[97,128,128]{2,1,0:T(8,128)(2,1)}, bf16[97,128,128]{2,1,0:T(8,128)(2,1)}, u32[]{:S(2)}, u32[]{:S(2)}) collective-permute-start(bf16[97,128,128]{2,1,0:T(8,128)(2,1)} %pack.1.refs_0_), channel_id=1, source_target_pairs={{0,8},{1,17},{2,10},{3,19},{4,12},{5,21},{6,14},{7,23},{8,0},{9,25... | collective-permute-start | bytes 9535496 | tf_op jit(solution)/shard_map/ppermute | solution.py:454
  4.9 0.9 collective-permute-start.1
  5.9 1.1 collective-permute-done.rest_0_.refs_3_
  9.7 31.0 %collective-permute-done.2.refs_0_ = bf16[97,128,128]{2,1,0:T(8,128)(2,1)} collective-permute-done((bf16[97,128,128]{2,1,0:T(8,128)(2,1)}, bf16[97,128,128]{2,1,0:T(8,128)(2,1)}, u32[]{:S(2)}, u32[]{:S(2)}) %collective-permute-start.2) | collective-permute-done | bytes 3178528 | tf_op jit(solution)/shard_map/ppermute | solution.py:454
  40.8 3.3 %collective-permute-start.12 = (bf16[97,128,128]{2,1,0:T(8,128)(2,1)}, bf16[97,128,128]{2,1,0:T(8,128)(2,1)S(1)}, u32[]{:S(2)}, u32[]{:S(2)}) collective-permute-start(bf16[97,128,128]{2,1,0:T(8,128)(2,1)} %tie.6.refs_0_), channel_id=1, source_target_pairs={{1,9},{3,11},{5,13},{7,15},{9,1},{11,3},{13,5},{15,7},{17,25},{19,... | collective-permute-start | bytes 9535496 | tf_op jit(solution)/shard_map/ppermute | solution.py:454
  44.8 1.3 %collective-permute-start.9 = (bf16[864,128]{1,0:T(8,128)(2,1)}, bf16[864,128]{1,0:T(8,128)(2,1)S(1)}, u32[]{:S(2)}, u32[]{:S(2)}) collective-permute-start(bf16[864,128]{1,0:T(8,128)(2,1)} %get-tuple-element.46), channel_id=1, source_target_pairs={{0,2},{1,17},{2,0},{3,19},{4,6},{5,21},{6,4},{7,23},{8,10},{9,25},... | collective-permute-start | bytes 663560 | tf_op jit(solution)/shard_map/ppermute | solution.py:454
  46.3 1.2 %collective-permute-start.11 = (bf16[864,128]{1,0:T(8,128)(2,1)}, bf16[864,128]{1,0:T(8,128)(2,1)S(1)}, u32[]{:S(2)}, u32[]{:S(2)}) collective-permute-start(bf16[864,128]{1,0:T(8,128)(2,1)} %get-tuple-element.48), channel_id=1, source_target_pairs={{0,6},{1,17},{2,4},{3,19},{4,2},{5,21},{6,0},{7,23},{8,14},{9,25},... | collective-permute-start | bytes 663560 | tf_op jit(solution)/shard_map/ppermute | solution.py:454
  48.6 1.3 %collective-permute-done.9.refs_6_ = bf16[864,128]{1,0:T(8,128)(2,1)S(1)} collective-permute-done((bf16[864,128]{1,0:T(8,128)(2,1)}, bf16[864,128]{1,0:T(8,128)(2,1)S(1)}, u32[]{:S(2)}, u32[]{:S(2)}) %collective-permute-start.9) | collective-permute-done | bytes 221216 | tf_op jit(solution)/shard_map/ppermute | solution.py:454
  49.9 1.2 %collective-permute-start.7 = (bf16[864,128]{1,0:T(8,128)(2,1)}, bf16[864,128]{1,0:T(8,128)(2,1)S(1)}, u32[]{:S(2)}, u32[]{:S(2)}) collective-permute-start(bf16[864,128]{1,0:T(8,128)(2,1)} %get-tuple-element.44), channel_id=1, source_target_pairs={{0,4},{1,17},{2,6},{3,19},{4,0},{5,21},{6,2},{7,23},{8,12},{9,25},... | collective-permute-start | bytes 663560 | tf_op jit(solution)/shard_map/ppermute | solution.py:454
  51.1 1.1 collective-permute-done.10.refs_7_
  52.2 1.2 %collective-permute-start.8 = (bf16[864,128]{1,0:T(8,128)(2,1)}, bf16[864,128]{1,0:T(8,128)(2,1)S(1)}, u32[]{:S(2)}, u32[]{:S(2)}) collective-permute-start(bf16[864,128]{1,0:T(8,128)(2,1)} %get-tuple-element.45), channel_id=1, source_target_pairs={{0,6},{1,17},{2,4},{3,19},{4,2},{5,21},{6,0},{7,23},{8,14},{9,25},... | collective-permute-start | bytes 663560 | tf_op jit(solution)/shard_map/ppermute | solution.py:454
  53.5 1.4 %collective-permute-done.11.refs_8_ = bf16[864,128]{1,0:T(8,128)(2,1)S(1)} collective-permute-done((bf16[864,128]{1,0:T(8,128)(2,1)}, bf16[864,128]{1,0:T(8,128)(2,1)S(1)}, u32[]{:S(2)}, u32[]{:S(2)}) %collective-permute-start.11) | collective-permute-done | bytes 221216 | tf_op jit(solution)/shard_map/ppermute | solution.py:454
  54.9 1.0 relay.2
  55.9 13.4 %collective-permute-start.13 = (bf16[864,128]{1,0:T(8,128)(2,1)}, bf16[864,128]{1,0:T(8,128)(2,1)S(1)}, u32[]{:S(2)}, u32[]{:S(2)}) collective-permute-start(bf16[864,128]{1,0:T(8,128)(2,1)} %get-tuple-element.53), channel_id=1, source_target_pairs={{0,1},{1,0},{2,3},{3,2},{4,5},{5,4},{6,7},{7,6},{8,9},{9,8},{10,11... | collective-permute-start | bytes 663560 | tf_op jit(solution)/shard_map/ppermute | solution.py:478
  69.4 1.2 collective-permute-start.14
  70.5 1.7 %collective-permute-start.15 = (bf16[864,128]{1,0:T(8,128)(2,1)}, bf16[864,128]{1,0:T(8,128)(2,1)S(1)}, u32[]{:S(2)}, u32[]{:S(2)}) collective-permute-start(bf16[864,128]{1,0:T(8,128)(2,1)} %get-tuple-element.55), channel_id=1, source_target_pairs={{0,5},{1,16},{2,7},{3,18},{4,1},{5,20},{6,3},{7,22},{8,13},{9,24},... | collective-permute-start | bytes 663560 | tf_op jit(solution)/shard_map/ppermute | solution.py:454
  72.3 3.2 %collective-permute-start.16 = (bf16[864,128]{1,0:T(8,128)(2,1)}, bf16[864,128]{1,0:T(8,128)(2,1)S(1)}, u32[]{:S(2)}, u32[]{:S(2)}) collective-permute-start(bf16[864,128]{1,0:T(8,128)(2,1)} %get-tuple-element.56), channel_id=1, source_target_pairs={{0,7},{1,16},{2,5},{3,18},{4,3},{5,20},{6,1},{7,22},{8,15},{9,24},... | collective-permute-start | bytes 663560 | tf_op jit(solution)/shard_map/ppermute | solution.py:454
  75.5 1.2 %relay.3 = (bf16[32,6144]{1,0:T(8,128)(2,1)}, bf16[864,128]{1,0:T(8,128)(2,1)}, bf16[1536,128]{1,0:T(8,128)(2,1)}, bf16[864,128]{1,0:T(8,128)(2,1)}, bf16[864,128]{1,0:T(8,128)(2,1)}, /*index=5*/bf16[864,128]{1,0:T(8,128)(2,1)}) custom-call(s32[2]{0:T(128)S(1)} %pad_add_fusion.info, bf16[2,32,6144]{2,1,0:T(8,128)(2,1)} %refs_0_.3, ...), custom_call_target="tpu_custom_call" | custom-call | tf_op jit(solution)/shard_map/relay/pallas_call | solution.py:491
  76.7 3.8 %collective-permute-start.18 = (bf16[864,128]{1,0:T(8,128)(2,1)}, bf16[864,128]{1,0:T(8,128)(2,1)S(1)}, u32[]{:S(2)}, u32[]{:S(2)}) collective-permute-start(bf16[864,128]{1,0:T(8,128)(2,1)} %get-tuple-element.58), channel_id=1, source_target_pairs={{0,3},{1,16},{2,1},{3,18},{4,7},{5,20},{6,5},{7,22},{8,11},{9,24},... | collective-permute-start | bytes 663560 | tf_op jit(solution)/shard_map/ppermute | solution.py:454
  80.6 2.8 %collective-permute-start.20 = (bf16[864,128]{1,0:T(8,128)(2,1)}, bf16[864,128]{1,0:T(8,128)(2,1)S(1)}, u32[]{:S(2)}, u32[]{:S(2)}) collective-permute-start(bf16[864,128]{1,0:T(8,128)(2,1)} %get-tuple-element.60), channel_id=1, source_target_pairs={{0,7},{1,16},{2,5},{3,18},{4,3},{5,20},{6,1},{7,22},{8,15},{9,24},... | collective-permute-start | bytes 663560 | tf_op jit(solution)/shard_map/ppermute | solution.py:454
  83.5 1.2 collective-permute-done.16.refs_5_
  84.6 1.7 %copy-done.9 = bf16[97,128,128]{2,1,0:T(8,128)(2,1)} copy-done((bf16[97,128,128]{2,1,0:T(8,128)(2,1)}, bf16[97,128,128]{2,1,0:T(8,128)(2,1)S(1)}, u32[]{:S(2)}) %copy-start.9) | copy-done | bytes 3178520
  86.3 5.9 %expert.6 = (bf16[864,128]{1,0:T(8,128)(2,1)}, bf16[864,128]{1,0:T(8,128)(2,1)}, bf16[864,128]{1,0:T(8,128)(2,1)}, bf16[864,128]{1,0:T(8,128)(2,1)}) custom-call(s32[2]{0:T(128)S(1)} %pad_add_fusion.info, bf16[97,128,128]{2,1,0:T(8,128)(2,1)} %tie.6.refs_0_, bf16[97,128,128]{2,1,0:T(8,128)(2,1)} %copy-done.9, ...), custom_call_target="tpu_custom_call" | custom-call | tf_op jit(solution)/shard_map/expert/pallas_call | solution.py:491
  92.4 2.4 %collective-permute-start.27 = (bf16[864,128]{1,0:T(8,128)(2,1)}, bf16[864,128]{1,0:T(8,128)(2,1)S(1)}, u32[]{:S(2)}, u32[]{:S(2)}) collective-permute-start(bf16[864,128]{1,0:T(8,128)(2,1)} %get-tuple-element.67), channel_id=1, source_target_pairs={{0,16},{1,5},{2,18},{3,7},{4,20},{5,1},{6,22},{7,3},{8,24},{9,13},... | collective-permute-start | bytes 663560 | tf_op jit(solution)/shard_map/ppermute | solution.py:454
  95.3 5.8 %expert.7 = (bf16[864,128]{1,0:T(8,128)(2,1)}, bf16[864,128]{1,0:T(8,128)(2,1)}, bf16[864,128]{1,0:T(8,128)(2,1)}, bf16[864,128]{1,0:T(8,128)(2,1)}) custom-call(s32[2]{0:T(128)S(1)} %pad_add_fusion.info, bf16[97,128,128]{2,1,0:T(8,128)(2,1)} %tie.6.refs_0_, bf16[97,128,128]{2,1,0:T(8,128)(2,1)} %copy-done.9, ...), custom_call_target="tpu_custom_call" | custom-call | tf_op jit(solution)/shard_map/expert/pallas_call | solution.py:491
  102.7 2.7 %collective-permute-start.23 = (bf16[864,128]{1,0:T(8,128)(2,1)}, bf16[864,128]{1,0:T(8,128)(2,1)S(1)}, u32[]{:S(2)}, u32[]{:S(2)}) collective-permute-start(bf16[864,128]{1,0:T(8,128)(2,1)} %get-tuple-element.63), channel_id=1, source_target_pairs={{0,16},{1,5},{2,18},{3,7},{4,20},{5,1},{6,22},{7,3},{8,24},{9,13},... | collective-permute-start | bytes 663560 | tf_op jit(solution)/shard_map/ppermute | solution.py:454
  105.9 1.3 %collective-permute-start.24 = (bf16[864,128]{1,0:T(8,128)(2,1)}, bf16[864,128]{1,0:T(8,128)(2,1)S(1)}, u32[]{:S(2)}, u32[]{:S(2)}) collective-permute-start(bf16[864,128]{1,0:T(8,128)(2,1)} %get-tuple-element.64), channel_id=1, source_target_pairs={{0,16},{1,7},{2,18},{3,5},{4,20},{5,3},{6,22},{7,1},{8,24},{9,15},... | collective-permute-start | bytes 663560 | tf_op jit(solution)/shard_map/ppermute | solution.py:454
  107.2 2.8 %last.2.rest_4_ = bf16[1,2,32,6144]{3,2,1,0:T(8,128)(2,1)} custom-call(s32[2]{0:T(128)S(1)} %pad_add_fusion.info, bf16[32,6144]{1,0:T(8,128)(2,1)} %get-tuple-element.49.refs_9_.first, bf16[1536,128]{1,0:T(8,128)(2,1)S(1)} %collective-permute-done.25.carried, s32[1,2,2,32]{3,2,1,0:T(2,128)S(1)} %bitcast.13, f32[1,2,2,32]{3,2,1,0:T(2,128)S(1)} %bitcast.17, ...), custom_call_target="tpu_custom_call" | custom-call | tf_op jit(solution)/shard_map/last/pallas_call | solution.py:491
  110.0 2.8 %collective-permute-done.23.rest_2_ = bf16[864,128]{1,0:T(8,128)(2,1)S(1)} collective-permute-done((bf16[864,128]{1,0:T(8,128)(2,1)}, bf16[864,128]{1,0:T(8,128)(2,1)S(1)}, u32[]{:S(2)}, u32[]{:S(2)}) %collective-permute-start.23) | collective-permute-done | bytes 221216 | tf_op jit(solution)/shard_map/ppermute | solution.py:454
  112.8 3.4 %collective-permute-done.24.rest_3_ = bf16[864,128]{1,0:T(8,128)(2,1)S(1)} collective-permute-done((bf16[864,128]{1,0:T(8,128)(2,1)}, bf16[864,128]{1,0:T(8,128)(2,1)S(1)}, u32[]{:S(2)}, u32[]{:S(2)}) %collective-permute-start.24) | collective-permute-done | bytes 221216 | tf_op jit(solution)/shard_map/ppermute | solution.py:454
  116.3 2.8 %last.3 = bf16[1,2,32,6144]{3,2,1,0:T(8,128)(2,1)} custom-call(s32[2]{0:T(128)S(1)} %pad_add_fusion.info, bf16[32,6144]{1,0:T(8,128)(2,1)} %get-tuple-element.50.refs_6_.first, bf16[1536,128]{1,0:T(8,128)(2,1)S(1)} %collective-permute-done.21.carried, s32[1,2,2,32]{3,2,1,0:T(2,128)S(1)} %bitcast.14, ...), custom_call_target="tpu_custom_call", output_to_operand_aliasing={{}: (9, {})} | custom-call | tf_op jit(solution)/shard_map/last/pallas_call | solution.py:491
  (62 shorter events, 7.5 us)
Async XLA Ops:
  3.6 37.1 %collective-permute-start.2 = (bf16[97,128,128]{2,1,0:T(8,128)(2,1)}, bf16[97,128,128]{2,1,0:T(8,128)(2,1)}, u32[]{:S(2)}, u32[]{:S(2)}) collective-permute-start(bf16[97,128,128]{2,1,0:T(8,128)(2,1)} %pack.1.refs_0_), channel_id=1, source_target_pairs={{0,8},{1,17},{2,10},{3,19},{4,12},{5,21},{6,14},{7,23},{8,0},{9,25... | collective-permute-start | bytes 9535496 | tf_op jit(solution)/shard_map/ppermute | solution.py:454
  4.9 2.1 %collective-permute-start.1 = (f32[1,6144]{1,0:T(1,128)S(1)}, f32[1,6144]{1,0:T(1,128)S(1)}, u32[]{:S(2)}, u32[]{:S(2)}) collective-permute-start(f32[1,6144]{1,0:T(1,128)S(1)} %copy-done.8), channel_id=1, source_target_pairs={{0,1},{1,0},{2,3},{3,2},{4,5},{5,4},{6,7},{7,6},{8,9},{9,8},{10,11... | collective-permute-start | bytes 73736 | tf_op jit(solution)/shard_map/ppermute | solution.py:478
  5.9 1.2 collective-permute-start
  7.6 2.1 %collective-permute-start.3 = (bf16[1728,128]{1,0:T(8,128)(2,1)S(1)}, bf16[1728,128]{1,0:T(8,128)(2,1)S(1)}, u32[]{:S(2)}, u32[]{:S(2)}) collective-permute-start(bf16[1728,128]{1,0:T(8,128)(2,1)S(1)} %get-tuple-element.37), channel_id=1, source_target_pairs={{0,2},{2,0},{4,6},{6,4},{8,10},{10,8},{12,14},{14,12},{16,18},{18,... | collective-permute-start | bytes 1327112 | tf_op jit(solution)/shard_map/ppermute | solution.py:454
  8.3 1.4 %collective-permute-start.4 = (bf16[1728,128]{1,0:T(8,128)(2,1)S(1)}, bf16[1728,128]{1,0:T(8,128)(2,1)S(1)}, u32[]{:S(2)}, u32[]{:S(2)}) collective-permute-start(bf16[1728,128]{1,0:T(8,128)(2,1)S(1)} %get-tuple-element.38), channel_id=1, source_target_pairs={{0,4},{2,6},{4,0},{6,2},{8,12},{10,14},{12,8},{14,10},{16,20},{18,... | collective-permute-start | bytes 1327112 | tf_op jit(solution)/shard_map/ppermute | solution.py:454
  9.0 0.7 collective-permute-start.5
  9.7 31.1 %copy-start = (bf16[1728,128]{1,0:T(8,128)(2,1)}, bf16[1728,128]{1,0:T(8,128)(2,1)S(1)}, u32[]{:S(2)}) copy-start(bf16[1728,128]{1,0:T(8,128)(2,1)S(1)} %collective-permute-done.3.refs_1_.refs_3_) | copy-start | bytes 1327108
  9.7 31.1 %copy-start.2 = (bf16[1728,128]{1,0:T(8,128)(2,1)}, bf16[1728,128]{1,0:T(8,128)(2,1)S(1)}, u32[]{:S(2)}) copy-start(bf16[1728,128]{1,0:T(8,128)(2,1)S(1)} %collective-permute-done.4.refs_2_.refs_4_) | copy-start | bytes 1327108
  9.7 31.0 %copy-start.4 = (bf16[1728,128]{1,0:T(8,128)(2,1)}, bf16[1728,128]{1,0:T(8,128)(2,1)S(1)}, u32[]{:S(2)}) copy-start(bf16[1728,128]{1,0:T(8,128)(2,1)S(1)} %collective-permute-done.5.refs_3_.refs_5_) | copy-start | bytes 1327108
  40.8 43.8 %collective-permute-start.12 = (bf16[97,128,128]{2,1,0:T(8,128)(2,1)}, bf16[97,128,128]{2,1,0:T(8,128)(2,1)S(1)}, u32[]{:S(2)}, u32[]{:S(2)}) collective-permute-start(bf16[97,128,128]{2,1,0:T(8,128)(2,1)} %tie.6.refs_0_), channel_id=1, source_target_pairs={{1,9},{3,11},{5,13},{7,15},{9,1},{11,3},{13,5},{15,7},{17,25},{19,... | collective-permute-start | bytes 9535496 | tf_op jit(solution)/shard_map/ppermute | solution.py:454
  44.8 5.1 %collective-permute-start.9 = (bf16[864,128]{1,0:T(8,128)(2,1)}, bf16[864,128]{1,0:T(8,128)(2,1)S(1)}, u32[]{:S(2)}, u32[]{:S(2)}) collective-permute-start(bf16[864,128]{1,0:T(8,128)(2,1)} %get-tuple-element.46), channel_id=1, source_target_pairs={{0,2},{1,17},{2,0},{3,19},{4,6},{5,21},{6,4},{7,23},{8,10},{9,25},... | collective-permute-start | bytes 663560 | tf_op jit(solution)/shard_map/ppermute | solution.py:454
  46.1 6.1 %collective-permute-start.10 = (bf16[864,128]{1,0:T(8,128)(2,1)}, bf16[864,128]{1,0:T(8,128)(2,1)S(1)}, u32[]{:S(2)}, u32[]{:S(2)}) collective-permute-start(bf16[864,128]{1,0:T(8,128)(2,1)} %get-tuple-element.47), channel_id=1, source_target_pairs={{0,4},{1,17},{2,6},{3,19},{4,0},{5,21},{6,2},{7,23},{8,12},{9,25},... | collective-permute-start | bytes 663560 | tf_op jit(solution)/shard_map/ppermute | solution.py:454
  46.3 8.6 %collective-permute-start.11 = (bf16[864,128]{1,0:T(8,128)(2,1)}, bf16[864,128]{1,0:T(8,128)(2,1)S(1)}, u32[]{:S(2)}, u32[]{:S(2)}) collective-permute-start(bf16[864,128]{1,0:T(8,128)(2,1)} %get-tuple-element.48), channel_id=1, source_target_pairs={{0,6},{1,17},{2,4},{3,19},{4,2},{5,21},{6,0},{7,23},{8,14},{9,25},... | collective-permute-start | bytes 663560 | tf_op jit(solution)/shard_map/ppermute | solution.py:454
  48.3 21.1 %collective-permute-start.6 = (bf16[864,128]{1,0:T(8,128)(2,1)}, bf16[864,128]{1,0:T(8,128)(2,1)S(1)}, u32[]{:S(2)}, u32[]{:S(2)}) collective-permute-start(bf16[864,128]{1,0:T(8,128)(2,1)} %get-tuple-element.43), channel_id=1, source_target_pairs={{0,2},{1,17},{2,0},{3,19},{4,6},{5,21},{6,4},{7,23},{8,10},{9,25},... | collective-permute-start | bytes 663560 | tf_op jit(solution)/shard_map/ppermute | solution.py:454
  49.9 20.7 %collective-permute-start.7 = (bf16[864,128]{1,0:T(8,128)(2,1)}, bf16[864,128]{1,0:T(8,128)(2,1)S(1)}, u32[]{:S(2)}, u32[]{:S(2)}) collective-permute-start(bf16[864,128]{1,0:T(8,128)(2,1)} %get-tuple-element.44), channel_id=1, source_target_pairs={{0,4},{1,17},{2,6},{3,19},{4,0},{5,21},{6,2},{7,23},{8,12},{9,25},... | collective-permute-start | bytes 663560 | tf_op jit(solution)/shard_map/ppermute | solution.py:454
  52.2 20.1 %collective-permute-start.8 = (bf16[864,128]{1,0:T(8,128)(2,1)}, bf16[864,128]{1,0:T(8,128)(2,1)S(1)}, u32[]{:S(2)}, u32[]{:S(2)}) collective-permute-start(bf16[864,128]{1,0:T(8,128)(2,1)} %get-tuple-element.45), channel_id=1, source_target_pairs={{0,6},{1,17},{2,4},{3,19},{4,2},{5,21},{6,0},{7,23},{8,14},{9,25},... | collective-permute-start | bytes 663560 | tf_op jit(solution)/shard_map/ppermute | solution.py:454
  55.9 20.8 %collective-permute-start.13 = (bf16[864,128]{1,0:T(8,128)(2,1)}, bf16[864,128]{1,0:T(8,128)(2,1)S(1)}, u32[]{:S(2)}, u32[]{:S(2)}) collective-permute-start(bf16[864,128]{1,0:T(8,128)(2,1)} %get-tuple-element.53), channel_id=1, source_target_pairs={{0,1},{1,0},{2,3},{3,2},{4,5},{5,4},{6,7},{7,6},{8,9},{9,8},{10,11... | collective-permute-start | bytes 663560 | tf_op jit(solution)/shard_map/ppermute | solution.py:478
  69.4 11.2 %collective-permute-start.14 = (bf16[864,128]{1,0:T(8,128)(2,1)}, bf16[864,128]{1,0:T(8,128)(2,1)S(1)}, u32[]{:S(2)}, u32[]{:S(2)}) collective-permute-start(bf16[864,128]{1,0:T(8,128)(2,1)} %get-tuple-element.54), channel_id=1, source_target_pairs={{0,3},{1,16},{2,1},{3,18},{4,7},{5,20},{6,5},{7,22},{8,11},{9,24},... | collective-permute-start | bytes 663560 | tf_op jit(solution)/shard_map/ppermute | solution.py:454
  70.5 10.1 %collective-permute-start.15 = (bf16[864,128]{1,0:T(8,128)(2,1)}, bf16[864,128]{1,0:T(8,128)(2,1)S(1)}, u32[]{:S(2)}, u32[]{:S(2)}) collective-permute-start(bf16[864,128]{1,0:T(8,128)(2,1)} %get-tuple-element.55), channel_id=1, source_target_pairs={{0,5},{1,16},{2,7},{3,18},{4,1},{5,20},{6,3},{7,22},{8,13},{9,24},... | collective-permute-start | bytes 663560 | tf_op jit(solution)/shard_map/ppermute | solution.py:454
  72.3 12.3 %collective-permute-start.16 = (bf16[864,128]{1,0:T(8,128)(2,1)}, bf16[864,128]{1,0:T(8,128)(2,1)S(1)}, u32[]{:S(2)}, u32[]{:S(2)}) collective-permute-start(bf16[864,128]{1,0:T(8,128)(2,1)} %get-tuple-element.56), channel_id=1, source_target_pairs={{0,7},{1,16},{2,5},{3,18},{4,3},{5,20},{6,1},{7,22},{8,15},{9,24},... | collective-permute-start | bytes 663560 | tf_op jit(solution)/shard_map/ppermute | solution.py:454
  76.7 15.7 %collective-permute-start.18 = (bf16[864,128]{1,0:T(8,128)(2,1)}, bf16[864,128]{1,0:T(8,128)(2,1)S(1)}, u32[]{:S(2)}, u32[]{:S(2)}) collective-permute-start(bf16[864,128]{1,0:T(8,128)(2,1)} %get-tuple-element.58), channel_id=1, source_target_pairs={{0,3},{1,16},{2,1},{3,18},{4,7},{5,20},{6,5},{7,22},{8,11},{9,24},... | collective-permute-start | bytes 663560 | tf_op jit(solution)/shard_map/ppermute | solution.py:454
  80.5 14.3 %collective-permute-start.19 = (bf16[864,128]{1,0:T(8,128)(2,1)}, bf16[864,128]{1,0:T(8,128)(2,1)S(1)}, u32[]{:S(2)}, u32[]{:S(2)}) collective-permute-start(bf16[864,128]{1,0:T(8,128)(2,1)} %get-tuple-element.59), channel_id=1, source_target_pairs={{0,5},{1,16},{2,7},{3,18},{4,1},{5,20},{6,3},{7,22},{8,13},{9,24},... | collective-permute-start | bytes 663560 | tf_op jit(solution)/shard_map/ppermute | solution.py:454
  80.6 14.4 %collective-permute-start.20 = (bf16[864,128]{1,0:T(8,128)(2,1)}, bf16[864,128]{1,0:T(8,128)(2,1)S(1)}, u32[]{:S(2)}, u32[]{:S(2)}) collective-permute-start(bf16[864,128]{1,0:T(8,128)(2,1)} %get-tuple-element.60), channel_id=1, source_target_pairs={{0,7},{1,16},{2,5},{3,18},{4,3},{5,20},{6,1},{7,22},{8,15},{9,24},... | collective-permute-start | bytes 663560 | tf_op jit(solution)/shard_map/ppermute | solution.py:454
  92.2 3.1 %collective-permute-start.17 = (bf16[864,128]{1,0:T(8,128)(2,1)}, bf16[864,128]{1,0:T(8,128)(2,1)S(1)}, u32[]{:S(2)}, u32[]{:S(2)}) collective-permute-start(bf16[864,128]{1,0:T(8,128)(2,1)} %tie.7), channel_id=1, source_target_pairs={{0,1},{1,0},{2,3},{3,2},{4,5},{5,4},{6,7},{7,6},{8,9},{9,8},{10,11... | collective-permute-start | bytes 663560 | tf_op jit(solution)/shard_map/ppermute | solution.py:478
  92.3 9.0 %collective-permute-start.26 = (bf16[864,128]{1,0:T(8,128)(2,1)}, bf16[864,128]{1,0:T(8,128)(2,1)S(1)}, u32[]{:S(2)}, u32[]{:S(2)}) collective-permute-start(bf16[864,128]{1,0:T(8,128)(2,1)} %get-tuple-element.66), channel_id=1, source_target_pairs={{0,16},{1,3},{2,18},{3,1},{4,20},{5,7},{6,22},{7,5},{8,24},{9,11},... | collective-permute-start | bytes 663560 | tf_op jit(solution)/shard_map/ppermute | solution.py:454
  92.4 10.4 %collective-permute-start.27 = (bf16[864,128]{1,0:T(8,128)(2,1)}, bf16[864,128]{1,0:T(8,128)(2,1)S(1)}, u32[]{:S(2)}, u32[]{:S(2)}) collective-permute-start(bf16[864,128]{1,0:T(8,128)(2,1)} %get-tuple-element.67), channel_id=1, source_target_pairs={{0,16},{1,5},{2,18},{3,7},{4,20},{5,1},{6,22},{7,3},{8,24},{9,13},... | collective-permute-start | bytes 663560 | tf_op jit(solution)/shard_map/ppermute | solution.py:454
  94.8 11.1 %collective-permute-start.28 = (bf16[864,128]{1,0:T(8,128)(2,1)}, bf16[864,128]{1,0:T(8,128)(2,1)S(1)}, u32[]{:S(2)}, u32[]{:S(2)}) collective-permute-start(bf16[864,128]{1,0:T(8,128)(2,1)} %get-tuple-element.68), channel_id=1, source_target_pairs={{0,16},{1,7},{2,18},{3,5},{4,20},{5,3},{6,22},{7,1},{8,24},{9,15},... | collective-permute-start | bytes 663560 | tf_op jit(solution)/shard_map/ppermute | solution.py:454
  95.0 12.2 %collective-permute-start.25 = (bf16[1536,128]{1,0:T(8,128)(2,1)}, bf16[1536,128]{1,0:T(8,128)(2,1)S(1)}, u32[]{:S(2)}, u32[]{:S(2)}) collective-permute-start(bf16[1536,128]{1,0:T(8,128)(2,1)} %tie.9), channel_id=1, source_target_pairs={{0,1},{1,0},{2,3},{3,2},{4,5},{5,4},{6,7},{7,6},{8,9},{9,8},{10,11... | collective-permute-start | bytes 1179656 | tf_op jit(solution)/shard_map/ppermute | solution.py:478
  101.2 15.1 %collective-permute-start.21 = (bf16[1536,128]{1,0:T(8,128)(2,1)}, bf16[1536,128]{1,0:T(8,128)(2,1)S(1)}, u32[]{:S(2)}, u32[]{:S(2)}) collective-permute-start(bf16[1536,128]{1,0:T(8,128)(2,1)} %tie.8), channel_id=1, source_target_pairs={{0,1},{1,0},{2,3},{3,2},{4,5},{5,4},{6,7},{7,6},{8,9},{9,8},{10,11... | collective-permute-start | bytes 1179656 | tf_op jit(solution)/shard_map/ppermute | solution.py:478
  101.3 8.7 %collective-permute-start.22 = (bf16[864,128]{1,0:T(8,128)(2,1)}, bf16[864,128]{1,0:T(8,128)(2,1)S(1)}, u32[]{:S(2)}, u32[]{:S(2)}) collective-permute-start(bf16[864,128]{1,0:T(8,128)(2,1)} %get-tuple-element.62), channel_id=1, source_target_pairs={{0,16},{1,3},{2,18},{3,1},{4,20},{5,7},{6,22},{7,5},{8,24},{9,11},... | collective-permute-start | bytes 663560 | tf_op jit(solution)/shard_map/ppermute | solution.py:454
  102.7 10.1 %collective-permute-start.23 = (bf16[864,128]{1,0:T(8,128)(2,1)}, bf16[864,128]{1,0:T(8,128)(2,1)S(1)}, u32[]{:S(2)}, u32[]{:S(2)}) collective-permute-start(bf16[864,128]{1,0:T(8,128)(2,1)} %get-tuple-element.63), channel_id=1, source_target_pairs={{0,16},{1,5},{2,18},{3,7},{4,20},{5,1},{6,22},{7,3},{8,24},{9,13},... | collective-permute-start | bytes 663560 | tf_op jit(solution)/shard_map/ppermute | solution.py:454
  105.9 10.3 %collective-permute-start.24 = (bf16[864,128]{1,0:T(8,128)(2,1)}, bf16[864,128]{1,0:T(8,128)(2,1)S(1)}, u32[]{:S(2)}, u32[]{:S(2)}) collective-permute-start(bf16[864,128]{1,0:T(8,128)(2,1)} %get-tuple-element.64), channel_id=1, source_target_pairs={{0,16},{1,7},{2,18},{3,5},{4,20},{5,3},{6,22},{7,1},{8,24},{9,15},... | collective-permute-start | bytes 663560 | tf_op jit(solution)/shard_map/ppermute | solution.py:454
  (7 other events, 29.7 us)
